TPU v7x, 32 devices: a whole 2x2x4 slice. The times are simulated.
32 devices in a mesh: slab: 8 (over z, y), lat: 4 (over x, core).
Axes of the slice: x: 2, y: 2, z: 4, core: 2. Of those that a mesh axis runs over, the one named last changes fastest.
Arguments:
- residual_blocks: float32 [1024, 2, 64, 128], P(('slab', 'lat')), may hold values from -1.5 to 1.5
- residual_slab: int32 [1024, 1], P(('slab', 'lat')), may hold values from 0 to 7; in each aligned block of 32 rows (0 to 31, 32 to 63, ...) at most 4 rows name the same one
- residual_pos: int32 [1024], P(('slab', 'lat')), may hold values from 0 to 3
- shot_ids: int32 [64], replicated, may hold values from 0 to 63, each once
- wavelet: float32 [64, 2], replicated, may hold values from -4 to 4
- down_panel: float32 [8, 4, 2, 512, 512], P('slab', 'lat'), may hold values from -1 to 1
- up_panel: float32 [8, 4, 2, 512, 512], P('slab', 'lat'), may hold values from -1 to 1
- recovery: float32 [8, 4, 2, 768, 1024], P('slab', 'lat'), may hold values from -0.109375 to 0.109375
- forward_field: float32 [8, 4, 2, 64, 1024], P('slab', 'lat'), may hold values from -3 to 3
- element_owner: int32 [256, 1], P(('slab', 'lat')), may hold values from 0 to 7; in each aligned block of 8 rows (0 to 7, 8 to 15, ...) at most 2 rows name the same one
- element_slot: int32 [256], P(('slab', 'lat')), may hold values from 0 to 7
Outputs:
- adjoint_trace: float32 [8, 4, 2, 64, 512], P('slab', 'lat')
- velocity_gradient: float32 [8, 4, 8, 128], P('slab', 'lat')
Inputs may be any that keep to these rules, and one draw needn't show every extreme that they name: `residual_slab`: in the 32 rows of one device no slab is named more than 4 times, a bound that some block reaches. `shot_ids`: each shot number appears once. `element_owner`: in the 8 rows of one device no slab is named more than 2 times, a bound that some block reaches.
All inputs are finite; a program needn't handle non-finite values.
Results may differ from a plain program's by a relative error of at most 0.00014.
Values sent between devices are 32-bit elements; how exact they have to be, the bound alone decides.
No kernel may reach another device: no remote copies, remote signals or barrier semaphores. Data moves between devices by JAX's collectives and lax.ppermute only.
A program may use at most 128 MiB of HBM per device.

v0:
```python
import jax
import jax.numpy as jnp
from jax import lax
from jax.sharding import PartitionSpec as P

MBLK = 8
GCAP = 2


def shifted(block, axis, distance):
    devices = range(lax.axis_size(axis))
    route = [(i - distance, i) for i in devices if i - distance in devices]
    return lax.ppermute(block, axis, route)


def padded(cells, sides, width):
    for axis, dim in sides:
        count = lax.axis_size(axis)
        ends = count - 1
        head = lax.slice_in_dim(cells, 0, width, axis=dim)
        tail = lax.slice_in_dim(cells, cells.shape[dim] - width, cells.shape[dim], axis=dim)
        cells = jnp.concatenate(
            [
                lax.ppermute(tail, axis, [(i, (i + 1) % count) for i in range(ends)]),
                cells,
                lax.ppermute(head, axis, [((i + 1) % count, i) for i in range(ends)]),
            ],
            axis=dim,
        )
    return cells


def complex_product(vector, panel):
    value_re = vector[..., 0, :, :]
    value_im = vector[..., 1, :, :]
    panel_re = panel[..., 0, :, :]
    panel_im = panel[..., 1, :, :]
    first = jnp.matmul(value_re, panel_re, precision=lax.Precision.HIGHEST) - jnp.matmul(
        value_im, panel_im, precision=lax.Precision.HIGHEST
    )
    second = jnp.matmul(value_re, panel_im, precision=lax.Precision.HIGHEST) + jnp.matmul(
        value_im, panel_re, precision=lax.Precision.HIGHEST
    )
    return jnp.stack([first, second], axis=-3)


def slot_numbers(targets, count):
    member = (targets[:, None] == jnp.arange(count, dtype=jnp.int32)[None, :]).astype(jnp.int32)
    return jnp.sum(jnp.cumsum(member, axis=0) * member, axis=1) - 1


def body(
    residual_blocks,
    residual_slab,
    residual_pos,
    shot_ids,
    wavelet,
    down_panel,
    up_panel,
    recovery,
    forward_field,
    element_owner,
    element_slot,
):
    slab_count = lax.axis_size("slab")
    block_count = residual_blocks.shape[0]
    shots = residual_blocks.shape[2]
    width = residual_blocks.shape[3]
    trace = down_panel.shape[-1]
    places = trace // width
    targets = residual_slab[:, 0]
    capacity = block_count // 8
    where_to = targets * capacity + slot_numbers(targets, slab_count)
    outgoing = (
        jnp.zeros((slab_count * capacity, 2, shots, width), jnp.float32)
        .at[where_to]
        .set(residual_blocks)
    )
    outgoing_pos = jnp.full((slab_count * capacity,), -1, jnp.int32).at[where_to].set(residual_pos)
    arrived, arrived_pos = (
        lax.all_to_all(outgoing, "slab", split_axis=0, concat_axis=0, tiled=True),
        lax.all_to_all(outgoing_pos, "slab", split_axis=0, concat_axis=0, tiled=True),
    )
    select = (arrived_pos[:, None] == jnp.arange(places, dtype=jnp.int32)[None, :]).astype(
        jnp.float32
    )
    summed = jnp.einsum("rp,rcsw->cspw", select, arrived, precision=lax.Precision.HIGHEST)
    summed = summed.reshape(2, shots, trace)
    picker = (shot_ids[:, None] == jnp.arange(shots, dtype=jnp.int32)[None, :]).astype(jnp.float32)
    weights = jnp.dot(picker, wavelet, precision=lax.Precision.HIGHEST)
    weight_re = weights[:, 0:1]
    weight_im = weights[:, 1:2]
    sources = jnp.stack(
        [
            weight_re * summed[0] - weight_im * summed[1],
            weight_re * summed[1] + weight_im * summed[0],
        ],
        axis=0,
    )
    downward = down_panel[0, 0]
    upward = up_panel[0, 0]

    def down_turn(counter, state):
        arrived = shifted(state, "slab", 1)
        return complex_product(arrived, downward) + sources

    downs = lax.fori_loop(0, slab_count, down_turn, jnp.zeros_like(sources))

    def up_turn(counter, state):
        arrived = shifted(state, "slab", -1)
        return complex_product(arrived, upward) + downs

    ups = lax.fori_loop(0, slab_count, up_turn, jnp.zeros_like(sources))
    extended = padded(ups, (("lat", 2),), width)
    interior = complex_product(extended, recovery[0, 0])
    gradient = jnp.sum(forward_field[0, 0] * interior, axis=(0, 1)) * shots ** (-0.5)
    pieces = gradient.reshape(-1, width)
    owners = element_owner[:, 0]
    where_to = owners * GCAP + slot_numbers(owners, slab_count)
    outgoing = jnp.zeros((slab_count * GCAP, width), jnp.float32).at[where_to].set(pieces)
    outgoing_slot = jnp.full((slab_count * GCAP,), -1, jnp.int32).at[where_to].set(element_slot)
    arrived, arrived_slot = (
        lax.all_to_all(outgoing, "slab", split_axis=0, concat_axis=0, tiled=True),
        lax.all_to_all(outgoing_slot, "slab", split_axis=0, concat_axis=0, tiled=True),
    )
    select = (arrived_slot[:, None] == jnp.arange(MBLK, dtype=jnp.int32)[None, :]).astype(
        jnp.float32
    )
    model = jnp.dot(select.T, arrived, precision=lax.Precision.HIGHEST)
    return (ups[None, None], model[None, None])


def solution(mesh):
    placed = (
        P(("slab", "lat"), None, None, None),
        P(("slab", "lat"), None),
        P(("slab", "lat")),
        P(),
        P(),
        P("slab", "lat", None, None, None),
        P("slab", "lat", None, None, None),
        P("slab", "lat", None, None, None),
        P("slab", "lat", None, None, None),
        P(("slab", "lat"), None),
        P(("slab", "lat")),
    )
    return jax.shard_map(
        body,
        mesh=mesh,
        in_specs=placed,
        out_specs=(P("slab", "lat", None, None, None), P("slab", "lat", None, None)),
        check_vma=False,
    )
```

profile of v0, /device:TPU:1, one launch (start us, length us, event | category | flops | bytes accessed | tf_op | source)
XLA Modules:
  0.0 344.9 jit_solution(6505905451638878027)
XLA Ops:
  4.6 6.4 %all-to-all-start.1 = ((s32[8,4,1]{1,2,0:T(1,128)}), s32[8,4,1]{1,2,0:T(1,128)S(1)}, u32[]{:S(2)}, u32[]{:S(2)}) async-start(s32[8,4,1]{1,2,0:T(1,128)} %bitcast.6), calls=%async_computation.1 | async-start | bytes 8192 | tf_op jit(solution)/shard_map/all_to_all | solution.py:82
  12.5 5.4 %scatter_fusion = f32[32,2,64,128]{3,2,1,0:T(8,128)} fusion(f32[32,2,64,128]{3,2,1,0:T(8,128)} %broadcast_in_dim.8, s32[32]{0:T(128)S(1)} %fusion.67, f32[32,2,64,128]{3,2,1,0:T(8,128)S(1)} %copy-done.4), kind=kCustom, calls=%fused_computation | custom fusion | bytes 6291584 | tf_op jit(solution)/shard_map/scatter | solution.py:77
  17.9 5.5 %all-to-all-start = ((f32[32,2,64,128]{3,2,1,0:T(8,128)}), f32[32,2,64,128]{3,2,1,0:T(8,128)}, u32[]{:S(2)}, u32[]{:S(2)}) async-start(f32[32,2,64,128]{3,2,1,0:T(8,128)} %scatter_fusion), calls=%async_computation | async-start | bytes 4194304 | tf_op jit(solution)/shard_map/all_to_all | solution.py:81
  25.2 45.1 %all-to-all-done = f32[32,2,64,128]{3,2,1,0:T(8,128)} async-done(((f32[32,2,64,128]{3,2,1,0:T(8,128)}), f32[32,2,64,128]{3,2,1,0:T(8,128)}, u32[]{:S(2)}, u32[]{:S(2)}) %all-to-all-start) | async-done | bytes 2097184 | tf_op jit(solution)/shard_map/all_to_all | solution.py:81
  70.3 3.4 fusion.38
  74.1 87.5 %while.22 = (s32[]{:T(128)}, f32[2,64,512]{2,1,0:T(8,128)S(1)}, f32[2,512,512]{2,1,0:T(8,128)S(1)}, f32[2,64,512]{2,1,0:T(8,128)S(1)}, s32[]{:T(128)}, /*index=5*/s32[]{:T(128)}) while((s32[]{:T(128)}, f32[2,64,512]{2,1,0:T(8,128)S(1)}, f32[2,512,512]{2,1,0:T(8,128)S(1)}, f32[2,64,512]{2,1,0:T(8,128)S(1)}, s32[]{:T(128)}, ...), condition=%wide.region_5.6_spmd.clone, body=%wide.region_4.5_spmd.clone.sunk | while | flops 805568512 | bytes 7864439 | solution.py:107
  74.1 4.1 %collective-permute-start = (f32[2,64,512]{2,1,0:T(8,128)S(1)}, f32[2,64,512]{2,1,0:T(8,128)S(1)}, u32[]{:S(2)}, u32[]{:S(2)}) collective-permute-start(f32[2,64,512]{2,1,0:T(8,128)S(1)} %broadcast_select_fusion.4), channel_id=1, source_target_pairs={{0,4},{4,8},{8,12},{12,16},{16,20},{20,24},{24,28},{1,5},{5,9},{9,... | collective-permute-start | bytes 786440 | tf_op jit(solution)/shard_map/while/body/eval_jaxpr/ppermute | solution.py:13
  78.2 4.1 %collective-permute-done = f32[2,64,512]{2,1,0:T(8,128)S(1)} collective-permute-done((f32[2,64,512]{2,1,0:T(8,128)S(1)}, f32[2,64,512]{2,1,0:T(8,128)S(1)}, u32[]{:S(2)}, u32[]{:S(2)}) %collective-permute-start) | collective-permute-done | bytes 262176 | tf_op jit(solution)/shard_map/while/body/eval_jaxpr/ppermute | solution.py:13
  85.4 4.1 %collective-permute-start = (f32[2,64,512]{2,1,0:T(8,128)S(1)}, f32[2,64,512]{2,1,0:T(8,128)S(1)}, u32[]{:S(2)}, u32[]{:S(2)}) collective-permute-start(f32[2,64,512]{2,1,0:T(8,128)S(1)} %broadcast_select_fusion.4), channel_id=1, source_target_pairs={{0,4},{4,8},{8,12},{12,16},{16,20},{20,24},{24,28},{1,5},{5,9},{9,... | collective-permute-start | bytes 786440 | tf_op jit(solution)/shard_map/while/body/eval_jaxpr/ppermute | solution.py:13
  89.5 3.3 collective-permute-done
  95.9 3.8 %collective-permute-start = (f32[2,64,512]{2,1,0:T(8,128)S(1)}, f32[2,64,512]{2,1,0:T(8,128)S(1)}, u32[]{:S(2)}, u32[]{:S(2)}) collective-permute-start(f32[2,64,512]{2,1,0:T(8,128)S(1)} %broadcast_select_fusion.4), channel_id=1, source_target_pairs={{0,4},{4,8},{8,12},{12,16},{16,20},{20,24},{24,28},{1,5},{5,9},{9,... | collective-permute-start | bytes 786440 | tf_op jit(solution)/shard_map/while/body/eval_jaxpr/ppermute | solution.py:13
  99.8 3.3 collective-permute-done
  106.2 4.5 %collective-permute-start = (f32[2,64,512]{2,1,0:T(8,128)S(1)}, f32[2,64,512]{2,1,0:T(8,128)S(1)}, u32[]{:S(2)}, u32[]{:S(2)}) collective-permute-start(f32[2,64,512]{2,1,0:T(8,128)S(1)} %broadcast_select_fusion.4), channel_id=1, source_target_pairs={{0,4},{4,8},{8,12},{12,16},{16,20},{20,24},{24,28},{1,5},{5,9},{9,... | collective-permute-start | bytes 786440 | tf_op jit(solution)/shard_map/while/body/eval_jaxpr/ppermute | solution.py:13
  110.7 3.3 collective-permute-done
  117.1 4.7 %collective-permute-start = (f32[2,64,512]{2,1,0:T(8,128)S(1)}, f32[2,64,512]{2,1,0:T(8,128)S(1)}, u32[]{:S(2)}, u32[]{:S(2)}) collective-permute-start(f32[2,64,512]{2,1,0:T(8,128)S(1)} %broadcast_select_fusion.4), channel_id=1, source_target_pairs={{0,4},{4,8},{8,12},{12,16},{16,20},{20,24},{24,28},{1,5},{5,9},{9,... | collective-permute-start | bytes 786440 | tf_op jit(solution)/shard_map/while/body/eval_jaxpr/ppermute | solution.py:13
  121.8 3.3 collective-permute-done
  128.2 4.7 %collective-permute-start = (f32[2,64,512]{2,1,0:T(8,128)S(1)}, f32[2,64,512]{2,1,0:T(8,128)S(1)}, u32[]{:S(2)}, u32[]{:S(2)}) collective-permute-start(f32[2,64,512]{2,1,0:T(8,128)S(1)} %broadcast_select_fusion.4), channel_id=1, source_target_pairs={{0,4},{4,8},{8,12},{12,16},{16,20},{20,24},{24,28},{1,5},{5,9},{9,... | collective-permute-start | bytes 786440 | tf_op jit(solution)/shard_map/while/body/eval_jaxpr/ppermute | solution.py:13
  132.9 3.3 collective-permute-done
  139.3 4.7 %collective-permute-start = (f32[2,64,512]{2,1,0:T(8,128)S(1)}, f32[2,64,512]{2,1,0:T(8,128)S(1)}, u32[]{:S(2)}, u32[]{:S(2)}) collective-permute-start(f32[2,64,512]{2,1,0:T(8,128)S(1)} %broadcast_select_fusion.4), channel_id=1, source_target_pairs={{0,4},{4,8},{8,12},{12,16},{16,20},{20,24},{24,28},{1,5},{5,9},{9,... | collective-permute-start | bytes 786440 | tf_op jit(solution)/shard_map/while/body/eval_jaxpr/ppermute | solution.py:13
  144.1 3.3 collective-permute-done
  150.5 4.7 %collective-permute-start = (f32[2,64,512]{2,1,0:T(8,128)S(1)}, f32[2,64,512]{2,1,0:T(8,128)S(1)}, u32[]{:S(2)}, u32[]{:S(2)}) collective-permute-start(f32[2,64,512]{2,1,0:T(8,128)S(1)} %broadcast_select_fusion.4), channel_id=1, source_target_pairs={{0,4},{4,8},{8,12},{12,16},{16,20},{20,24},{24,28},{1,5},{5,9},{9,... | collective-permute-start | bytes 786440 | tf_op jit(solution)/shard_map/while/body/eval_jaxpr/ppermute | solution.py:13
  155.2 3.3 collective-permute-done
  161.6 119.4 %while.23 = (s32[]{:T(128)}, f32[2,64,512]{2,1,0:T(8,128)S(1)}, f32[2,512,512]{2,1,0:T(8,128)}, f32[2,64,512]{2,1,0:T(8,128)S(1)}, s32[]{:T(128)}, /*index=5*/s32[]{:T(128)}) while((s32[]{:T(128)}, f32[2,64,512]{2,1,0:T(8,128)S(1)}, f32[2,512,512]{2,1,0:T(8,128)}, f32[2,64,512]{2,1,0:T(8,128)S(1)}, s32[]{:T(128)}, ...), condition=%wide.region_7.8_spmd.clone, body=%wide.region_6.7_spmd.clone.sunk | while | flops 805568512 | bytes 16253075 | solution.py:113
  163.0 7.2 %collective-permute-done.1 = f32[2,64,512]{2,1,0:T(8,128)S(1)} collective-permute-done((f32[2,64,512]{2,1,0:T(8,128)S(1)}, f32[2,64,512]{2,1,0:T(8,128)S(1)}, u32[]{:S(2)}, u32[]{:S(2)}) %collective-permute-start.1) | collective-permute-done | bytes 262176 | tf_op jit(solution)/shard_map/while/body/eval_jaxpr/ppermute | solution.py:13
  177.2 7.2 %collective-permute-done.1 = f32[2,64,512]{2,1,0:T(8,128)S(1)} collective-permute-done((f32[2,64,512]{2,1,0:T(8,128)S(1)}, f32[2,64,512]{2,1,0:T(8,128)S(1)}, u32[]{:S(2)}, u32[]{:S(2)}) %collective-permute-start.1) | collective-permute-done | bytes 262176 | tf_op jit(solution)/shard_map/while/body/eval_jaxpr/ppermute | solution.py:13
  186.3 2.0 fusion.105
  191.4 7.5 %collective-permute-done.1 = f32[2,64,512]{2,1,0:T(8,128)S(1)} collective-permute-done((f32[2,64,512]{2,1,0:T(8,128)S(1)}, f32[2,64,512]{2,1,0:T(8,128)S(1)}, u32[]{:S(2)}, u32[]{:S(2)}) %collective-permute-start.1) | collective-permute-done | bytes 262176 | tf_op jit(solution)/shard_map/while/body/eval_jaxpr/ppermute | solution.py:13
  200.8 2.0 fusion.105
  205.9 7.3 %collective-permute-done.1 = f32[2,64,512]{2,1,0:T(8,128)S(1)} collective-permute-done((f32[2,64,512]{2,1,0:T(8,128)S(1)}, f32[2,64,512]{2,1,0:T(8,128)S(1)}, u32[]{:S(2)}, u32[]{:S(2)}) %collective-permute-start.1) | collective-permute-done | bytes 262176 | tf_op jit(solution)/shard_map/while/body/eval_jaxpr/ppermute | solution.py:13
  215.1 2.0 fusion.105
  220.2 11.0 %collective-permute-done.1 = f32[2,64,512]{2,1,0:T(8,128)S(1)} collective-permute-done((f32[2,64,512]{2,1,0:T(8,128)S(1)}, f32[2,64,512]{2,1,0:T(8,128)S(1)}, u32[]{:S(2)}, u32[]{:S(2)}) %collective-permute-start.1) | collective-permute-done | bytes 262176 | tf_op jit(solution)/shard_map/while/body/eval_jaxpr/ppermute | solution.py:13
  233.1 2.0 fusion.105
  238.2 9.4 %collective-permute-done.1 = f32[2,64,512]{2,1,0:T(8,128)S(1)} collective-permute-done((f32[2,64,512]{2,1,0:T(8,128)S(1)}, f32[2,64,512]{2,1,0:T(8,128)S(1)}, u32[]{:S(2)}, u32[]{:S(2)}) %collective-permute-start.1) | collective-permute-done | bytes 262176 | tf_op jit(solution)/shard_map/while/body/eval_jaxpr/ppermute | solution.py:13
  254.6 7.4 %collective-permute-done.1 = f32[2,64,512]{2,1,0:T(8,128)S(1)} collective-permute-done((f32[2,64,512]{2,1,0:T(8,128)S(1)}, f32[2,64,512]{2,1,0:T(8,128)S(1)}, u32[]{:S(2)}, u32[]{:S(2)}) %collective-permute-start.1) | collective-permute-done | bytes 262176 | tf_op jit(solution)/shard_map/while/body/eval_jaxpr/ppermute | solution.py:13
  262.0 2.0 fusion.107
  264.0 2.0 fusion.105
  269.0 6.4 %collective-permute-done.1 = f32[2,64,512]{2,1,0:T(8,128)S(1)} collective-permute-done((f32[2,64,512]{2,1,0:T(8,128)S(1)}, f32[2,64,512]{2,1,0:T(8,128)S(1)}, u32[]{:S(2)}, u32[]{:S(2)}) %collective-permute-start.1) | collective-permute-done | bytes 262176 | tf_op jit(solution)/shard_map/while/body/eval_jaxpr/ppermute | solution.py:13
  277.4 2.0 fusion.105
  281.0 21.5 %collective-permute-start.2 = (f32[2,64,128]{2,1,0:T(8,128)S(1)}, f32[2,64,128]{2,1,0:T(8,128)S(1)}, u32[]{:S(2)}, u32[]{:S(2)}) collective-permute-start(f32[2,64,128]{2,1,0:T(8,128)S(1)} %get-tuple-element.97), channel_id=1, source_target_pairs={{0,1},{1,2},{2,3},{4,5},{5,6},{6,7},{8,9},{9,10},{10,11},{12,13},{... | collective-permute-start | bytes 196616 | tf_op jit(solution)/shard_map/ppermute | solution.py:24
  303.9 6.8 %all-to-all-start.2 = ((s32[8,2,1]{1,2,0:T(1,128)}), s32[8,2,1]{1,2,0:T(1,128)S(1)}, u32[]{:S(2)}, u32[]{:S(2)}) async-start(s32[8,2,1]{1,2,0:T(1,128)} %bitcast.15), calls=%async_computation.2 | async-start | bytes 8192 | tf_op jit(solution)/shard_map/all_to_all | solution.py:124
  310.7 2.1 collective-permute-start.3
  312.9 3.4 collective-permute-done.3
  316.3 3.9 %fusion.26 = f32[64,1024]{1,0:T(8,128)S(1)} fusion(f32[1,1,2,768,1024]{4,3,2,1,0:T(8,128)} %param.22, f32[2,64,768]{2,1,0:T(8,128)S(1)} %constant_dynamic-update-slice_fusion), kind=kOutput, calls=%fused_computation.42 | convolution fusion | flops 603979776 | bytes 3604480 | tf_op jit(solution)/shard_map/dot_general | solution.py:38
  320.2 3.9 %fusion.28 = f32[64,1024]{1,0:T(8,128)S(1)} fusion(f32[1,1,2,768,1024]{4,3,2,1,0:T(8,128)} %param.22, f32[2,64,768]{2,1,0:T(8,128)S(1)} %constant_dynamic-update-slice_fusion), kind=kOutput, calls=%fused_computation.44 | convolution fusion | flops 603979776 | bytes 3604480 | tf_op jit(solution)/shard_map/dot_general | solution.py:41
  324.1 3.9 %fusion.50 = f32[1,64,1024]{2,1,0:T(8,128)S(1)} fusion(f32[64,1024]{1,0:T(8,128)S(1)} %fusion.26, f32[1,1,2,768,1024]{4,3,2,1,0:T(8,128)} %param.22, f32[2,64,768]{2,1,0:T(8,128)S(1)} %constant_dynamic-update-slice_fusion), kind=kOutput, calls=%fused_computation.58 | convolution fusion | flops 604045312 | bytes 3866624 | tf_op jit(solution)/shard_map/dot_general | solution.py:38
  328.0 4.0 %fusion.47 = f32[1,64,1024]{2,1,0:T(8,128)S(1)} fusion(f32[64,1024]{1,0:T(8,128)S(1)} %fusion.28, f32[1,1,2,768,1024]{4,3,2,1,0:T(8,128)} %param.22, f32[2,64,768]{2,1,0:T(8,128)S(1)} %constant_dynamic-update-slice_fusion), kind=kOutput, calls=%fused_computation.57 | convolution fusion | flops 604045312 | bytes 3866624 | tf_op jit(solution)/shard_map/dot_general | solution.py:41
  333.2 5.4 %all-to-all-start.3 = ((f32[8,2,128]{2,1,0:T(2,128)}), f32[8,2,128]{2,1,0:T(2,128)S(1)}, u32[]{:S(2)}, u32[]{:S(2)}) async-start(f32[8,2,128]{2,1,0:T(2,128)} %bitcast.24), calls=%async_computation.3 | async-start | bytes 16384 | tf_op jit(solution)/shard_map/all_to_all | solution.py:123
  339.4 4.7 %all-to-all-done.3 = f32[8,2,128]{2,1,0:T(2,128)S(1)} async-done(((f32[8,2,128]{2,1,0:T(2,128)}), f32[8,2,128]{2,1,0:T(2,128)S(1)}, u32[]{:S(2)}, u32[]{:S(2)}) %all-to-all-start.3) | async-done | bytes 8224 | tf_op jit(solution)/shard_map/all_to_all | solution.py:123
  (164 shorter events, 78.1 us)
Async XLA Ops:
  0.6 23.1 %copy-start = (f32[64,2]{0,1:T(2,128)S(1)}, f32[64,2]{0,1:T(2,128)}, u32[]{:S(2)}) copy-start(f32[64,2]{0,1:T(2,128)} %param.19) | copy-start | bytes 1540
  0.6 11.9 %copy-start.4 = (f32[32,2,64,128]{3,2,1,0:T(8,128)S(1)}, f32[32,2,64,128]{3,2,1,0:T(8,128)}, u32[]{:S(2)}) copy-start(f32[32,2,64,128]{3,2,1,0:T(8,128)} %param.15) | copy-start | bytes 6291460
  4.6 13.4 %all-to-all-start.1 = ((s32[8,4,1]{1,2,0:T(1,128)}), s32[8,4,1]{1,2,0:T(1,128)S(1)}, u32[]{:S(2)}, u32[]{:S(2)}) async-start(s32[8,4,1]{1,2,0:T(1,128)} %bitcast.6), calls=%async_computation.1 | async-start | bytes 8192 | tf_op jit(solution)/shard_map/all_to_all | solution.py:82
  17.9 5.5 %copy-start.6 = (s32[8,1]{0,1:T(1,128)S(1)}, s32[8,1]{0,1:T(1,128)}, u32[]{:S(2)}) copy-start(s32[8,1]{0,1:T(1,128)} %param.24) | copy-start | bytes 100
  17.9 5.8 %copy-start.7 = (s32[64]{0:T(128)S(1)}, s32[64]{0:T(128)}, u32[]{:S(2)}) copy-start(s32[64]{0:T(128)} %param.18) | copy-start | bytes 772
  17.9 52.4 %all-to-all-start = ((f32[32,2,64,128]{3,2,1,0:T(8,128)}), f32[32,2,64,128]{3,2,1,0:T(8,128)}, u32[]{:S(2)}, u32[]{:S(2)}) async-start(f32[32,2,64,128]{3,2,1,0:T(8,128)} %scatter_fusion), calls=%async_computation | async-start | bytes 4194304 | tf_op jit(solution)/shard_map/all_to_all | solution.py:81
  25.2 48.8 %copy-start.1 = (f32[1,1,2,512,512]{4,3,2,1,0:T(8,128)S(1)}, f32[1,1,2,512,512]{4,3,2,1,0:T(8,128)}, u32[]{:S(2)}) copy-start(f32[1,1,2,512,512]{4,3,2,1,0:T(8,128)} %param.20) | copy-start | bytes 6291460
  74.1 8.2 %collective-permute-start = (f32[2,64,512]{2,1,0:T(8,128)S(1)}, f32[2,64,512]{2,1,0:T(8,128)S(1)}, u32[]{:S(2)}, u32[]{:S(2)}) collective-permute-start(f32[2,64,512]{2,1,0:T(8,128)S(1)} %broadcast_select_fusion.4), channel_id=1, source_target_pairs={{0,4},{4,8},{8,12},{12,16},{16,20},{20,24},{24,28},{1,5},{5,9},{9,... | collective-permute-start | bytes 786440 | tf_op jit(solution)/shard_map/while/body/eval_jaxpr/ppermute | solution.py:13
  85.4 7.4 %collective-permute-start = (f32[2,64,512]{2,1,0:T(8,128)S(1)}, f32[2,64,512]{2,1,0:T(8,128)S(1)}, u32[]{:S(2)}, u32[]{:S(2)}) collective-permute-start(f32[2,64,512]{2,1,0:T(8,128)S(1)} %broadcast_select_fusion.4), channel_id=1, source_target_pairs={{0,4},{4,8},{8,12},{12,16},{16,20},{20,24},{24,28},{1,5},{5,9},{9,... | collective-permute-start | bytes 786440 | tf_op jit(solution)/shard_map/while/body/eval_jaxpr/ppermute | solution.py:13
  95.9 7.1 %collective-permute-start = (f32[2,64,512]{2,1,0:T(8,128)S(1)}, f32[2,64,512]{2,1,0:T(8,128)S(1)}, u32[]{:S(2)}, u32[]{:S(2)}) collective-permute-start(f32[2,64,512]{2,1,0:T(8,128)S(1)} %broadcast_select_fusion.4), channel_id=1, source_target_pairs={{0,4},{4,8},{8,12},{12,16},{16,20},{20,24},{24,28},{1,5},{5,9},{9,... | collective-permute-start | bytes 786440 | tf_op jit(solution)/shard_map/while/body/eval_jaxpr/ppermute | solution.py:13
  106.2 7.8 %collective-permute-start = (f32[2,64,512]{2,1,0:T(8,128)S(1)}, f32[2,64,512]{2,1,0:T(8,128)S(1)}, u32[]{:S(2)}, u32[]{:S(2)}) collective-permute-start(f32[2,64,512]{2,1,0:T(8,128)S(1)} %broadcast_select_fusion.4), channel_id=1, source_target_pairs={{0,4},{4,8},{8,12},{12,16},{16,20},{20,24},{24,28},{1,5},{5,9},{9,... | collective-permute-start | bytes 786440 | tf_op jit(solution)/shard_map/while/body/eval_jaxpr/ppermute | solution.py:13
  117.1 8.0 %collective-permute-start = (f32[2,64,512]{2,1,0:T(8,128)S(1)}, f32[2,64,512]{2,1,0:T(8,128)S(1)}, u32[]{:S(2)}, u32[]{:S(2)}) collective-permute-start(f32[2,64,512]{2,1,0:T(8,128)S(1)} %broadcast_select_fusion.4), channel_id=1, source_target_pairs={{0,4},{4,8},{8,12},{12,16},{16,20},{20,24},{24,28},{1,5},{5,9},{9,... | collective-permute-start | bytes 786440 | tf_op jit(solution)/shard_map/while/body/eval_jaxpr/ppermute | solution.py:13
  128.2 8.0 %collective-permute-start = (f32[2,64,512]{2,1,0:T(8,128)S(1)}, f32[2,64,512]{2,1,0:T(8,128)S(1)}, u32[]{:S(2)}, u32[]{:S(2)}) collective-permute-start(f32[2,64,512]{2,1,0:T(8,128)S(1)} %broadcast_select_fusion.4), channel_id=1, source_target_pairs={{0,4},{4,8},{8,12},{12,16},{16,20},{20,24},{24,28},{1,5},{5,9},{9,... | collective-permute-start | bytes 786440 | tf_op jit(solution)/shard_map/while/body/eval_jaxpr/ppermute | solution.py:13
  139.3 8.0 %collective-permute-start = (f32[2,64,512]{2,1,0:T(8,128)S(1)}, f32[2,64,512]{2,1,0:T(8,128)S(1)}, u32[]{:S(2)}, u32[]{:S(2)}) collective-permute-start(f32[2,64,512]{2,1,0:T(8,128)S(1)} %broadcast_select_fusion.4), channel_id=1, source_target_pairs={{0,4},{4,8},{8,12},{12,16},{16,20},{20,24},{24,28},{1,5},{5,9},{9,... | collective-permute-start | bytes 786440 | tf_op jit(solution)/shard_map/while/body/eval_jaxpr/ppermute | solution.py:13
  150.5 8.0 %collective-permute-start = (f32[2,64,512]{2,1,0:T(8,128)S(1)}, f32[2,64,512]{2,1,0:T(8,128)S(1)}, u32[]{:S(2)}, u32[]{:S(2)}) collective-permute-start(f32[2,64,512]{2,1,0:T(8,128)S(1)} %broadcast_select_fusion.4), channel_id=1, source_target_pairs={{0,4},{4,8},{8,12},{12,16},{16,20},{20,24},{24,28},{1,5},{5,9},{9,... | collective-permute-start | bytes 786440 | tf_op jit(solution)/shard_map/while/body/eval_jaxpr/ppermute | solution.py:13
  161.6 12.6 %copy-start.2 = (f32[2,512,512]{2,1,0:T(8,128)S(1)}, f32[2,512,512]{2,1,0:T(8,128)}, u32[]{:S(2)}) copy-start(f32[2,512,512]{2,1,0:T(8,128)} %get-tuple-element.184) | copy-start | bytes 6291460 | tf_op jit(solution)/shard_map/while
  161.6 8.6 %collective-permute-start.1 = (f32[2,64,512]{2,1,0:T(8,128)S(1)}, f32[2,64,512]{2,1,0:T(8,128)S(1)}, u32[]{:S(2)}, u32[]{:S(2)}) collective-permute-start(f32[2,64,512]{2,1,0:T(8,128)S(1)} %broadcast_select_fusion.5), channel_id=1, source_target_pairs={{4,0},{8,4},{12,8},{16,12},{20,16},{24,20},{28,24},{5,1},{9,5},{13... | collective-permute-start | bytes 786440 | tf_op jit(solution)/shard_map/while/body/eval_jaxpr/ppermute | solution.py:13
  175.7 12.6 %copy-start.2 = (f32[2,512,512]{2,1,0:T(8,128)S(1)}, f32[2,512,512]{2,1,0:T(8,128)}, u32[]{:S(2)}) copy-start(f32[2,512,512]{2,1,0:T(8,128)} %get-tuple-element.184) | copy-start | bytes 6291460 | tf_op jit(solution)/shard_map/while
  175.8 8.6 %collective-permute-start.1 = (f32[2,64,512]{2,1,0:T(8,128)S(1)}, f32[2,64,512]{2,1,0:T(8,128)S(1)}, u32[]{:S(2)}, u32[]{:S(2)}) collective-permute-start(f32[2,64,512]{2,1,0:T(8,128)S(1)} %broadcast_select_fusion.5), channel_id=1, source_target_pairs={{4,0},{8,4},{12,8},{16,12},{20,16},{24,20},{28,24},{5,1},{9,5},{13... | collective-permute-start | bytes 786440 | tf_op jit(solution)/shard_map/while/body/eval_jaxpr/ppermute | solution.py:13
  189.9 12.9 %copy-start.2 = (f32[2,512,512]{2,1,0:T(8,128)S(1)}, f32[2,512,512]{2,1,0:T(8,128)}, u32[]{:S(2)}) copy-start(f32[2,512,512]{2,1,0:T(8,128)} %get-tuple-element.184) | copy-start | bytes 6291460 | tf_op jit(solution)/shard_map/while
  189.9 8.9 %collective-permute-start.1 = (f32[2,64,512]{2,1,0:T(8,128)S(1)}, f32[2,64,512]{2,1,0:T(8,128)S(1)}, u32[]{:S(2)}, u32[]{:S(2)}) collective-permute-start(f32[2,64,512]{2,1,0:T(8,128)S(1)} %broadcast_select_fusion.5), channel_id=1, source_target_pairs={{4,0},{8,4},{12,8},{16,12},{20,16},{24,20},{28,24},{5,1},{9,5},{13... | collective-permute-start | bytes 786440 | tf_op jit(solution)/shard_map/while/body/eval_jaxpr/ppermute | solution.py:13
  204.4 12.7 %copy-start.2 = (f32[2,512,512]{2,1,0:T(8,128)S(1)}, f32[2,512,512]{2,1,0:T(8,128)}, u32[]{:S(2)}) copy-start(f32[2,512,512]{2,1,0:T(8,128)} %get-tuple-element.184) | copy-start | bytes 6291460 | tf_op jit(solution)/shard_map/while
  204.4 8.7 %collective-permute-start.1 = (f32[2,64,512]{2,1,0:T(8,128)S(1)}, f32[2,64,512]{2,1,0:T(8,128)S(1)}, u32[]{:S(2)}, u32[]{:S(2)}) collective-permute-start(f32[2,64,512]{2,1,0:T(8,128)S(1)} %broadcast_select_fusion.5), channel_id=1, source_target_pairs={{4,0},{8,4},{12,8},{16,12},{20,16},{24,20},{28,24},{5,1},{9,5},{13... | collective-permute-start | bytes 786440 | tf_op jit(solution)/shard_map/while/body/eval_jaxpr/ppermute | solution.py:13
  218.7 16.4 %copy-start.2 = (f32[2,512,512]{2,1,0:T(8,128)S(1)}, f32[2,512,512]{2,1,0:T(8,128)}, u32[]{:S(2)}) copy-start(f32[2,512,512]{2,1,0:T(8,128)} %get-tuple-element.184) | copy-start | bytes 6291460 | tf_op jit(solution)/shard_map/while
  218.7 12.4 %collective-permute-start.1 = (f32[2,64,512]{2,1,0:T(8,128)S(1)}, f32[2,64,512]{2,1,0:T(8,128)S(1)}, u32[]{:S(2)}, u32[]{:S(2)}) collective-permute-start(f32[2,64,512]{2,1,0:T(8,128)S(1)} %broadcast_select_fusion.5), channel_id=1, source_target_pairs={{4,0},{8,4},{12,8},{16,12},{20,16},{24,20},{28,24},{5,1},{9,5},{13... | collective-permute-start | bytes 786440 | tf_op jit(solution)/shard_map/while/body/eval_jaxpr/ppermute | solution.py:13
  236.7 14.8 %copy-start.2 = (f32[2,512,512]{2,1,0:T(8,128)S(1)}, f32[2,512,512]{2,1,0:T(8,128)}, u32[]{:S(2)}) copy-start(f32[2,512,512]{2,1,0:T(8,128)} %get-tuple-element.184) | copy-start | bytes 6291460 | tf_op jit(solution)/shard_map/while
  236.7 10.8 %collective-permute-start.1 = (f32[2,64,512]{2,1,0:T(8,128)S(1)}, f32[2,64,512]{2,1,0:T(8,128)S(1)}, u32[]{:S(2)}, u32[]{:S(2)}) collective-permute-start(f32[2,64,512]{2,1,0:T(8,128)S(1)} %broadcast_select_fusion.5), channel_id=1, source_target_pairs={{4,0},{8,4},{12,8},{16,12},{20,16},{24,20},{28,24},{5,1},{9,5},{13... | collective-permute-start | bytes 786440 | tf_op jit(solution)/shard_map/while/body/eval_jaxpr/ppermute | solution.py:13
  253.1 12.9 %copy-start.2 = (f32[2,512,512]{2,1,0:T(8,128)S(1)}, f32[2,512,512]{2,1,0:T(8,128)}, u32[]{:S(2)}) copy-start(f32[2,512,512]{2,1,0:T(8,128)} %get-tuple-element.184) | copy-start | bytes 6291460 | tf_op jit(solution)/shard_map/while
  253.1 8.9 %collective-permute-start.1 = (f32[2,64,512]{2,1,0:T(8,128)S(1)}, f32[2,64,512]{2,1,0:T(8,128)S(1)}, u32[]{:S(2)}, u32[]{:S(2)}) collective-permute-start(f32[2,64,512]{2,1,0:T(8,128)S(1)} %broadcast_select_fusion.5), channel_id=1, source_target_pairs={{4,0},{8,4},{12,8},{16,12},{20,16},{24,20},{28,24},{5,1},{9,5},{13... | collective-permute-start | bytes 786440 | tf_op jit(solution)/shard_map/while/body/eval_jaxpr/ppermute | solution.py:13
  267.5 11.9 %copy-start.2 = (f32[2,512,512]{2,1,0:T(8,128)S(1)}, f32[2,512,512]{2,1,0:T(8,128)}, u32[]{:S(2)}) copy-start(f32[2,512,512]{2,1,0:T(8,128)} %get-tuple-element.184) | copy-start | bytes 6291460 | tf_op jit(solution)/shard_map/while
  267.6 7.9 %collective-permute-start.1 = (f32[2,64,512]{2,1,0:T(8,128)S(1)}, f32[2,64,512]{2,1,0:T(8,128)S(1)}, u32[]{:S(2)}, u32[]{:S(2)}) collective-permute-start(f32[2,64,512]{2,1,0:T(8,128)S(1)} %broadcast_select_fusion.5), channel_id=1, source_target_pairs={{4,0},{8,4},{12,8},{16,12},{20,16},{24,20},{28,24},{5,1},{9,5},{13... | collective-permute-start | bytes 786440 | tf_op jit(solution)/shard_map/while/body/eval_jaxpr/ppermute | solution.py:13
  281.0 39.2 %copy-start.3 = (f32[2,64,512]{2,1,0:T(8,128)}, f32[2,64,512]{2,1,0:T(8,128)S(1)}, u32[]{:S(2)}) copy-start(f32[2,64,512]{2,1,0:T(8,128)S(1)} %get-tuple-element.47) | copy-start | bytes 786436
  281.0 31.8 %collective-permute-start.2 = (f32[2,64,128]{2,1,0:T(8,128)S(1)}, f32[2,64,128]{2,1,0:T(8,128)S(1)}, u32[]{:S(2)}, u32[]{:S(2)}) collective-permute-start(f32[2,64,128]{2,1,0:T(8,128)S(1)} %get-tuple-element.97), channel_id=1, source_target_pairs={{0,1},{1,2},{2,3},{4,5},{5,6},{6,7},{8,9},{9,10},{10,11},{12,13},{... | collective-permute-start | bytes 196616 | tf_op jit(solution)/shard_map/ppermute | solution.py:24
  303.9 29.3 %all-to-all-start.2 = ((s32[8,2,1]{1,2,0:T(1,128)}), s32[8,2,1]{1,2,0:T(1,128)S(1)}, u32[]{:S(2)}, u32[]{:S(2)}) async-start(s32[8,2,1]{1,2,0:T(1,128)} %bitcast.15), calls=%async_computation.2 | async-start | bytes 8192 | tf_op jit(solution)/shard_map/all_to_all | solution.py:124
  310.7 5.6 %collective-permute-start.3 = (f32[2,64,128]{2,1,0:T(8,128)S(1)}, f32[2,64,128]{2,1,0:T(8,128)S(1)}, u32[]{:S(2)}, u32[]{:S(2)}) collective-permute-start(f32[2,64,128]{2,1,0:T(8,128)S(1)} %get-tuple-element.96), channel_id=1, source_target_pairs={{1,0},{2,1},{3,2},{5,4},{6,5},{7,6},{9,8},{10,9},{11,10},{13,12},{... | collective-permute-start | bytes 196616 | tf_op jit(solution)/shard_map/ppermute | solution.py:26
  328.0 4.0 %copy-start.5 = (f32[1,1,2,64,1024]{4,3,2,1,0:T(8,128)S(1)}, f32[1,1,2,64,1024]{4,3,2,1,0:T(8,128)}, u32[]{:S(2)}) copy-start(f32[1,1,2,64,1024]{4,3,2,1,0:T(8,128)} %param.23) | copy-start | bytes 1572868
  333.2 10.8 %all-to-all-start.3 = ((f32[8,2,128]{2,1,0:T(2,128)}), f32[8,2,128]{2,1,0:T(2,128)S(1)}, u32[]{:S(2)}, u32[]{:S(2)}) async-start(f32[8,2,128]{2,1,0:T(2,128)} %bitcast.24), calls=%async_computation.3 | async-start | bytes 16384 | tf_op jit(solution)/shard_map/all_to_all | solution.py:123
where the time goes:
time: 347 us; the launch traced here: 345 us
  waiting for transfers between devices  144 us (41%)
  starting transfers between devices  94.5 us (27%)
  matrix products  88 us (25%)
  local copies, waits for them, and re-layouts  10.8 us (3%)
  other arithmetic  6.31 us (2%)
    ppermute x16, waiting for transfers between devices, shifted(): return lax.ppermute(block, axis, route)  90.4 us
    all_to_all x2, waiting for transfers between devices, body(): lax.all_to_all(outgoing, 'slab', split_axis=0, concat_axis=0, tiled=True)  49.7 us
    ppermute x16, starting transfers between devices, shifted(): return lax.ppermute(block, axis, route)  46.8 us
    dot_general x17, matrix products, complex_product(): jnp.matmul(value_im, panel_re, precision=lax.Precision.HIGHEST)  25.8 us
    dot_general x17, matrix products, complex_product(): jnp.matmul(value_im, panel_im, precision=lax.Precision.HIGHEST)  25.6 us
    ppermute x1, starting transfers between devices, padded(): lax.ppermute(tail, axis, [(i, (i + 1) % count) for i in range(ends)])  21.5 us
    dot_general x17, matrix products, complex_product(): jnp.matmul(value_re, panel_im, precision=lax.Precision.HIGHEST)  16.1 us
    dot_general x17, matrix products, complex_product(): jnp.matmul(value_re, panel_re, precision=lax.Precision.HIGHEST)  16 us
  transfers between devices with their start and end apart: 22, of which 19 were waited for; matrix products, arithmetic and copies ran while one was open for 8% of the time, Pallas kernels for 0%

commit v1 on v0

v1 whole, which is shorter than its diff:
```python
import functools

import jax
import jax.numpy as jnp
from jax import lax
from jax.experimental import pallas as pl
from jax.experimental.pallas import tpu as pltpu
from jax.sharding import PartitionSpec as P

MBLK = 8
VMEM = pl.BlockSpec(memory_space=pltpu.VMEM)
SMEM = pl.BlockSpec(memory_space=pltpu.SMEM)
ANY = pl.BlockSpec(memory_space=pl.ANY)
LIMIT = 40 * 1024 * 1024


def split(value):
    high = value.astype(jnp.bfloat16)
    low = (value - high.astype(jnp.float32)).astype(jnp.bfloat16)
    return high, low


def product(vector, high, low):
    m, n = vector.shape[1], high.shape[1] // 2
    top, rest = split(vector.reshape(2 * m, -1))
    wide = jnp.dot(top, high, preferred_element_type=jnp.float32)
    wide += jnp.dot(rest, high, preferred_element_type=jnp.float32)
    wide += jnp.dot(top, low, preferred_element_type=jnp.float32)
    return wide[:m, :n] - wide[m:, n:], wide[:m, n:] + wide[m:, :n]


def halves_kernel(panel_ref, high_ref, low_ref):
    n = panel_ref.shape[-1]
    for part in range(2):
        high, low = split(panel_ref[part])
        high_ref[:, part * n : (part + 1) * n] = high
        low_ref[:, part * n : (part + 1) * n] = low


def halves(panel, rows=128):
    _, k, n = panel.shape
    block = pl.BlockSpec((rows, 2 * n), lambda i: (i, 0))
    return pl.pallas_call(
        halves_kernel,
        grid=(k // rows,),
        in_specs=[pl.BlockSpec((2, rows, n), lambda i: (0, i, 0))],
        out_specs=[block, block],
        out_shape=[jax.ShapeDtypeStruct((k, 2 * n), jnp.bfloat16)] * 2,
        compiler_params=pltpu.CompilerParams(vmem_limit_bytes=LIMIT),
        name="halves",
    )(panel)


def collect_kernel(group_ref, slab_ref, pos_ref, blocks_ref, *outs):
    groups = len(outs)
    width = blocks_ref.shape[-1]
    for out in outs:
        out[...] = jnp.zeros_like(out)

    def place(row, carry):
        slab = slab_ref[row, 0]
        group = lax.rem(lax.div(slab, 2) - group_ref[0] + groups, groups)
        side = lax.rem(slab, 2)
        lanes = pl.ds(pl.multiple_of(pos_ref[row] * width, width), width)
        for number, out in enumerate(outs):

            @pl.when(group == number)
            def _():
                for part in range(2):
                    out[side, part, :, lanes] += blocks_ref[row, part]

        return carry

    lax.fori_loop(0, blocks_ref.shape[0], place, 0)


def collect(group, slab, pos, blocks, groups, trace):
    _, _, shots, _ = blocks.shape
    return pl.pallas_call(
        collect_kernel,
        in_specs=[SMEM, SMEM, SMEM, VMEM],
        out_specs=[VMEM] * groups,
        out_shape=[jax.ShapeDtypeStruct((2, 2, shots, trace), jnp.float32)] * groups,
        compiler_params=pltpu.CompilerParams(vmem_limit_bytes=LIMIT),
        name="collect",
    )(group, slab, pos, blocks)


def pair_kernel(odd_ref, arrived_ref, dh_ref, dl_ref, uh_ref, ul_ref, high_ref, low_ref):
    n = high_ref.shape[-1] // 2

    def run(high, low):
        for part, value in enumerate(product(arrived_ref[...], high[...], low[...])):
            top, rest = split(value)
            high_ref[:, part * n : (part + 1) * n] = top
            low_ref[:, part * n : (part + 1) * n] = rest

    @pl.when(odd_ref[0] == 1)
    def _():
        run(dh_ref, dl_ref)

    @pl.when(odd_ref[0] == 0)
    def _():
        run(uh_ref, ul_ref)


def pair_panel(odd, arrived, down, up, rows=128):
    _, k, n = arrived.shape
    whole = pl.BlockSpec((k, 2 * n), lambda i: (0, 0))
    block = pl.BlockSpec((rows, 2 * n), lambda i: (i, 0))
    return pl.pallas_call(
        pair_kernel,
        grid=(k // rows,),
        in_specs=[SMEM, pl.BlockSpec((2, rows, n), lambda i: (0, i, 0))] + [whole] * 4,
        out_specs=[block, block],
        out_shape=[jax.ShapeDtypeStruct((k, 2 * n), jnp.bfloat16)] * 2,
        compiler_params=pltpu.CompilerParams(vmem_limit_bytes=LIMIT),
        name="pair_panel",
    )(odd, arrived, *down, *up)


def step_kernel(active_ref, arrived_ref, high_ref, low_ref, own_ref, old_ref, out_ref):
    @pl.when(active_ref[0] == 1)
    def _():
        real, imag = product(arrived_ref[...], high_ref[...], low_ref[...])
        out_ref[0] = real + own_ref[0]
        out_ref[1] = imag + own_ref[1]

    @pl.when(active_ref[0] == 0)
    def _():
        out_ref[...] = old_ref[...]


def step(active, arrived, panel, own, old):
    return pl.pallas_call(
        step_kernel,
        in_specs=[SMEM] + [VMEM] * 5,
        out_specs=VMEM,
        out_shape=jax.ShapeDtypeStruct(own.shape, jnp.float32),
        compiler_params=pltpu.CompilerParams(vmem_limit_bytes=LIMIT),
        name="step",
    )(active, arrived, *panel, own, old)


def middle_kernel(field_ref, high_ref, low_ref, out_ref):
    real, imag = product(field_ref[...], high_ref[...], low_ref[...])
    out_ref[0] = real
    out_ref[1] = imag


def middle(field, high, low, width):
    _, shots, trace = field.shape
    n = high.shape[-1] // 2
    return pl.pallas_call(
        middle_kernel,
        in_specs=[VMEM] * 3,
        out_specs=VMEM,
        out_shape=jax.ShapeDtypeStruct((2, shots, n), jnp.float32),
        compiler_params=pltpu.CompilerParams(vmem_limit_bytes=LIMIT),
        name="middle",
    )(field, high[width : width + trace], low[width : width + trace])


def rim_kernel(owner_ref, slot_ref, part_ref, left_ref, right_ref, *refs):
    lh_ref, ll_ref, rh_ref, rl_ref, forward_ref, out_ref = refs
    shots, width = left_ref.shape[1], left_ref.shape[2]
    real, imag = product(left_ref[...], lh_ref[...], ll_ref[...])
    more_real, more_imag = product(right_ref[...], rh_ref[...], rl_ref[...])
    total = forward_ref[0] * (part_ref[0] + real + more_real)
    total += forward_ref[1] * (part_ref[1] + imag + more_imag)
    gradient = jnp.sum(total, axis=0, keepdims=True) * shots ** (-0.5)
    out_ref[...] = jnp.zeros_like(out_ref)
    for block in range(gradient.shape[1] // width):
        row = owner_ref[block, 0] * MBLK + slot_ref[block]
        out_ref[pl.ds(row, 1), :] += gradient[:, block * width : (block + 1) * width]


def rim(owner, slot, part, left, right, high, low, forward, slabs):
    width = left.shape[2]
    return pl.pallas_call(
        rim_kernel,
        in_specs=[SMEM, SMEM] + [VMEM] * 8,
        out_specs=VMEM,
        out_shape=jax.ShapeDtypeStruct((slabs * MBLK, width), jnp.float32),
        compiler_params=pltpu.CompilerParams(vmem_limit_bytes=LIMIT),
        name="rim",
    )(owner, slot, part, left, right, high[:width], low[:width], high[-width:], low[-width:], forward)


def body(
    residual_blocks,
    residual_slab,
    residual_pos,
    shot_ids,
    wavelet,
    down_panel,
    up_panel,
    recovery,
    forward_field,
    element_owner,
    element_slot,
):
    slabs = lax.axis_size("slab")
    lats = lax.axis_size("lat")
    groups = slabs // 2
    shots, width = residual_blocks.shape[2:]
    trace = down_panel.shape[-1]
    me = lax.axis_index("slab").astype(jnp.int32)
    group, odd = me // 2, me % 2
    is_odd = odd == 1

    def flag(condition):
        return condition.astype(jnp.int32).reshape(1)

    def hop(value, route):
        return lax.ppermute(value, "slab", route)

    parts = collect(
        group.reshape(1), residual_slab, residual_pos, residual_blocks, groups, trace
    )
    summed = parts[0]
    for turn in range(1, groups):
        summed = summed + hop(parts[turn], [(s, (s + 2 * turn) % slabs) for s in range(slabs)])

    panel_out = jnp.where(is_odd, up_panel[0, 0], down_panel[0, 0])
    panel_in = hop(panel_out, [(s, s ^ 1) for s in range(slabs)])
    down = halves(down_panel[0, 0])
    up = halves(up_panel[0, 0])
    maps = halves(recovery[0, 0])
    pair = pair_panel(odd.reshape(1), panel_in, down, up)

    picker = shot_ids[:, None] == jnp.arange(shots, dtype=jnp.int32)[None, :]
    weights = jnp.sum(jnp.where(picker[:, :, None], wavelet[None], 0.0), axis=1)
    weight_re, weight_im = weights[:, 0:1], weights[:, 1:2]

    def weighted(value):
        return jnp.stack(
            [
                weight_re * value[0] - weight_im * value[1],
                weight_re * value[1] + weight_im * value[0],
            ]
        )

    source_even = weighted(summed[0] + hop(summed[0], [(s, s ^ 1) for s in range(slabs)]))
    source_odd = weighted(summed[1] + hop(summed[1], [(s, s + 1) for s in range(0, slabs, 2)]))

    own = step(flag(is_odd), source_even, down, source_odd, source_odd)
    state = own
    for k in range(1, groups):
        arrived = hop(state, [(2 * k - 1, 2 * k + 1)])
        state = step(flag(me == 2 * k + 1), arrived, pair, own, state)
    before = hop(state, [(2 * k - 1, 2 * k) for k in range(1, groups)])
    beside = hop(state, [(2 * k + 1, 2 * k) for k in range(groups)])
    even_down = step(flag(~is_odd), before, down, source_even, source_even)
    own = step(flag(~is_odd), beside, up, even_down, even_down)
    above = own
    for k in range(groups - 2, -1, -1):
        arrived = hop(above, [(2 * k + 2, 2 * k)])
        above = step(flag(me == 2 * k), arrived, pair, own, above)
    after = hop(above, [(2 * k + 2, 2 * k + 1) for k in range(groups - 1)])
    ups = step(flag(is_odd), after, up, state, above)

    left = lax.ppermute(ups[:, :, trace - width :], "lat", [(i, i + 1) for i in range(lats - 1)])
    right = lax.ppermute(ups[:, :, :width], "lat", [(i + 1, i) for i in range(lats - 1)])
    part = middle(ups, *maps, width)
    outgoing = rim(
        element_owner, element_slot, part, left, right, *maps, forward_field[0, 0], slabs
    )
    arrived = lax.all_to_all(outgoing, "slab", split_axis=0, concat_axis=0, tiled=True)
    model = jnp.sum(arrived.reshape(slabs, MBLK, width), axis=0)
    return (ups[None, None], model[None, None])


def solution(mesh):
    placed = (
        P(("slab", "lat"), None, None, None),
        P(("slab", "lat"), None),
        P(("slab", "lat")),
        P(),
        P(),
        P("slab", "lat", None, None, None),
        P("slab", "lat", None, None, None),
        P("slab", "lat", None, None, None),
        P("slab", "lat", None, None, None),
        P(("slab", "lat"), None),
        P(("slab", "lat")),
    )
    return jax.shard_map(
        body,
        mesh=mesh,
        in_specs=placed,
        out_specs=(P("slab", "lat", None, None, None), P("slab", "lat", None, None)),
        check_vma=False,
    )
```

time: 347 us -> 186 us (0.54)
  matrix products: 88 us -> 0 us
  starting transfers between devices: 94.5 us -> 28.7 us
  waiting for transfers between devices: 144 us -> 90.9 us
  Pallas kernels: 0 us -> 28.2 us
  local copies, waits for them, and re-layouts: 10.8 us -> 20.4 us
  blocking collectives: 0 us -> 8.15 us
    dot_general x71 -> x0, matrix products: 88 us -> none  [the longest x17 25.8 us: complex_product(): jnp.matmul(value_im, panel_re, precision=lax.Precision.HIGHEST)]
    all_to_all x4 -> x0, waiting for transfers between devices: 49.7 us -> none  [the longest x2 49.7 us: body(): lax.all_to_all(outgoing, 'slab', split_axis=0, concat_axis=0, tiled=True)]
    ppermute x18 -> x17, starting transfers between devices: 70.4 us -> 28.7 us  [the longest x15 21.4 us: hop(): return lax.ppermute(value, 'slab', route)]
    pallas_call x0 -> x17, Pallas kernels: none -> 28.2 us  [the longest x10 14 us: step(): pl.pallas_call(step_kernel, in_specs=[SMEM] + [VMEM] * 5, out_specs=VMEM,...]
    all_to_all x4 -> x0, starting transfers between devices: 24.1 us -> none  [the longest x2 11 us: body(): lax.all_to_all(outgoing, 'slab', split_axis=0, concat_axis=0, tiled=True)]
    unnamed x16 -> x62, local copies, waits for them, and re-layouts: 0.06 us -> 15 us
    all_to_all x0 -> x1, blocking collectives: none -> 8.15 us  [body(): lax.all_to_all(outgoing, 'slab', split_axis=0, concat_axis=0, tiled=True)]
    scatter x3 -> x0, local copies, waits for them, and re-layouts: 6.95 us -> none  [the longest x1 5.42 us: body(): outgoing = jnp.zeros((slab_count * capacity, 2, shots, width), jnp.float3...]
  transfers between devices with their start and end apart: 22 -> 17, of which waited for: 19 -> 6; matrix products, arithmetic and copies ran while one was open for 8% -> 6% of each run, Pallas kernels for 0% -> 6%
where the time goes in v1:
time: 186 us; the launch traced here: 184 us
  waiting for transfers between devices  90.9 us (49%)
  starting transfers between devices  28.7 us (15%)
  Pallas kernels  28.2 us (15%)
  local copies, waits for them, and re-layouts  20.4 us (11%)
  blocking collectives  8.15 us (4%)
  other arithmetic  6.95 us (4%)
    ppermute x15, waiting for transfers between devices, hop(): return lax.ppermute(value, 'slab', route)  90.9 us
    ppermute x15, starting transfers between devices, hop(): return lax.ppermute(value, 'slab', route)  21.4 us
    unnamed x62, local copies, waits for them, and re-layouts  15 us
    pallas_call x10, Pallas kernels, step(): pl.pallas_call(step_kernel, in_specs=[SMEM] + [VMEM] * 5, out_specs=VMEM,...  14 us
    all_to_all x1, blocking collectives, body(): lax.all_to_all(outgoing, 'slab', split_axis=0, concat_axis=0, tiled=True)  8.15 us
    pallas_call x1, Pallas kernels, pair_panel(): pl.pallas_call(pair_kernel, grid=(k // rows,), in_specs=[SMEM, pl.BlockSp...  5.48 us
    ppermute x1, starting transfers between devices, body(): lax.ppermute(ups[:, :, :width], 'lat', [(i + 1, i) for i in range(lats -...  4.28 us
  transfers between devices with their start and end apart: 17, of which 6 were waited for; matrix products, arithmetic and copies ran while one was open for 6% of the time, Pallas kernels for 6%

profile of v1, /device:TPU:1, one launch (start us, length us, event | category | flops | bytes accessed | tf_op | source)
XLA Modules:
  0.0 184.4 jit_solution(5068380552069437283)
XLA Ops:
  1.5 1.6 copy-done.15
  3.8 3.4 %collect.1 = (f32[2,2,64,512]{3,2,1,0:T(8,128)S(1)}, f32[2,2,64,512]{3,2,1,0:T(8,128)S(1)}, f32[2,2,64,512]{3,2,1,0:T(8,128)}, f32[2,2,64,512]{3,2,1,0:T(8,128)}) custom-call(s32[1]{0:T(128)} %bitcast.9.group_ref, s32[32,1]{1,0:T(8,128)S(1)} %copy.16.slab_ref, s32[32]{0:T(128)S(1)} %copy-done.23, f32[32,2,64,128]{3,2,1,0:T(8,128)S(1)} %copy-done.15), custom_call_target="tpu_custom_call" | custom-call | tf_op jit(solution)/shard_map/collect/pallas_call | solution.py:79
  7.2 2.1 %collective-permute-start = (f32[2,2,64,512]{3,2,1,0:T(8,128)S(1)}, f32[2,2,64,512]{3,2,1,0:T(8,128)}, u32[]{:S(2)}, u32[]{:S(2)}) collective-permute-start(f32[2,2,64,512]{3,2,1,0:T(8,128)S(1)} %get-tuple-element.15), channel_id=1, source_target_pairs={{0,8},{4,12},{8,16},{12,20},{16,24},{20,28},{24,0},{28,4},{1,9},{5... | collective-permute-start | bytes 1572872 | tf_op jit(solution)/shard_map/ppermute | solution.py:216
  9.3 2.3 %collective-permute-start.1 = (f32[2,2,64,512]{3,2,1,0:T(8,128)}, f32[2,2,64,512]{3,2,1,0:T(8,128)}, u32[]{:S(2)}, u32[]{:S(2)}) collective-permute-start(f32[2,2,64,512]{3,2,1,0:T(8,128)} %get-tuple-element.16), channel_id=1, source_target_pairs={{0,16},{4,20},{8,24},{12,28},{16,0},{20,4},{24,8},{28,12},{1,17},{... | collective-permute-start | bytes 1572872 | tf_op jit(solution)/shard_map/ppermute | solution.py:216
  11.6 1.1 collective-permute-start.2
  12.7 3.4 %broadcast_select_fusion = f32[2,512,512]{2,1,0:T(8,128)} fusion(pred[]{:T(512)S(6)} %eq.40, f32[1,1,2,512,512]{4,3,2,1,0:T(8,128)} %param.17, f32[1,1,2,512,512]{4,3,2,1,0:T(8,128)S(1)} %copy-done.9), kind=kLoop, calls=%fused_computation | loop fusion | flops 524288 | bytes 6291457 | tf_op jit(solution)/shard_map/jit(_where)/select_n | solution.py:225
  16.1 1.2 collective-permute-start.6
  17.4 5.7 %collective-permute-done = f32[2,2,64,512]{3,2,1,0:T(8,128)} collective-permute-done((f32[2,2,64,512]{3,2,1,0:T(8,128)S(1)}, f32[2,2,64,512]{3,2,1,0:T(8,128)}, u32[]{:S(2)}, u32[]{:S(2)}) %collective-permute-start) | collective-permute-done | bytes 524320 | tf_op jit(solution)/shard_map/ppermute | solution.py:216
  23.2 23.2 %collective-permute-done.1 = f32[2,2,64,512]{3,2,1,0:T(8,128)} collective-permute-done((f32[2,2,64,512]{3,2,1,0:T(8,128)}, f32[2,2,64,512]{3,2,1,0:T(8,128)}, u32[]{:S(2)}, u32[]{:S(2)}) %collective-permute-start.1) | collective-permute-done | bytes 524320 | tf_op jit(solution)/shard_map/ppermute | solution.py:216
  46.4 1.6 add_add_fusion
  48.8 3.1 %collective-permute-start.4 = (f32[2,64,512]{2,1,0:T(8,128)}, f32[2,64,512]{2,1,0:T(8,128)S(1)}, u32[]{:S(2)}, u32[]{:S(2)}) collective-permute-start(f32[2,64,512]{2,1,0:T(8,128)} %get-tuple-element.32), channel_id=1, source_target_pairs={{0,4},{8,12},{16,20},{24,28},{1,5},{9,13},{17,21},{25,29},{2,6},{1... | collective-permute-start | bytes 786440 | tf_op jit(solution)/shard_map/ppermute | solution.py:216
  52.8 13.9 %collective-permute-done.4 = f32[2,64,512]{2,1,0:T(8,128)S(1)} collective-permute-done((f32[2,64,512]{2,1,0:T(8,128)}, f32[2,64,512]{2,1,0:T(8,128)S(1)}, u32[]{:S(2)}, u32[]{:S(2)}) %collective-permute-start.4) | collective-permute-done | bytes 262176 | tf_op jit(solution)/shard_map/ppermute | solution.py:216
  66.7 5.6 %collective-permute-done.3 = f32[2,64,512]{2,1,0:T(8,128)} collective-permute-done((f32[2,64,512]{2,1,0:T(8,128)}, f32[2,64,512]{2,1,0:T(8,128)}, u32[]{:S(2)}, u32[]{:S(2)}) %collective-permute-start.3) | collective-permute-done | bytes 262176 | tf_op jit(solution)/shard_map/ppermute | solution.py:216
  72.3 1.0 fusion.1
  73.6 1.4 collective-permute-start.5
  75.0 1.7 copy-done.10
  77.3 5.5 %pair_panel.1 = (bf16[512,1024]{1,0:T(8,128)(2,1)S(1)}, bf16[512,1024]{1,0:T(8,128)(2,1)S(1)}) custom-call(s32[1]{0:T(128)} %bitcast.14.odd_ref, f32[2,512,512]{2,1,0:T(8,128)} %collective-permute-done.6.arrived_ref, bf16[512,1024]{1,0:T(8,128)(2,1)S(1)} %copy-done.4, bf16[512,1024]{1,0:T(8,128)(2,1)S(1)} %copy-done.7, ...), custom_call_target="tpu_custom_call" | custom-call | tf_op jit(solution)/shard_map/pair_panel/pallas_call | solution.py:111
  82.8 1.7 step.11.old_ref
  84.5 1.4 collective-permute-start.7
  85.9 1.7 step.12.old_ref
  87.6 1.4 collective-permute-start.8
  89.0 1.8 step.13.own_ref
  90.7 1.3 collective-permute-start.10
  92.1 1.3 collective-permute-start.9
  93.4 1.3 copy-done.5
  94.7 1.2 copy-done.8
  96.9 1.5 step.14.own_ref.old_ref
  98.4 7.1 %collective-permute-done.9.arrived_ref = f32[2,64,512]{2,1,0:T(8,128)S(1)} collective-permute-done((f32[2,64,512]{2,1,0:T(8,128)}, f32[2,64,512]{2,1,0:T(8,128)S(1)}, u32[]{:S(2)}, u32[]{:S(2)}) %collective-permute-start.9) | collective-permute-done | bytes 262176 | tf_op jit(solution)/shard_map/ppermute | solution.py:216
  106.2 0.9 copy-done.22
  107.8 1.4 collective-permute-start.11
  109.1 1.7 step.16.old_ref
  110.8 1.4 collective-permute-start.12
  112.1 1.7 step.17.old_ref
  113.9 1.3 collective-permute-start.13
  115.2 35.4 %collective-permute-done.13.arrived_ref = f32[2,64,512]{2,1,0:T(8,128)} collective-permute-done((f32[2,64,512]{2,1,0:T(8,128)}, f32[2,64,512]{2,1,0:T(8,128)}, u32[]{:S(2)}, u32[]{:S(2)}) %collective-permute-start.13) | collective-permute-done | bytes 262176 | tf_op jit(solution)/shard_map/ppermute | solution.py:216
  150.5 1.6 step.18.old_ref
  152.9 2.8 %copy-done.12 = f32[1,1,2,768,1024]{4,3,2,1,0:T(8,128)S(1)} copy-done((f32[1,1,2,768,1024]{4,3,2,1,0:T(8,128)S(1)}, f32[1,1,2,768,1024]{4,3,2,1,0:T(8,128)}, u32[]{:S(2)}) %copy-start.12) | copy-done | bytes 6291480
  155.7 1.6 halves.5
  157.3 1.7 step.19.field_ref
  159.0 1.5 fusion.4
  160.5 4.3 %collective-permute-start.16 = (f32[2,64,128]{2,1,0:T(8,128)}, f32[2,64,128]{2,1,0:T(8,128)S(1)}, u32[]{:S(2)}, u32[]{:S(2)}) collective-permute-start(f32[2,64,128]{2,1,0:T(8,128)} %get-tuple-element.38), channel_id=1, source_target_pairs={{1,0},{2,1},{3,2},{5,4},{6,5},{7,6},{9,8},{10,9},{11,10},{13,12},{... | collective-permute-start | bytes 196616 | tf_op jit(solution)/shard_map/ppermute | solution.py:264
  164.8 3.0 %collective-permute-start.15 = (f32[2,64,128]{2,1,0:T(8,128)}, f32[2,64,128]{2,1,0:T(8,128)S(1)}, u32[]{:S(2)}, u32[]{:S(2)}) collective-permute-start(f32[2,64,128]{2,1,0:T(8,128)} %get-tuple-element.39), channel_id=1, source_target_pairs={{0,1},{1,2},{2,3},{4,5},{5,6},{6,7},{8,9},{9,10},{10,11},{12,13},{... | collective-permute-start | bytes 196616 | tf_op jit(solution)/shard_map/ppermute | solution.py:263
  167.8 1.2 fusion.2
  169.3 1.6 slice.63.low_ref
  171.0 1.6 copy-done.11
  172.6 1.0 middle.1.part_ref
  174.1 1.6 rim.1
  175.7 8.1 %all_to_all.9 = f32[8,8,128]{2,1,0:T(8,128)S(1)} all-to-all(f32[8,8,128]{2,1,0:T(8,128)S(1)} %bitcast.36), channel_id=1, replica_groups=mesh['slab'=8,'lat'=4] {'slab'}, dimensions={0} | all-to-all | bytes 65536 | tf_op jit(solution)/shard_map/all_to_all | solution.py:269
  (80 shorter events, 8.4 us)
Async XLA Ops:
  0.6 12.1 %copy-start.9 = (f32[1,1,2,512,512]{4,3,2,1,0:T(8,128)S(1)}, f32[1,1,2,512,512]{4,3,2,1,0:T(8,128)}, u32[]{:S(2)}) copy-start(f32[1,1,2,512,512]{4,3,2,1,0:T(8,128)} %param.16) | copy-start | bytes 6291460
  1.5 1.6 copy-start.15
  3.1 0.7 copy-start.23
  7.2 16.0 %collective-permute-start = (f32[2,2,64,512]{3,2,1,0:T(8,128)S(1)}, f32[2,2,64,512]{3,2,1,0:T(8,128)}, u32[]{:S(2)}, u32[]{:S(2)}) collective-permute-start(f32[2,2,64,512]{3,2,1,0:T(8,128)S(1)} %get-tuple-element.15), channel_id=1, source_target_pairs={{0,8},{4,12},{8,16},{12,20},{16,24},{20,28},{24,0},{28,4},{1,9},{5... | collective-permute-start | bytes 1572872 | tf_op jit(solution)/shard_map/ppermute | solution.py:216
  9.3 37.0 %collective-permute-start.1 = (f32[2,2,64,512]{3,2,1,0:T(8,128)}, f32[2,2,64,512]{3,2,1,0:T(8,128)}, u32[]{:S(2)}, u32[]{:S(2)}) collective-permute-start(f32[2,2,64,512]{3,2,1,0:T(8,128)} %get-tuple-element.16), channel_id=1, source_target_pairs={{0,16},{4,20},{8,24},{12,28},{16,0},{20,4},{24,8},{28,12},{1,17},{... | collective-permute-start | bytes 1572872 | tf_op jit(solution)/shard_map/ppermute | solution.py:216
  11.6 34.7 %collective-permute-start.2 = (f32[2,2,64,512]{3,2,1,0:T(8,128)}, f32[2,2,64,512]{3,2,1,0:T(8,128)}, u32[]{:S(2)}, u32[]{:S(2)}) collective-permute-start(f32[2,2,64,512]{3,2,1,0:T(8,128)} %get-tuple-element.17), channel_id=1, source_target_pairs={{0,24},{4,28},{8,0},{12,4},{16,8},{20,12},{24,16},{28,20},{1,25},{... | collective-permute-start | bytes 1572872 | tf_op jit(solution)/shard_map/ppermute | solution.py:216
  12.7 4.7 %copy-start.28 = (s32[64]{0:T(128)S(1)}, s32[64]{0:T(128)}, u32[]{:S(2)}) copy-start(s32[64]{0:T(128)} %param.14) | copy-start | bytes 772
  16.1 36.0 %copy-start.27 = (f32[64,2]{0,1:T(2,128)S(1)}, f32[64,2]{0,1:T(2,128)}, u32[]{:S(2)}) copy-start(f32[64,2]{0,1:T(2,128)} %param.15) | copy-start | bytes 1540
  16.1 61.2 %collective-permute-start.6 = (f32[2,512,512]{2,1,0:T(8,128)}, f32[2,512,512]{2,1,0:T(8,128)}, u32[]{:S(2)}, u32[]{:S(2)}) collective-permute-start(f32[2,512,512]{2,1,0:T(8,128)} %broadcast_select_fusion), channel_id=1, source_target_pairs={{0,4},{4,0},{8,12},{12,8},{16,20},{20,16},{24,28},{28,24},{1,5},{5... | collective-permute-start | bytes 6291464 | tf_op jit(solution)/shard_map/ppermute | solution.py:216
  47.9 4.2 %copy-start.25 = (f32[2,2,64,512]{3,2,1,0:T(8,128)}, f32[2,2,64,512]{3,2,1,0:T(8,128)S(1)}, u32[]{:S(2)}) copy-start(f32[2,2,64,512]{3,2,1,0:T(8,128)S(1)} %add_add_fusion) | copy-start | bytes 1572868
  48.8 17.9 %collective-permute-start.4 = (f32[2,64,512]{2,1,0:T(8,128)}, f32[2,64,512]{2,1,0:T(8,128)S(1)}, u32[]{:S(2)}, u32[]{:S(2)}) collective-permute-start(f32[2,64,512]{2,1,0:T(8,128)} %get-tuple-element.32), channel_id=1, source_target_pairs={{0,4},{8,12},{16,20},{24,28},{1,5},{9,13},{17,21},{25,29},{2,6},{1... | collective-permute-start | bytes 786440 | tf_op jit(solution)/shard_map/ppermute | solution.py:216
  52.0 20.3 %collective-permute-start.3 = (f32[2,64,512]{2,1,0:T(8,128)}, f32[2,64,512]{2,1,0:T(8,128)}, u32[]{:S(2)}, u32[]{:S(2)}) collective-permute-start(f32[2,64,512]{2,1,0:T(8,128)} %get-tuple-element.33), channel_id=1, source_target_pairs={{0,4},{4,0},{8,12},{12,8},{16,20},{20,16},{24,28},{28,24},{1,5},{5... | collective-permute-start | bytes 786440 | tf_op jit(solution)/shard_map/ppermute | solution.py:216
  52.2 20.1 %copy-start.26 = (f32[2,2,64,512]{3,2,1,0:T(8,128)S(1)}, f32[2,2,64,512]{3,2,1,0:T(8,128)}, u32[]{:S(2)}) copy-start(f32[2,2,64,512]{3,2,1,0:T(8,128)} %copy-done.25) | copy-start | bytes 1572868
  52.8 20.8 %copy-start.3 = (bf16[512,1024]{1,0:T(8,128)(2,1)}, bf16[512,1024]{1,0:T(8,128)(2,1)S(1)}, u32[]{:S(2)}) copy-start(bf16[512,1024]{1,0:T(8,128)(2,1)S(1)} %get-tuple-element.18.high_ref.dh_ref) | copy-start | bytes 3145732
  52.8 20.8 %copy-start.6 = (bf16[512,1024]{1,0:T(8,128)(2,1)}, bf16[512,1024]{1,0:T(8,128)(2,1)S(1)}, u32[]{:S(2)}) copy-start(bf16[512,1024]{1,0:T(8,128)(2,1)S(1)} %get-tuple-element.19.low_ref.dl_ref) | copy-start | bytes 3145732
  73.5 1.5 copy-start.13
  73.6 9.2 %collective-permute-start.5 = (f32[2,64,512]{2,1,0:T(8,128)S(1)}, f32[2,64,512]{2,1,0:T(8,128)}, u32[]{:S(2)}, u32[]{:S(2)}) collective-permute-start(f32[2,64,512]{2,1,0:T(8,128)S(1)} %step.10.own_ref.old_ref), channel_id=1, source_target_pairs={{4,12},{5,13},{6,14},{7,15}} | collective-permute-start | bytes 786440 | tf_op jit(solution)/shard_map/ppermute | solution.py:216
  75.0 2.3 %copy-start.4 = (bf16[512,1024]{1,0:T(8,128)(2,1)S(1)}, bf16[512,1024]{1,0:T(8,128)(2,1)}, u32[]{:S(2)}) copy-start(bf16[512,1024]{1,0:T(8,128)(2,1)} %copy-done.3) | copy-start | bytes 3145732
  75.0 2.3 %copy-start.7 = (bf16[512,1024]{1,0:T(8,128)(2,1)S(1)}, bf16[512,1024]{1,0:T(8,128)(2,1)}, u32[]{:S(2)}) copy-start(bf16[512,1024]{1,0:T(8,128)(2,1)} %copy-done.6) | copy-start | bytes 3145732
  75.0 1.7 copy-start.10
  77.3 5.5 %copy-start = (bf16[512,1024]{1,0:T(8,128)(2,1)}, bf16[512,1024]{1,0:T(8,128)(2,1)S(1)}, u32[]{:S(2)}) copy-start(bf16[512,1024]{1,0:T(8,128)(2,1)S(1)} %get-tuple-element.21.ul_ref.low_ref) | copy-start | bytes 3145732
  84.5 1.4 collective-permute-start.7
  87.6 1.4 collective-permute-start.8
  90.7 2.7 %collective-permute-start.10 = (f32[2,64,512]{2,1,0:T(8,128)}, f32[2,64,512]{2,1,0:T(8,128)}, u32[]{:S(2)}, u32[]{:S(2)}) collective-permute-start(f32[2,64,512]{2,1,0:T(8,128)} %step.13.own_ref), channel_id=1, source_target_pairs={{4,8},{12,16},{20,24},{5,9},{13,17},{21,25},{6,10},{14,18},{22,26}... | collective-permute-start | bytes 786440 | tf_op jit(solution)/shard_map/ppermute | solution.py:216
  92.1 13.4 %collective-permute-start.9 = (f32[2,64,512]{2,1,0:T(8,128)}, f32[2,64,512]{2,1,0:T(8,128)S(1)}, u32[]{:S(2)}, u32[]{:S(2)}) collective-permute-start(f32[2,64,512]{2,1,0:T(8,128)} %step.13.own_ref), channel_id=1, source_target_pairs={{4,0},{12,8},{20,16},{28,24},{5,1},{13,9},{21,17},{29,25},{6,2},{1... | collective-permute-start | bytes 786440 | tf_op jit(solution)/shard_map/ppermute | solution.py:216
  93.4 12.8 %copy-start.1 = (bf16[512,1024]{1,0:T(8,128)(2,1)S(1)}, bf16[512,1024]{1,0:T(8,128)(2,1)}, u32[]{:S(2)}) copy-start(bf16[512,1024]{1,0:T(8,128)(2,1)} %copy-done) | copy-start | bytes 3145732
  93.4 1.3 copy-start.5
  94.7 1.2 copy-start.8
  95.9 0.9 copy-start.14
  105.5 0.7 copy-start.21
  106.2 1.0 copy-start.22
  107.8 1.4 collective-permute-start.11
  110.8 1.4 collective-permute-start.12
  113.9 36.7 %collective-permute-start.13 = (f32[2,64,512]{2,1,0:T(8,128)}, f32[2,64,512]{2,1,0:T(8,128)}, u32[]{:S(2)}, u32[]{:S(2)}) collective-permute-start(f32[2,64,512]{2,1,0:T(8,128)} %step.17.old_ref), channel_id=1, source_target_pairs={{8,0},{9,1},{10,2},{11,3}} | collective-permute-start | bytes 786440 | tf_op jit(solution)/shard_map/ppermute | solution.py:216
  152.2 5.1 %collective-permute-start.14 = (f32[2,64,512]{2,1,0:T(8,128)S(1)}, f32[2,64,512]{2,1,0:T(8,128)S(1)}, u32[]{:S(2)}, u32[]{:S(2)}) collective-permute-start(f32[2,64,512]{2,1,0:T(8,128)S(1)} %step.18.old_ref), channel_id=1, source_target_pairs={{8,4},{16,12},{24,20},{9,5},{17,13},{25,21},{10,6},{18,14},{26,22}... | collective-permute-start | bytes 786440 | tf_op jit(solution)/shard_map/ppermute | solution.py:216
  152.9 2.8 %copy-start.12 = (f32[1,1,2,768,1024]{4,3,2,1,0:T(8,128)S(1)}, f32[1,1,2,768,1024]{4,3,2,1,0:T(8,128)}, u32[]{:S(2)}) copy-start(f32[1,1,2,768,1024]{4,3,2,1,0:T(8,128)} %param.18) | copy-start | bytes 18874372
  155.7 1.7 copy-start.2
  160.5 13.1 %collective-permute-start.16 = (f32[2,64,128]{2,1,0:T(8,128)}, f32[2,64,128]{2,1,0:T(8,128)S(1)}, u32[]{:S(2)}, u32[]{:S(2)}) collective-permute-start(f32[2,64,128]{2,1,0:T(8,128)} %get-tuple-element.38), channel_id=1, source_target_pairs={{1,0},{2,1},{3,2},{5,4},{6,5},{7,6},{9,8},{10,9},{11,10},{13,12},{... | collective-permute-start | bytes 196616 | tf_op jit(solution)/shard_map/ppermute | solution.py:264
  164.8 8.8 %collective-permute-start.15 = (f32[2,64,128]{2,1,0:T(8,128)}, f32[2,64,128]{2,1,0:T(8,128)S(1)}, u32[]{:S(2)}, u32[]{:S(2)}) collective-permute-start(f32[2,64,128]{2,1,0:T(8,128)} %get-tuple-element.39), channel_id=1, source_target_pairs={{0,1},{1,2},{2,3},{4,5},{5,6},{6,7},{8,9},{9,10},{10,11},{12,13},{... | collective-permute-start | bytes 196616 | tf_op jit(solution)/shard_map/ppermute | solution.py:263
  169.3 1.6 copy-start.29
  169.3 1.7 copy-start.19
  171.0 1.6 copy-start.11
  172.6 1.0 copy-start.16
  172.6 1.2 copy-start.17
  172.6 1.4 copy-start.18
  172.6 1.5 copy-start.20
  172.6 1.5 copy-start.24

commit v2 on v0

v2 whole, which is shorter than its diff:
```python
import jax
import jax.numpy as jnp
from jax import lax
from jax.experimental import pallas as pl
from jax.experimental.pallas import tpu as pltpu
from jax.sharding import PartitionSpec as P

MBLK = 8
VMEM = pl.BlockSpec(memory_space=pltpu.VMEM)
SMEM = pl.BlockSpec(memory_space=pltpu.SMEM)
ANY = pl.BlockSpec(memory_space=pl.ANY)
PARAMS = pltpu.CompilerParams(vmem_limit_bytes=16 * 1024 * 1024)


def floats(*shape):
    return jax.ShapeDtypeStruct(shape, jnp.float32)


def cost(flops):
    return pl.CostEstimate(flops=flops, bytes_accessed=flops // 1000, transcendentals=0)


def split(value):
    high = value.astype(jnp.bfloat16)
    low = (value - high.astype(jnp.float32)).astype(jnp.bfloat16)
    return high, low


def product(vector, high, low):
    m, n = vector.shape[1], high.shape[1] // 2
    top, rest = split(vector.reshape(2 * m, -1))
    wide = jnp.dot(top, high, preferred_element_type=jnp.float32)
    wide += jnp.dot(rest, high, preferred_element_type=jnp.float32)
    wide += jnp.dot(top, low, preferred_element_type=jnp.float32)
    return wide[:m, :n] - wide[m:, n:], wide[:m, n:] + wide[m:, :n]


def call(kernel, name, ins, outs, out_specs, after, flops=0, **keywords):
    specs, values = zip(*ins)
    count = len(values)

    def run(*refs):
        kernel(*refs[:count], *refs[count + len(after) :])

    return pl.pallas_call(
        run,
        in_specs=list(specs) + [ANY] * len(after),
        out_specs=out_specs,
        out_shape=outs,
        compiler_params=PARAMS,
        cost_estimate=cost(flops) if flops else None,
        name=name,
        **keywords,
    )(*values, *after)


def halves_kernel(panel_ref, high_ref, low_ref):
    n = panel_ref.shape[-1]
    for part in range(2):
        high, low = split(panel_ref[part])
        high_ref[:, part * n : (part + 1) * n] = high
        low_ref[:, part * n : (part + 1) * n] = low


def halves(panel, after, rows=128):
    _, k, n = panel.shape
    block = pl.BlockSpec((rows, 2 * n), lambda i: (i, 0))
    return call(
        halves_kernel,
        "halves",
        [(pl.BlockSpec((2, rows, n), lambda i: (0, i, 0)), panel)],
        [jax.ShapeDtypeStruct((k, 2 * n), jnp.bfloat16)] * 2,
        [block, block],
        after,
        2 * 10**9,
        grid=(k // rows,),
    )


def hold_kernel(panel_ref, out_ref):
    out_ref[...] = panel_ref[...]


def hold(panel, after, rows=128):
    _, k, n = panel.shape
    block = pl.BlockSpec((2, rows, n), lambda i: (0, i, 0))
    return call(
        hold_kernel, "hold", [(block, panel)], floats(2, k, n), block, after, grid=(k // rows,)
    )


def collect_kernel(me_ref, slab_ref, pos_ref, blocks_ref, *outs, sets):
    width = blocks_ref.shape[-1]
    me = me_ref[0]
    for out in outs:
        out[...] = jnp.zeros_like(out)

    def place(row, carry):
        slab = slab_ref[row]
        apart = lax.bitwise_xor(slab, me)
        side = lax.rem(apart, 2)
        lanes = pl.ds(pl.multiple_of(pos_ref[row] * width, width), width)
        for number, (size, which) in enumerate(sets):
            turn = lax.rem(lax.div(apart, 2), 2) if size == 4 else 0
            for other in range(2):

                @pl.when((lax.div(slab, size) == which) & (side == other))
                def _():
                    for part in range(2):
                        outs[2 * number + other][turn, part, :, lanes] += blocks_ref[row, part]

        return carry

    lax.fori_loop(0, blocks_ref.shape[0], place, 0)


def collect(me, slab, pos, blocks, sets, trace, after):
    shots = blocks.shape[2]
    shapes = [floats(size // 2, 2, shots, trace) for size, _ in sets for _ in range(2)]
    outs = call(
        lambda *refs: collect_kernel(*refs, sets=sets),
        "collect",
        [(SMEM, me), (SMEM, slab), (SMEM, pos), (VMEM, blocks)],
        shapes,
        [VMEM] * len(shapes),
        after,
        2 * 10**9,
    )
    return [outs[2 * i : 2 * i + 2] for i in range(len(sets))]


def ready_kernel(ids_ref, owner_ref, slot_ref, wavelet_ref, weights_ref, rows_ref):
    def pick(row, carry):
        weights_ref[pl.ds(row, 1), :] = wavelet_ref[pl.ds(ids_ref[row], 1), :]
        return carry

    lax.fori_loop(0, weights_ref.shape[0], pick, 0)

    def target(row, carry):
        rows_ref[row] = owner_ref[row] * MBLK + slot_ref[row]
        return carry

    lax.fori_loop(0, rows_ref.shape[0], target, 0)


def ready(ids, owner, slot, wavelet, after):
    return call(
        ready_kernel,
        "ready",
        [(SMEM, ids), (SMEM, owner), (SMEM, slot), (VMEM, wavelet)],
        [floats(*wavelet.shape), jax.ShapeDtypeStruct(slot.shape, jnp.int32)],
        [VMEM, SMEM],
        after,
    )


def join_kernel(mine_ref, arrived_ref, *refs, count):
    outs = refs[len(refs) - count :]
    last = mine_ref.shape[0] - 1
    outs[0][...] = mine_ref[0] + arrived_ref[0]
    outs[1][...] = mine_ref[last] + arrived_ref[last]
    if count == 3:
        outs[2][...] = refs[0][...]


def join(mine, arrived, following, after):
    count = 2 + len(following)
    return call(
        lambda *refs: join_kernel(*refs, count=count),
        "join",
        [(VMEM, value) for value in (mine, arrived, *following)],
        [floats(*mine.shape[1:])] * 2 + [floats(*value.shape) for value in following],
        [VMEM] * count,
        after,
    )


def add_kernel(one_ref, two_ref, out_ref):
    out_ref[...] = one_ref[...] + two_ref[...]


def add(one, two, after):
    return call(add_kernel, "add", [(VMEM, one), (VMEM, two)], floats(*one.shape), VMEM, after)


def source_kernel(one_ref, two_ref, weights_ref, out_ref):
    weight_re, weight_im = weights_ref[:, 0:1], weights_ref[:, 1:2]
    real, imag = one_ref[0] + two_ref[0], one_ref[1] + two_ref[1]
    out_ref[0] = weight_re * real - weight_im * imag
    out_ref[1] = weight_re * imag + weight_im * real


def source(one, two, weights, after):
    return call(
        source_kernel,
        "source",
        [(VMEM, one), (VMEM, two), (VMEM, weights)],
        floats(*one.shape),
        VMEM,
        after,
    )


def cleave_kernel(field_ref, *outs):
    rows = outs[0].shape[1]
    for number, out in enumerate(outs):
        out[...] = field_ref[:, number * rows : (number + 1) * rows]


def cleave(field, streams, after):
    parts, shots, trace = field.shape
    return call(
        cleave_kernel,
        "cleave",
        [(VMEM, field)],
        [floats(parts, shots // streams, trace)] * streams,
        [VMEM] * streams,
        after,
    )


def down_kernel(me_ref, arrived_ref, high_ref, low_ref, own_ref, old_ref, out_ref, *, at, cut):
    @pl.when(me_ref[0] == at)
    def _():
        real, imag = product(arrived_ref[...], high_ref[...], low_ref[...])
        out_ref[0] = real + own_ref[0, cut]
        out_ref[1] = imag + own_ref[1, cut]

    @pl.when(me_ref[0] != at)
    def _():
        out_ref[...] = old_ref[...]


def down_step(me, at, arrived, panel, own, first, old, after):
    cut = slice(first, first + old.shape[1])
    return call(
        lambda *refs: down_kernel(*refs, at=at, cut=cut),
        "down",
        [(SMEM, me)] + [(VMEM, value) for value in (arrived, *panel, own, old)],
        floats(*old.shape),
        VMEM,
        after,
    )


def up_kernel(me_ref, arrived_ref, oh, ol, beside_ref, eh, el, own_ref, old_ref, out_ref, *, at, top):
    @pl.when(me_ref[0] == at)
    def _():
        if top:
            out_ref[...] = beside_ref[...]
        else:
            real, imag = product(arrived_ref[...], oh[...], ol[...])
            out_ref[0] = real + beside_ref[0]
            out_ref[1] = imag + beside_ref[1]
        real, imag = product(out_ref[...], eh[...], el[...])
        out_ref[0] = real + own_ref[0]
        out_ref[1] = imag + own_ref[1]

    @pl.when(me_ref[0] != at)
    def _():
        out_ref[...] = old_ref[...]


def up_step(me, at, arrived, odd, beside, even, own, old, top, after):
    return call(
        lambda *refs: up_kernel(*refs, at=at, top=top),
        "up",
        [(SMEM, me)] + [(VMEM, value) for value in (arrived, *odd, beside, *even, own, old)],
        floats(*own.shape),
        VMEM,
        after,
    )


def finish_kernel(me_ref, *refs, streams, width):
    arrived, owns, olds = (refs[i * streams : (i + 1) * streams] for i in range(3))
    high_ref, low_ref, out_ref, head_ref, tail_ref = refs[3 * streams :]
    trace = out_ref.shape[-1]

    @pl.when(lax.rem(me_ref[0], 2) == 1)
    def _():
        field = jnp.concatenate([ref[...] for ref in arrived], axis=1)
        real, imag = product(field, high_ref[...], low_ref[...])
        out_ref[0] = real + jnp.concatenate([ref[0] for ref in owns], axis=0)
        out_ref[1] = imag + jnp.concatenate([ref[1] for ref in owns], axis=0)

    @pl.when(lax.rem(me_ref[0], 2) == 0)
    def _():
        out_ref[...] = jnp.concatenate([ref[...] for ref in olds], axis=1)

    head_ref[...] = out_ref[:, :, :width]
    tail_ref[...] = out_ref[:, :, trace - width :]


def finish(me, arrived, panel, own, old, width, after):
    streams = len(own)
    _, rows, trace = own[0].shape
    shots = rows * streams
    return call(
        lambda *refs: finish_kernel(*refs, streams=streams, width=width),
        "finish",
        [(SMEM, me)] + [(VMEM, value) for value in (*arrived, *own, *old, *panel)],
        [floats(2, shots, trace), floats(2, shots, width), floats(2, shots, width)],
        [VMEM] * 3,
        after,
    )


def middle_kernel(field_ref, high_ref, low_ref, forward_ref, out_ref, *, width):
    inner = slice(width, width + field_ref.shape[-1])
    real, imag = product(field_ref[...], high_ref[inner], low_ref[inner])
    total = forward_ref[0] * real + forward_ref[1] * imag
    out_ref[...] = jnp.sum(total, axis=0, keepdims=True)


def middle(field, maps, forward, width):
    return call(
        lambda *refs: middle_kernel(*refs, width=width),
        "middle",
        [(VMEM, value) for value in (field, *maps, forward)],
        floats(1, forward.shape[-1]),
        VMEM,
        (),
        4 * 10**9,
    )


def rim_kernel(rows_ref, part_ref, left_ref, right_ref, high_ref, low_ref, forward_ref, out_ref):
    shots, width = left_ref.shape[1], left_ref.shape[2]
    depth = high_ref.shape[0]

    def ends(ref):
        return jnp.concatenate([ref[:width], ref[depth - width :]], axis=0)

    field = jnp.concatenate([left_ref[...], right_ref[...]], axis=-1)
    real, imag = product(field, ends(high_ref), ends(low_ref))
    total = forward_ref[0] * real + forward_ref[1] * imag
    gradient = part_ref[...] + jnp.sum(total, axis=0, keepdims=True)
    gradient = gradient * shots ** (-0.5)
    out_ref[...] = jnp.zeros_like(out_ref)
    for block in range(gradient.shape[1] // width):
        row = rows_ref[block]
        out_ref[pl.ds(row, 1), :] += gradient[:, block * width : (block + 1) * width]


def rim(rows, part, left, right, maps, forward, slabs):
    return call(
        rim_kernel,
        "rim",
        [(SMEM, rows)] + [(VMEM, value) for value in (part, left, right, *maps, forward)],
        floats(slabs * MBLK, left.shape[2]),
        VMEM,
        (),
    )


def body(
    residual_blocks,
    residual_slab,
    residual_pos,
    shot_ids,
    wavelet,
    down_panel,
    up_panel,
    recovery,
    forward_field,
    element_owner,
    element_slot,
):
    slabs = lax.axis_size("slab")
    lats = lax.axis_size("lat")
    groups = slabs // 2
    shots, width = residual_blocks.shape[2:]
    trace = down_panel.shape[-1]
    streams = 2 if shots % 32 == 0 else 1
    lanes = range(streams)
    rows = shots // streams
    me = lax.axis_index("slab").astype(jnp.int32).reshape(1)
    quads = slabs // 4
    sets = [(2, 0), (2, 1)] + [(4, quad) for quad in range(1, quads)]
    hops = quads.bit_length() - 1
    swapping = [(s, s ^ 1) for s in range(slabs)]

    def hop(value, route):
        return lax.ppermute(value, "slab", route)

    def toward(number, turn):
        size, which = sets[number]
        if size == 4 and turn == 0:
            return [(s, s ^ 2) for s in range(slabs)]
        bit = 1 << (turn if size == 2 else turn - 1)
        return [
            (s, s ^ (size * bit)) for s in range(slabs) if ((s // size) ^ which) & (2 * bit - 1) == bit
        ]

    def gather(which, after):
        return collect(
            me, residual_slab[:, 0], residual_pos, residual_blocks, which, trace, after
        )

    parts = gather(sets[:1], [])
    swapped = [hop(parts[0][1], swapping)]
    weights, targets = ready(shot_ids, element_owner[:, 0], element_slot, wavelet, [parts[0][0]])
    down = halves(down_panel[0, 0], [weights])
    parts += gather(sets[1:], [down[0]])
    total, sent, base = {}, {}, {}

    def stage_join(number, token):
        following = [part[1] for part in parts[number + 1 : number + 2]]
        keep, joined, *gate = join(parts[number][0], swapped[number], following, token)
        total[number] = keep
        sent[number] = hop(joined, toward(number, 0))
        swapped.extend(hop(value, swapping) for value in gate)
        return [keep]

    def stage_add(number, turn, token):
        total[number] = add(total[number], sent[number], token)
        sent[number] = hop(total[number], toward(number, turn))
        return [total[number]]

    def stage_source(number, token):
        base[number] = source(total[number], sent[number], weights, token)
        return [base[number]]

    token = stage_join(0, [parts[1][0]])
    for turn in range(1, hops + 1):
        token = stage_add(0, turn, token)
    token = stage_join(1, token)
    up = halves(up_panel[0, 0], token)
    maps = halves(recovery[0, 0], [up[0]])
    token = stage_add(1, 1, [maps[0]])
    token = stage_source(0, token)
    state = list(cleave(base[0], streams, token))
    token = [state[0]]
    beside_panel = None
    for s in range(1, slabs):
        arrived = [hop(state[t], [(s - 1, s)]) for t in lanes]
        number = s // 2 if s < 4 else s // 4 + 1
        for t in lanes:
            state[t] = down_step(
                me, s, arrived[t], down, base[number], t * rows, state[t], token
            )
            token = [state[t]]
        if s == 1:
            for turn in range(2, hops + 1):
                token = stage_add(1, turn, token)
            token = stage_source(1, token)
        number = s // 4 + 2
        if number < len(sets):
            if s % 4 == 1:
                token = stage_join(number, token)
            if s % 4 == 2:
                for turn in range(1, hops + 1):
                    token = stage_add(number, turn, token)
            if s % 4 == 3:
                token = stage_source(number, token)
        if s == 1:
            held = hold(up_panel[0, 0], token)
            token = [held]
            beside_panel = hop(held, [(p + 1, p) for p in range(0, slabs - 2, 2)])
    beside = [hop(state[t], [(p + 1, p) for p in range(0, slabs, 2)]) for t in lanes]
    odd_up = halves(beside_panel, token)
    token = [odd_up[0]]
    above = list(state)
    for t in lanes:
        above[t] = up_step(
            me, slabs - 2, state[t], odd_up, beside[t], up, state[t], above[t], True, token
        )
        token = [above[t]]
    for p in range(slabs - 4, -1, -2):
        arrived = [hop(above[t], [(p + 2, p)]) for t in lanes]
        if p == 0:
            after = [hop(above[t], [(q + 2, q + 1) for q in range(0, slabs - 2, 2)]) for t in lanes]
        for t in lanes:
            above[t] = up_step(
                me, p, arrived[t], odd_up, beside[t], up, state[t], above[t], False, token
            )
            token = [above[t]]
    ups, head, tail = finish(me, after, up, state, above, width, token)

    left = lax.ppermute(tail, "lat", [(i, i + 1) for i in range(lats - 1)])
    right = lax.ppermute(head, "lat", [(i + 1, i) for i in range(lats - 1)])
    part = middle(ups, maps, forward_field[0, 0], width)
    outgoing = rim(targets, part, left, right, maps, forward_field[0, 0], slabs)
    arrived = lax.all_to_all(outgoing, "slab", split_axis=0, concat_axis=0, tiled=True)
    model = jnp.sum(arrived.reshape(slabs, MBLK, width), axis=0)
    return (ups[None, None], model[None, None])


def solution(mesh):
    placed = (
        P(("slab", "lat"), None, None, None),
        P(("slab", "lat"), None),
        P(("slab", "lat")),
        P(),
        P(),
        P("slab", "lat", None, None, None),
        P("slab", "lat", None, None, None),
        P("slab", "lat", None, None, None),
        P("slab", "lat", None, None, None),
        P(("slab", "lat"), None),
        P(("slab", "lat")),
    )
    return jax.shard_map(
        body,
        mesh=mesh,
        in_specs=placed,
        out_specs=(P("slab", "lat", None, None, None), P("slab", "lat", None, None)),
        check_vma=False,
    )
```

time: 347 us -> 144 us (0.41)
  matrix products: 88 us -> 0 us
  waiting for transfers between devices: 144 us -> 64.2 us
  starting transfers between devices: 94.5 us -> 47 us
  Pallas kernels: 0 us -> 15.6 us
  blocking collectives: 0 us -> 9.81 us
  local copies, waits for them, and re-layouts: 10.8 us -> 4.99 us
  other arithmetic: 6.31 us -> 0.6 us
    dot_general x71 -> x0, matrix products: 88 us -> none  [the longest x17 25.8 us: complex_product(): jnp.matmul(value_im, panel_re, precision=lax.Precision.HIGHEST)]
    all_to_all x4 -> x0, waiting for transfers between devices: 49.7 us -> none  [the longest x2 49.7 us: body(): lax.all_to_all(outgoing, 'slab', split_axis=0, concat_axis=0, tiled=True)]
    ppermute x18 -> x36, waiting for transfers between devices: 93.9 us -> 64.2 us  [the longest x34 62.5 us: hop(): return lax.ppermute(value, 'slab', route)]
    all_to_all x4 -> x0, starting transfers between devices: 24.1 us -> none  [the longest x2 11 us: body(): lax.all_to_all(outgoing, 'slab', split_axis=0, concat_axis=0, tiled=True)]
    ppermute x18 -> x36, starting transfers between devices: 70.4 us -> 47 us  [the longest x34 32.8 us: hop(): return lax.ppermute(value, 'slab', route)]
    pallas_call x0 -> x43, Pallas kernels: none -> 15.6 us  [call(): pl.pallas_call(run, in_specs=list(specs) + [ANY] * len(after), out_specs=...]
    all_to_all x0 -> x1, blocking collectives: none -> 9.81 us  [body(): lax.all_to_all(outgoing, 'slab', split_axis=0, concat_axis=0, tiled=True)]
    scatter x3 -> x0, local copies, waits for them, and re-layouts: 6.95 us -> none  [the longest x1 5.42 us: body(): outgoing = jnp.zeros((slab_count * capacity, 2, shots, width), jnp.float3...]
  transfers between devices with their start and end apart: 22 -> 36, of which waited for: 19 -> 14; matrix products, arithmetic and copies ran while one was open for 8% -> 0% of each run, Pallas kernels for 0% -> 8%
where the time goes in v2:
time: 144 us
  waiting for transfers between devices  64.2 us (45%)
  starting transfers between devices  47 us (33%)
  Pallas kernels  15.6 us (11%)
  blocking collectives  9.81 us (7%)
  local copies, waits for them, and re-layouts  4.99 us (3%)
  between operations  1.49 us (1%)
    ppermute x34, waiting for transfers between devices, hop(): return lax.ppermute(value, 'slab', route)  62.5 us
    ppermute x34, starting transfers between devices, hop(): return lax.ppermute(value, 'slab', route)  32.8 us
    pallas_call x43, Pallas kernels, call(): pl.pallas_call(run, in_specs=list(specs) + [ANY] * len(after), out_specs=...  15.6 us
    ppermute x1, starting transfers between devices, body(): left = lax.ppermute(tail, 'lat', [(i, i + 1) for i in range(lats - 1)])  12.2 us
    all_to_all x1, blocking collectives, body(): lax.all_to_all(outgoing, 'slab', split_axis=0, concat_axis=0, tiled=True)  9.81 us
    unnamed x33, local copies, waits for them, and re-layouts  4.99 us
  transfers between devices with their start and end apart: 36, of which 14 were waited for; matrix products, arithmetic and copies ran while one was open for 0% of the time, Pallas kernels for 8%

profile of v2, /device:TPU:1, one launch (start us, length us, event | category | flops | bytes accessed | tf_op | source)
XLA Modules:
  0.0 143.7 jit_solution(11631697808610209610)
XLA Ops:
  0.6 1.6 %copy-done.6 = f32[32,2,64,128]{3,2,1,0:T(8,128)S(1)} copy-done((f32[32,2,64,128]{3,2,1,0:T(8,128)S(1)}, f32[32,2,64,128]{3,2,1,0:T(8,128)}, u32[]{:S(2)}) %copy-start.6) | copy-done | bytes 2097176
  3.6 1.4 collect.2
  5.0 2.1 %collective-permute-start = (f32[1,2,64,512]{3,2,1,0:T(8,128)S(1)}, f32[1,2,64,512]{3,2,1,0:T(8,128)S(1)}, u32[]{:S(2)}, u32[]{:S(2)}) collective-permute-start(f32[1,2,64,512]{3,2,1,0:T(8,128)S(1)} %get-tuple-element.32), channel_id=1, source_target_pairs={{0,4},{4,0},{8,12},{12,8},{16,20},{20,16},{24,28},{28,24},{1,5},{5... | collective-permute-start | bytes 786440 | tf_op jit(solution)/shard_map/ppermute | solution.py:385
  7.2 1.6 %ready.1 = (f32[64,2]{1,0:T(8,128)S(1)}, s32[8]{0:T(128)S(1)}) custom-call(s32[64]{0:T(128)S(1)} %copy-done.2, s32[8]{0:T(128)S(1)} %bitcast.15, s32[8]{0:T(128)S(1)} %copy-done.4, f32[64,2]{1,0:T(8,128)S(1)} %copy.13.refs_3_, f32[1,2,64,512]{3,2,1,0:T(8,128)S(1)} %get-tuple-element.31.refs_4_.refs_0_), custom_call_target="tpu_custom_call" | custom-call | tf_op jit(solution)/shard_map/ready/pallas_call | solution.py:45
  9.4 1.0 copy-done.7
  10.5 2.1 %collect.3 = (f32[1,2,64,512]{3,2,1,0:T(8,128)S(1)}, f32[1,2,64,512]{3,2,1,0:T(8,128)S(1)}, f32[2,2,64,512]{3,2,1,0:T(8,128)S(1)}, f32[2,2,64,512]{3,2,1,0:T(8,128)S(1)}) custom-call(s32[1]{0:T(128)} %bitcast.refs_0_, s32[32]{0:T(128)S(1)} %bitcast.22, s32[32]{0:T(128)S(1)} %copy-done.12, f32[32,2,64,128]{3,2,1,0:T(8,128)S(1)} %copy-done.7, ...), custom_call_target="tpu_custom_call" | custom-call | flops 2000000000 | bytes 2000000 | tf_op jit(solution)/shard_map/collect/pallas_call | solution.py:45
  13.2 1.3 collective-permute-start.1
  14.5 1.2 collective-permute-start.3
  15.7 6.0 %collective-permute-done.1.refs_1_ = f32[2,64,512]{2,1,0:T(8,128)S(1)} collective-permute-done((f32[2,64,512]{2,1,0:T(8,128)S(1)}, f32[2,64,512]{2,1,0:T(8,128)S(1)}, u32[]{:S(2)}, u32[]{:S(2)}) %collective-permute-start.1) | collective-permute-done | bytes 262176 | tf_op jit(solution)/shard_map/ppermute | solution.py:385
  21.7 1.4 collective-permute-start.2
  23.2 1.7 %collective-permute-start.4 = (f32[2,64,512]{2,1,0:T(8,128)S(1)}, f32[2,64,512]{2,1,0:T(8,128)S(1)}, u32[]{:S(2)}, u32[]{:S(2)}) collective-permute-start(f32[2,64,512]{2,1,0:T(8,128)S(1)} %get-tuple-element.42), channel_id=1, source_target_pairs={{0,8},{4,12},{16,24},{20,28},{1,9},{5,13},{17,25},{21,29},{2,10},{... | collective-permute-start | bytes 786440 | tf_op jit(solution)/shard_map/ppermute | solution.py:385
  25.0 0.9 collective-permute-start.9
  26.4 1.6 %halves.6 = (bf16[768,2048]{1,0:T(8,128)(2,1)S(1)}, bf16[768,2048]{1,0:T(8,128)(2,1)S(1)}) custom-call(f32[2,768,1024]{2,1,0:T(8,128)S(1)} %bitcast.18, bf16[512,1024]{1,0:T(8,128)(2,1)S(1)} %get-tuple-element.43.refs_1_.refs_5_.refs_7_), custom_call_target="tpu_custom_call" | custom-call | flops 2000000000 | bytes 2000000 | tf_op jit(solution)/shard_map/halves/pallas_call | solution.py:45
  28.3 0.7 collective-permute-start.7
  29.0 1.3 collective-permute-done.2.refs_1_
  30.4 2.3 %collective-permute-start.5 = (f32[2,32,512]{2,1,0:T(8,128)S(1)}, f32[2,32,512]{2,1,0:T(8,128)S(1)}, u32[]{:S(2)}, u32[]{:S(2)}) collective-permute-start(f32[2,32,512]{2,1,0:T(8,128)S(1)} %get-tuple-element.45.refs_5_.refs_6_), channel_id=1, source_target_pairs={{0,4},{1,5},{2,6},{3,7}} | collective-permute-start | bytes 393224 | tf_op jit(solution)/shard_map/ppermute | solution.py:385
  32.7 1.3 collective-permute-start.8
  34.0 2.8 %collective-permute-done.5.refs_1_ = f32[2,32,512]{2,1,0:T(8,128)S(1)} collective-permute-done((f32[2,32,512]{2,1,0:T(8,128)S(1)}, f32[2,32,512]{2,1,0:T(8,128)S(1)}, u32[]{:S(2)}, u32[]{:S(2)}) %collective-permute-start.5) | collective-permute-done | bytes 131104 | tf_op jit(solution)/shard_map/ppermute | solution.py:385
  36.9 2.8 %collective-permute-done.8.refs_1_ = f32[2,32,512]{2,1,0:T(8,128)S(1)} collective-permute-done((f32[2,32,512]{2,1,0:T(8,128)S(1)}, f32[2,32,512]{2,1,0:T(8,128)S(1)}, u32[]{:S(2)}, u32[]{:S(2)}) %collective-permute-start.8) | collective-permute-done | bytes 131104 | tf_op jit(solution)/shard_map/ppermute | solution.py:385
  40.4 1.3 collective-permute-start.22
  43.9 3.1 %collective-permute-done.11.refs_1_ = f32[2,64,512]{2,1,0:T(8,128)S(1)} collective-permute-done((f32[2,64,512]{2,1,0:T(8,128)S(1)}, f32[2,64,512]{2,1,0:T(8,128)S(1)}, u32[]{:S(2)}, u32[]{:S(2)}) %collective-permute-start.11) | collective-permute-done | bytes 262176 | tf_op jit(solution)/shard_map/ppermute | solution.py:385
  47.0 1.3 collective-permute-start.14
  50.4 1.6 %collective-permute-done.14.refs_1_ = f32[2,64,512]{2,1,0:T(8,128)S(1)} collective-permute-done((f32[2,64,512]{2,1,0:T(8,128)S(1)}, f32[2,64,512]{2,1,0:T(8,128)S(1)}, u32[]{:S(2)}, u32[]{:S(2)}) %collective-permute-start.14) | collective-permute-done | bytes 262176 | tf_op jit(solution)/shard_map/ppermute | solution.py:385
  52.2 0.7 collective-permute-start.16
  52.9 0.7 collective-permute-start.19
  53.6 0.7 collective-permute-start.18
  54.3 0.7 collective-permute-start.21
  56.5 1.3 collective-permute-start.24
  57.8 1.3 collective-permute-start.26
  59.1 27.4 %collective-permute-done.22.refs_0_ = f32[2,512,512]{2,1,0:T(8,128)S(1)} collective-permute-done((f32[2,512,512]{2,1,0:T(8,128)S(1)}, f32[2,512,512]{2,1,0:T(8,128)S(1)}, u32[]{:S(2)}, u32[]{:S(2)}) %collective-permute-start.22) | collective-permute-done | bytes 2097184 | tf_op jit(solution)/shard_map/ppermute | solution.py:385
  87.1 2.3 %collective-permute-done.24.refs_4_ = f32[2,32,512]{2,1,0:T(8,128)S(1)} collective-permute-done((f32[2,32,512]{2,1,0:T(8,128)S(1)}, f32[2,32,512]{2,1,0:T(8,128)S(1)}, u32[]{:S(2)}, u32[]{:S(2)}) %collective-permute-start.24) | collective-permute-done | bytes 131104 | tf_op jit(solution)/shard_map/ppermute | solution.py:385
  89.3 0.7 collective-permute-start.25
  90.0 2.1 %collective-permute-done.26.refs_4_ = f32[2,32,512]{2,1,0:T(8,128)S(1)} collective-permute-done((f32[2,32,512]{2,1,0:T(8,128)S(1)}, f32[2,32,512]{2,1,0:T(8,128)S(1)}, u32[]{:S(2)}, u32[]{:S(2)}) %collective-permute-start.26) | collective-permute-done | bytes 131104 | tf_op jit(solution)/shard_map/ppermute | solution.py:385
  92.9 0.7 collective-permute-start.27
  94.5 1.3 collective-permute-start.32
  95.8 1.3 collective-permute-start.33
  98.5 10.9 %collective-permute-done.32.refs_1_ = f32[2,32,512]{2,1,0:T(8,128)S(1)} collective-permute-done((f32[2,32,512]{2,1,0:T(8,128)S(1)}, f32[2,32,512]{2,1,0:T(8,128)S(1)}, u32[]{:S(2)}, u32[]{:S(2)}) %collective-permute-start.32) | collective-permute-done | bytes 131104 | tf_op jit(solution)/shard_map/ppermute | solution.py:385
  109.4 1.3 up.14.refs_9_.refs_5_
  110.7 1.5 %collective-permute-done.33.refs_1_ = f32[2,32,512]{2,1,0:T(8,128)S(1)} collective-permute-done((f32[2,32,512]{2,1,0:T(8,128)S(1)}, f32[2,32,512]{2,1,0:T(8,128)S(1)}, u32[]{:S(2)}, u32[]{:S(2)}) %collective-permute-start.33) | collective-permute-done | bytes 131104 | tf_op jit(solution)/shard_map/ppermute | solution.py:385
  112.2 1.3 up.15.refs_6_.refs_9_
  113.5 0.7 finish.1
  114.3 12.2 %collective-permute-start.34 = (f32[2,64,128]{2,1,0:T(8,128)S(1)}, f32[2,64,128]{2,1,0:T(8,128)S(1)}, u32[]{:S(2)}, u32[]{:S(2)}) collective-permute-start(f32[2,64,128]{2,1,0:T(8,128)S(1)} %get-tuple-element.58), channel_id=1, source_target_pairs={{0,1},{1,2},{2,3},{4,5},{5,6},{6,7},{8,9},{9,10},{10,11},{12,13},{... | collective-permute-start | bytes 196616 | tf_op jit(solution)/shard_map/ppermute | solution.py:481
  126.5 1.9 %collective-permute-start.35 = (f32[2,64,128]{2,1,0:T(8,128)S(1)}, f32[2,64,128]{2,1,0:T(8,128)S(1)}, u32[]{:S(2)}, u32[]{:S(2)}) collective-permute-start(f32[2,64,128]{2,1,0:T(8,128)S(1)} %get-tuple-element.59), channel_id=1, source_target_pairs={{1,0},{2,1},{3,2},{5,4},{6,5},{7,6},{9,8},{10,9},{11,10},{13,12},{... | collective-permute-start | bytes 196616 | tf_op jit(solution)/shard_map/ppermute | solution.py:482
  128.5 0.9 copy-done.8
  129.4 1.0 middle.1.refs_1_
  130.4 1.7 %collective-permute-done.35.refs_3_ = f32[2,64,128]{2,1,0:T(8,128)S(1)} collective-permute-done((f32[2,64,128]{2,1,0:T(8,128)S(1)}, f32[2,64,128]{2,1,0:T(8,128)S(1)}, u32[]{:S(2)}, u32[]{:S(2)}) %collective-permute-start.35) | collective-permute-done | bytes 65568 | tf_op jit(solution)/shard_map/ppermute | solution.py:482
  132.1 1.2 rim.1
  133.3 9.8 %all_to_all.9 = f32[8,8,128]{2,1,0:T(8,128)S(1)} all-to-all(f32[8,8,128]{2,1,0:T(8,128)S(1)} %bitcast.14), channel_id=1, replica_groups=mesh['slab'=8,'lat'=4] {'slab'}, dimensions={0} | all-to-all | bytes 65536 | tf_op jit(solution)/shard_map/all_to_all | solution.py:485
  (103 shorter events, 14.3 us)
Async XLA Ops:
  0.6 1.6 %copy-start.6 = (f32[32,2,64,128]{3,2,1,0:T(8,128)S(1)}, f32[32,2,64,128]{3,2,1,0:T(8,128)}, u32[]{:S(2)}) copy-start(f32[32,2,64,128]{3,2,1,0:T(8,128)} %refs_3_.4) | copy-start | bytes 6291460
  3.5 3.6 %copy-start.13 = (f32[64,2]{0,1:T(2,128)S(1)}, f32[64,2]{0,1:T(2,128)}, u32[]{:S(2)}) copy-start(f32[64,2]{0,1:T(2,128)} %param.15) | copy-start | bytes 1540
  3.5 3.7 %copy-start.2 = (s32[64]{0:T(128)S(1)}, s32[64]{0:T(128)}, u32[]{:S(2)}) copy-start(s32[64]{0:T(128)} %refs_0_.1) | copy-start | bytes 772
  3.5 3.7 %copy-start.3 = (s32[8,1]{0,1:T(1,128)S(1)}, s32[8,1]{0,1:T(1,128)}, u32[]{:S(2)}) copy-start(s32[8,1]{0,1:T(1,128)} %param.20) | copy-start | bytes 100
  3.5 3.7 %copy-start.4 = (s32[8]{0:T(128)S(1)}, s32[8]{0:T(128)}, u32[]{:S(2)}) copy-start(s32[8]{0:T(128)} %refs_2_.4) | copy-start | bytes 100
  3.6 5.3 %copy-start.5 = (f32[1,1,2,512,512]{4,3,2,1,0:T(8,128)S(1)}, f32[1,1,2,512,512]{4,3,2,1,0:T(8,128)}, u32[]{:S(2)}) copy-start(f32[1,1,2,512,512]{4,3,2,1,0:T(8,128)} %param.16) | copy-start | bytes 6291460
  5.0 8.2 %collective-permute-start = (f32[1,2,64,512]{3,2,1,0:T(8,128)S(1)}, f32[1,2,64,512]{3,2,1,0:T(8,128)S(1)}, u32[]{:S(2)}, u32[]{:S(2)}) collective-permute-start(f32[1,2,64,512]{3,2,1,0:T(8,128)S(1)} %get-tuple-element.32), channel_id=1, source_target_pairs={{0,4},{4,0},{8,12},{12,8},{16,20},{20,16},{24,28},{28,24},{1,5},{5... | collective-permute-start | bytes 786440 | tf_op jit(solution)/shard_map/ppermute | solution.py:385
  8.9 1.6 %copy-start.7 = (f32[32,2,64,128]{3,2,1,0:T(8,128)S(1)}, f32[32,2,64,128]{3,2,1,0:T(8,128)}, u32[]{:S(2)}) copy-start(f32[32,2,64,128]{3,2,1,0:T(8,128)} %refs_3_.4) | copy-start | bytes 6291460
  8.9 1.6 %copy-start.10 = (s32[32,1]{0,1:T(1,128)S(1)}, s32[32,1]{0,1:T(1,128)}, u32[]{:S(2)}) copy-start(s32[32,1]{0,1:T(1,128)} %param.12) | copy-start | bytes 388
  10.5 15.9 %slice-start = ((s8[6291456]{0:T(1024)(128)(4,1)}), s8[4194304]{0:T(1024)(128)(4,1)S(1)}, s32[]{:S(2)}) async-start(s8[6291456]{0:T(1024)(128)(4,1)} %bitcast.16), calls=%async_computation.1 | async-start | bytes 8388608
  12.5 13.3 %copy-start = (f32[1,1,2,512,512]{4,3,2,1,0:T(8,128)S(1)}, f32[1,1,2,512,512]{4,3,2,1,0:T(8,128)}, u32[]{:S(2)}) copy-start(f32[1,1,2,512,512]{4,3,2,1,0:T(8,128)} %param.17) | copy-start | bytes 6291460
  13.2 8.5 %collective-permute-start.1 = (f32[2,64,512]{2,1,0:T(8,128)S(1)}, f32[2,64,512]{2,1,0:T(8,128)S(1)}, u32[]{:S(2)}, u32[]{:S(2)}) collective-permute-start(f32[2,64,512]{2,1,0:T(8,128)S(1)} %get-tuple-element.38), channel_id=1, source_target_pairs={{8,0},{12,4},{24,16},{28,20},{9,1},{13,5},{25,17},{29,21},{10,2},{... | collective-permute-start | bytes 786440 | tf_op jit(solution)/shard_map/ppermute | solution.py:385
  14.5 8.6 %collective-permute-start.3 = (f32[1,2,64,512]{3,2,1,0:T(8,128)S(1)}, f32[1,2,64,512]{3,2,1,0:T(8,128)S(1)}, u32[]{:S(2)}, u32[]{:S(2)}) collective-permute-start(f32[1,2,64,512]{3,2,1,0:T(8,128)S(1)} %get-tuple-element.39), channel_id=1, source_target_pairs={{0,4},{4,0},{8,12},{12,8},{16,20},{20,16},{24,28},{28,24},{1,5},{5... | collective-permute-start | bytes 786440 | tf_op jit(solution)/shard_map/ppermute | solution.py:385
  21.7 4.7 %slice-start.1 = ((s8[6291456]{0:T(1024)(128)(4,1)}), s8[2097152]{0:T(1024)(128)(4,1)S(1)}, s32[]{:S(2)}) async-start(s8[6291456]{0:T(1024)(128)(4,1)} %bitcast.16), calls=%async_computation.2 | async-start | bytes 4194304
  21.7 8.6 %collective-permute-start.2 = (f32[2,64,512]{2,1,0:T(8,128)S(1)}, f32[2,64,512]{2,1,0:T(8,128)S(1)}, u32[]{:S(2)}, u32[]{:S(2)}) collective-permute-start(f32[2,64,512]{2,1,0:T(8,128)S(1)} %add.3.refs_3_.refs_0_), channel_id=1, source_target_pairs={{16,0},{20,4},{17,1},{21,5},{18,2},{22,6},{19,3},{23,7}} | collective-permute-start | bytes 786440 | tf_op jit(solution)/shard_map/ppermute | solution.py:385
  23.2 5.0 %collective-permute-start.4 = (f32[2,64,512]{2,1,0:T(8,128)S(1)}, f32[2,64,512]{2,1,0:T(8,128)S(1)}, u32[]{:S(2)}, u32[]{:S(2)}) collective-permute-start(f32[2,64,512]{2,1,0:T(8,128)S(1)} %get-tuple-element.42), channel_id=1, source_target_pairs={{0,8},{4,12},{16,24},{20,28},{1,9},{5,13},{17,25},{21,29},{2,10},{... | collective-permute-start | bytes 786440 | tf_op jit(solution)/shard_map/ppermute | solution.py:385
  25.0 14.8 %collective-permute-start.9 = (f32[2,2,64,512]{3,2,1,0:T(8,128)S(1)}, f32[2,2,64,512]{3,2,1,0:T(8,128)S(1)}, u32[]{:S(2)}, u32[]{:S(2)}) collective-permute-start(f32[2,2,64,512]{3,2,1,0:T(8,128)S(1)} %get-tuple-element.49), channel_id=1, source_target_pairs={{0,4},{4,0},{8,12},{12,8},{16,20},{20,16},{24,28},{28,24},{1,5},{5... | collective-permute-start | bytes 1572872 | tf_op jit(solution)/shard_map/ppermute | solution.py:385
  28.3 11.4 %collective-permute-start.7 = (f32[2,64,512]{2,1,0:T(8,128)S(1)}, f32[2,64,512]{2,1,0:T(8,128)S(1)}, u32[]{:S(2)}, u32[]{:S(2)}) collective-permute-start(f32[2,64,512]{2,1,0:T(8,128)S(1)} %add.4.refs_3_.refs_0_), channel_id=1, source_target_pairs={{24,8},{28,12},{25,9},{29,13},{26,10},{30,14},{27,11},{31,15}} | collective-permute-start | bytes 786440 | tf_op jit(solution)/shard_map/ppermute | solution.py:385
  30.4 6.4 %collective-permute-start.5 = (f32[2,32,512]{2,1,0:T(8,128)S(1)}, f32[2,32,512]{2,1,0:T(8,128)S(1)}, u32[]{:S(2)}, u32[]{:S(2)}) collective-permute-start(f32[2,32,512]{2,1,0:T(8,128)S(1)} %get-tuple-element.45.refs_5_.refs_6_), channel_id=1, source_target_pairs={{0,4},{1,5},{2,6},{3,7}} | collective-permute-start | bytes 393224 | tf_op jit(solution)/shard_map/ppermute | solution.py:385
  32.7 6.9 %collective-permute-start.8 = (f32[2,32,512]{2,1,0:T(8,128)S(1)}, f32[2,32,512]{2,1,0:T(8,128)S(1)}, u32[]{:S(2)}, u32[]{:S(2)}) collective-permute-start(f32[2,32,512]{2,1,0:T(8,128)S(1)} %get-tuple-element.47.refs_5_), channel_id=1, source_target_pairs={{0,4},{1,5},{2,6},{3,7}} | collective-permute-start | bytes 393224 | tf_op jit(solution)/shard_map/ppermute | solution.py:385
  40.4 46.1 %collective-permute-start.22 = (f32[2,512,512]{2,1,0:T(8,128)S(1)}, f32[2,512,512]{2,1,0:T(8,128)S(1)}, u32[]{:S(2)}, u32[]{:S(2)}) collective-permute-start(f32[2,512,512]{2,1,0:T(8,128)S(1)} %hold.1.refs_6_), channel_id=1, source_target_pairs={{4,0},{12,8},{20,16},{5,1},{13,9},{21,17},{6,2},{14,10},{22,18},{7... | collective-permute-start | bytes 6291464 | tf_op jit(solution)/shard_map/ppermute | solution.py:385
  41.7 5.3 %collective-permute-start.11 = (f32[2,64,512]{2,1,0:T(8,128)S(1)}, f32[2,64,512]{2,1,0:T(8,128)S(1)}, u32[]{:S(2)}, u32[]{:S(2)}) collective-permute-start(f32[2,64,512]{2,1,0:T(8,128)S(1)} %get-tuple-element.51), channel_id=1, source_target_pairs={{0,8},{4,12},{8,0},{12,4},{16,24},{20,28},{24,16},{28,20},{1,9},{5... | collective-permute-start | bytes 786440 | tf_op jit(solution)/shard_map/ppermute | solution.py:385
  41.8 1.4 collective-permute-start.6
  42.4 1.4 collective-permute-start.12
  43.2 5.8 %collective-permute-start.10 = (f32[2,32,512]{2,1,0:T(8,128)S(1)}, f32[2,32,512]{2,1,0:T(8,128)S(1)}, u32[]{:S(2)}, u32[]{:S(2)}) collective-permute-start(f32[2,32,512]{2,1,0:T(8,128)S(1)} %down.16.refs_6_.refs_5_), channel_id=1, source_target_pairs={{8,12},{9,13},{10,14},{11,15}} | collective-permute-start | bytes 393224 | tf_op jit(solution)/shard_map/ppermute | solution.py:385
  47.0 5.0 %collective-permute-start.14 = (f32[2,64,512]{2,1,0:T(8,128)S(1)}, f32[2,64,512]{2,1,0:T(8,128)S(1)}, u32[]{:S(2)}, u32[]{:S(2)}) collective-permute-start(f32[2,64,512]{2,1,0:T(8,128)S(1)} %add.5.refs_6_.refs_0_), channel_id=1, source_target_pairs={{0,16},{4,20},{8,24},{12,28},{1,17},{5,21},{9,25},{13,29},{2,18},{... | collective-permute-start | bytes 786440 | tf_op jit(solution)/shard_map/ppermute | solution.py:385
  48.3 1.4 collective-permute-start.15
  49.0 3.1 %collective-permute-start.13 = (f32[2,32,512]{2,1,0:T(8,128)S(1)}, f32[2,32,512]{2,1,0:T(8,128)S(1)}, u32[]{:S(2)}, u32[]{:S(2)}) collective-permute-start(f32[2,32,512]{2,1,0:T(8,128)S(1)} %down.18.refs_6_.refs_5_), channel_id=1, source_target_pairs={{12,16},{13,17},{14,18},{15,19}} | collective-permute-start | bytes 393224 | tf_op jit(solution)/shard_map/ppermute | solution.py:385
  49.8 3.1 %collective-permute-start.17 = (f32[2,32,512]{2,1,0:T(8,128)S(1)}, f32[2,32,512]{2,1,0:T(8,128)S(1)}, u32[]{:S(2)}, u32[]{:S(2)}) collective-permute-start(f32[2,32,512]{2,1,0:T(8,128)S(1)} %down.19.refs_3_.refs_5_), channel_id=1, source_target_pairs={{12,16},{13,17},{14,18},{15,19}} | collective-permute-start | bytes 393224 | tf_op jit(solution)/shard_map/ppermute | solution.py:385
  52.2 1.4 collective-permute-start.16
  52.9 1.4 collective-permute-start.19
  53.6 1.4 collective-permute-start.18
  54.3 1.4 collective-permute-start.21
  55.0 1.4 collective-permute-start.20
  55.7 2.0 %collective-permute-start.23 = (f32[2,32,512]{2,1,0:T(8,128)S(1)}, f32[2,32,512]{2,1,0:T(8,128)S(1)}, u32[]{:S(2)}, u32[]{:S(2)}) collective-permute-start(f32[2,32,512]{2,1,0:T(8,128)S(1)} %down.25.refs_6_.refs_5_), channel_id=1, source_target_pairs={{24,28},{25,29},{26,30},{27,31}} | collective-permute-start | bytes 393224 | tf_op jit(solution)/shard_map/ppermute | solution.py:385
  56.5 32.9 %collective-permute-start.24 = (f32[2,32,512]{2,1,0:T(8,128)S(1)}, f32[2,32,512]{2,1,0:T(8,128)S(1)}, u32[]{:S(2)}, u32[]{:S(2)}) collective-permute-start(f32[2,32,512]{2,1,0:T(8,128)S(1)} %down.26.refs_6_.refs_1_.refs_7_.refs_8_.refs_3_), channel_id=1, source_target_pairs={{4,0},{12,8},{20,16},{28,24},{5,1},{13,9},{21,17},{29,25},{6,2},{1... | collective-permute-start | bytes 393224 | tf_op jit(solution)/shard_map/ppermute | solution.py:385
  57.8 34.3 %collective-permute-start.26 = (f32[2,32,512]{2,1,0:T(8,128)S(1)}, f32[2,32,512]{2,1,0:T(8,128)S(1)}, u32[]{:S(2)}, u32[]{:S(2)}) collective-permute-start(f32[2,32,512]{2,1,0:T(8,128)S(1)} %down.27.refs_1_.refs_7_.refs_8_.refs_4_), channel_id=1, source_target_pairs={{4,0},{12,8},{20,16},{28,24},{5,1},{13,9},{21,17},{29,25},{6,2},{1... | collective-permute-start | bytes 393224 | tf_op jit(solution)/shard_map/ppermute | solution.py:385
  89.3 3.5 %collective-permute-start.25 = (f32[2,32,512]{2,1,0:T(8,128)S(1)}, f32[2,32,512]{2,1,0:T(8,128)S(1)}, u32[]{:S(2)}, u32[]{:S(2)}) collective-permute-start(f32[2,32,512]{2,1,0:T(8,128)S(1)} %up.8.refs_9_.refs_8_), channel_id=1, source_target_pairs={{24,16},{25,17},{26,18},{27,19}} | collective-permute-start | bytes 393224 | tf_op jit(solution)/shard_map/ppermute | solution.py:385
  92.1 1.4 collective-permute-start.28
  92.9 1.6 %collective-permute-start.27 = (f32[2,32,512]{2,1,0:T(8,128)S(1)}, f32[2,32,512]{2,1,0:T(8,128)S(1)}, u32[]{:S(2)}, u32[]{:S(2)}) collective-permute-start(f32[2,32,512]{2,1,0:T(8,128)S(1)} %up.10.refs_9_.refs_8_), channel_id=1, source_target_pairs={{16,8},{17,9},{18,10},{19,11}} | collective-permute-start | bytes 393224 | tf_op jit(solution)/shard_map/ppermute | solution.py:385
  93.8 2.0 %collective-permute-start.30 = (f32[2,32,512]{2,1,0:T(8,128)S(1)}, f32[2,32,512]{2,1,0:T(8,128)S(1)}, u32[]{:S(2)}, u32[]{:S(2)}) collective-permute-start(f32[2,32,512]{2,1,0:T(8,128)S(1)} %up.11.refs_9_.refs_8_), channel_id=1, source_target_pairs={{16,8},{17,9},{18,10},{19,11}} | collective-permute-start | bytes 393224 | tf_op jit(solution)/shard_map/ppermute | solution.py:385
  94.5 14.9 %collective-permute-start.32 = (f32[2,32,512]{2,1,0:T(8,128)S(1)}, f32[2,32,512]{2,1,0:T(8,128)S(1)}, u32[]{:S(2)}, u32[]{:S(2)}) collective-permute-start(f32[2,32,512]{2,1,0:T(8,128)S(1)} %up.12.refs_9_.refs_8_), channel_id=1, source_target_pairs={{8,0},{9,1},{10,2},{11,3}} | collective-permute-start | bytes 393224 | tf_op jit(solution)/shard_map/ppermute | solution.py:385
  95.8 16.4 %collective-permute-start.33 = (f32[2,32,512]{2,1,0:T(8,128)S(1)}, f32[2,32,512]{2,1,0:T(8,128)S(1)}, u32[]{:S(2)}, u32[]{:S(2)}) collective-permute-start(f32[2,32,512]{2,1,0:T(8,128)S(1)} %up.13.refs_9_.refs_8_), channel_id=1, source_target_pairs={{8,0},{9,1},{10,2},{11,3}} | collective-permute-start | bytes 393224 | tf_op jit(solution)/shard_map/ppermute | solution.py:385
  97.1 16.4 %collective-permute-start.31 = (f32[2,32,512]{2,1,0:T(8,128)S(1)}, f32[2,32,512]{2,1,0:T(8,128)S(1)}, u32[]{:S(2)}, u32[]{:S(2)}) collective-permute-start(f32[2,32,512]{2,1,0:T(8,128)S(1)} %up.13.refs_9_.refs_8_), channel_id=1, source_target_pairs={{8,4},{16,12},{24,20},{9,5},{17,13},{25,21},{10,6},{18,14},{26,22}... | collective-permute-start | bytes 393224 | tf_op jit(solution)/shard_map/ppermute | solution.py:385
  97.8 15.7 %collective-permute-start.29 = (f32[2,32,512]{2,1,0:T(8,128)S(1)}, f32[2,32,512]{2,1,0:T(8,128)S(1)}, u32[]{:S(2)}, u32[]{:S(2)}) collective-permute-start(f32[2,32,512]{2,1,0:T(8,128)S(1)} %up.12.refs_9_.refs_8_), channel_id=1, source_target_pairs={{8,4},{16,12},{24,20},{9,5},{17,13},{25,21},{10,6},{18,14},{26,22}... | collective-permute-start | bytes 393224 | tf_op jit(solution)/shard_map/ppermute | solution.py:385
  113.5 14.9 %copy-start.1 = (f32[1,1,2,64,1024]{4,3,2,1,0:T(8,128)S(1)}, f32[1,1,2,64,1024]{4,3,2,1,0:T(8,128)}, u32[]{:S(2)}) copy-start(f32[1,1,2,64,1024]{4,3,2,1,0:T(8,128)} %param.19) | copy-start | bytes 1572868
  114.3 16.1 %collective-permute-start.34 = (f32[2,64,128]{2,1,0:T(8,128)S(1)}, f32[2,64,128]{2,1,0:T(8,128)S(1)}, u32[]{:S(2)}, u32[]{:S(2)}) collective-permute-start(f32[2,64,128]{2,1,0:T(8,128)S(1)} %get-tuple-element.58), channel_id=1, source_target_pairs={{0,1},{1,2},{2,3},{4,5},{5,6},{6,7},{8,9},{9,10},{10,11},{12,13},{... | collective-permute-start | bytes 196616 | tf_op jit(solution)/shard_map/ppermute | solution.py:481
  126.5 5.6 %collective-permute-start.35 = (f32[2,64,128]{2,1,0:T(8,128)S(1)}, f32[2,64,128]{2,1,0:T(8,128)S(1)}, u32[]{:S(2)}, u32[]{:S(2)}) collective-permute-start(f32[2,64,128]{2,1,0:T(8,128)S(1)} %get-tuple-element.59), channel_id=1, source_target_pairs={{1,0},{2,1},{3,2},{5,4},{6,5},{7,6},{9,8},{10,9},{11,10},{13,12},{... | collective-permute-start | bytes 196616 | tf_op jit(solution)/shard_map/ppermute | solution.py:482
  (4 other events, 3.8 us)

commit v3 on v2

--- a/solution.py
+++ b/solution.py
@@ -9,7 +9,8 @@
 VMEM = pl.BlockSpec(memory_space=pltpu.VMEM)
 SMEM = pl.BlockSpec(memory_space=pltpu.SMEM)
 ANY = pl.BlockSpec(memory_space=pl.ANY)
-PARAMS = pltpu.CompilerParams(vmem_limit_bytes=16 * 1024 * 1024)
+HBM = pl.BlockSpec(memory_space=pltpu.HBM)
+CHUNKS = 4
 
 
 def floats(*shape):
@@ -35,7 +36,7 @@
     return wide[:m, :n] - wide[m:, n:], wide[:m, n:] + wide[m:, :n]
 
 
-def call(kernel, name, ins, outs, out_specs, after, flops=0, **keywords):
+def call(kernel, name, ins, outs, out_specs, after, flops=0, room=16, **keywords):
     specs, values = zip(*ins)
     count = len(values)
 
@@ -47,7 +48,7 @@
         in_specs=list(specs) + [ANY] * len(after),
         out_specs=out_specs,
         out_shape=outs,
-        compiler_params=PARAMS,
+        compiler_params=pltpu.CompilerParams(vmem_limit_bytes=room * 1024 * 1024),
         cost_estimate=cost(flops) if flops else None,
         name=name,
         **keywords,
@@ -77,23 +78,78 @@
     )
 
 
-def hold_kernel(panel_ref, out_ref):
-    out_ref[...] = panel_ref[...]
-
-
-def hold(panel, after, rows=128):
-    _, k, n = panel.shape
-    block = pl.BlockSpec((2, rows, n), lambda i: (0, i, 0))
-    return call(
-        hold_kernel, "hold", [(block, panel)], floats(2, k, n), block, after, grid=(k // rows,)
-    )
-
-
-def collect_kernel(me_ref, slab_ref, pos_ref, blocks_ref, *outs, sets):
-    width = blocks_ref.shape[-1]
+def pair_kernel(me_ref, one_ref, two_ref, eh, el, high_ref, low_ref, *, top):
+    k, n = one_ref.shape[1:]
+    rows = 128
+    place = lax.rem(me_ref[0], 4)
+
+    def run(panel_ref):
+        def chunk(i, carry):
+            some = pl.ds(pl.multiple_of(i * rows, rows), rows)
+            for part, value in enumerate(product(panel_ref[:, some], eh[...], el[...])):
+                high, low = split(value)
+                high_ref[some, part * n : (part + 1) * n] = high
+                low_ref[some, part * n : (part + 1) * n] = low
+            return carry
+
+        lax.fori_loop(0, k // rows, chunk, 0)
+
+    @pl.when((place == 0) & (me_ref[0] < top))
+    def _():
+        run(one_ref)
+
+    @pl.when((place == 2) & (me_ref[0] < top))
+    def _():
+        run(two_ref)
+
+
+def pair_panel(me, one, two, even, after, top):
+    shape = jax.ShapeDtypeStruct(even[0].shape, jnp.bfloat16)
+    return call(
+        lambda *refs: pair_kernel(*refs, top=top),
+        "pair",
+        [(SMEM, me)] + [(VMEM, value) for value in (one, two, *even)],
+        [shape, shape],
+        [VMEM] * 2,
+        after,
+    )
+
+
+def hold_kernel(me_ref, panel_ref, out_ref, *, place):
+    @pl.when(lax.rem(me_ref[0], 4) == place)
+    def _():
+        out_ref[...] = panel_ref[...]
+
+
+def hold(me, place, panel, after):
+    return call(
+        lambda *refs: hold_kernel(*refs, place=place),
+        "hold",
+        [(SMEM, me), (VMEM, panel)],
+        floats(*panel.shape),
+        VMEM,
+        after,
+    )
+
+
+def collect_kernel(me_ref, slab_hbm, pos_hbm, blocks_hbm, *refs, sets):
+    outs, (slab_ref, pos_ref, blocks_ref, sems) = refs[:-4], refs[-4:]
+    count, width = blocks_ref.shape[0], blocks_ref.shape[-1]
+    chunk = count // CHUNKS
     me = me_ref[0]
+    copies = [
+        pltpu.make_async_copy(slab_hbm, slab_ref, sems.at[CHUNKS]),
+        pltpu.make_async_copy(pos_hbm, pos_ref, sems.at[CHUNKS + 1]),
+    ]
+    for i in range(CHUNKS):
+        some = pl.ds(i * chunk, chunk)
+        copies.append(pltpu.make_async_copy(blocks_hbm.at[some], blocks_ref.at[some], sems.at[i]))
+    for copy in copies:
+        copy.start()
     for out in outs:
         out[...] = jnp.zeros_like(out)
+    copies[0].wait()
+    copies[1].wait()
 
     def place(row, carry):
         slab = slab_ref[row]
@@ -111,7 +167,9 @@
 
         return carry
 
-    lax.fori_loop(0, blocks_ref.shape[0], place, 0)
+    for i in range(CHUNKS):
+        copies[2 + i].wait()
+        lax.fori_loop(i * chunk, (i + 1) * chunk, place, 0)
 
 
 def collect(me, slab, pos, blocks, sets, trace, after):
@@ -120,11 +178,18 @@
     outs = call(
         lambda *refs: collect_kernel(*refs, sets=sets),
         "collect",
-        [(SMEM, me), (SMEM, slab), (SMEM, pos), (VMEM, blocks)],
+        [(SMEM, me), (HBM, slab), (HBM, pos), (HBM, blocks)],
         shapes,
         [VMEM] * len(shapes),
         after,
         2 * 10**9,
+        59 if not after else 16,
+        scratch_shapes=[
+            pltpu.SMEM(slab.shape, jnp.int32),
+            pltpu.SMEM(pos.shape, jnp.int32),
+            pltpu.VMEM(blocks.shape, jnp.float32),
+            pltpu.SemaphoreType.DMA((CHUNKS + 2,)),
+        ],
     )
     return [outs[2 * i : 2 * i + 2] for i in range(len(sets))]
 
@@ -175,6 +240,23 @@
     )
 
 
+def gate_kernel(*refs):
+    count = len(refs) // 2
+    for value, out in zip(refs[:count], refs[count:]):
+        out[...] = value[...]
+
+
+def gate(values, after):
+    return call(
+        gate_kernel,
+        "gate",
+        [(VMEM, value) for value in values],
+        [floats(*value.shape) for value in values],
+        [VMEM] * len(values),
+        after,
+    )
+
+
 def add_kernel(one_ref, two_ref, out_ref):
     out_ref[...] = one_ref[...] + two_ref[...]
 
@@ -219,54 +301,27 @@
     )
 
 
-def down_kernel(me_ref, arrived_ref, high_ref, low_ref, own_ref, old_ref, out_ref, *, at, cut):
-    @pl.when(me_ref[0] == at)
+def step_kernel(me_ref, arrived_ref, high_ref, low_ref, own_ref, old_ref, out_ref, *, at, cut):
+    active = lax.rem(me_ref[0], 2) == 0 if at is None else me_ref[0] == at
+
+    @pl.when(active)
     def _():
         real, imag = product(arrived_ref[...], high_ref[...], low_ref[...])
         out_ref[0] = real + own_ref[0, cut]
         out_ref[1] = imag + own_ref[1, cut]
 
-    @pl.when(me_ref[0] != at)
+    @pl.when(jnp.logical_not(active))
     def _():
         out_ref[...] = old_ref[...]
 
 
-def down_step(me, at, arrived, panel, own, first, old, after):
+def step(name, me, at, arrived, panel, own, first, old, after):
     cut = slice(first, first + old.shape[1])
     return call(
-        lambda *refs: down_kernel(*refs, at=at, cut=cut),
-        "down",
+        lambda *refs: step_kernel(*refs, at=at, cut=cut),
+        name,
         [(SMEM, me)] + [(VMEM, value) for value in (arrived, *panel, own, old)],
         floats(*old.shape),
-        VMEM,
-        after,
-    )
-
-
-def up_kernel(me_ref, arrived_ref, oh, ol, beside_ref, eh, el, own_ref, old_ref, out_ref, *, at, top):
-    @pl.when(me_ref[0] == at)
-    def _():
-        if top:
-            out_ref[...] = beside_ref[...]
-        else:
-            real, imag = product(arrived_ref[...], oh[...], ol[...])
-            out_ref[0] = real + beside_ref[0]
-            out_ref[1] = imag + beside_ref[1]
-        real, imag = product(out_ref[...], eh[...], el[...])
-        out_ref[0] = real + own_ref[0]
-        out_ref[1] = imag + own_ref[1]
-
-    @pl.when(me_ref[0] != at)
-    def _():
-        out_ref[...] = old_ref[...]
-
-
-def up_step(me, at, arrived, odd, beside, even, own, old, top, after):
-    return call(
-        lambda *refs: up_kernel(*refs, at=at, top=top),
-        "up",
-        [(SMEM, me)] + [(VMEM, value) for value in (arrived, *odd, beside, *even, own, old)],
-        floats(*own.shape),
         VMEM,
         after,
     )
@@ -386,7 +441,7 @@
 
     def toward(number, turn):
         size, which = sets[number]
-        if size == 4 and turn == 0:
+        if turn == 0 and number != 1:
             return [(s, s ^ 2) for s in range(slabs)]
         bit = 1 << (turn if size == 2 else turn - 1)
         return [
@@ -406,7 +461,7 @@
     total, sent, base = {}, {}, {}
 
     def stage_join(number, token):
-        following = [part[1] for part in parts[number + 1 : number + 2]]
+        following = [part[1] for part in parts[number + 1 : number + 2]] if number >= 2 else []
         keep, joined, *gate = join(parts[number][0], swapped[number], following, token)
         total[number] = keep
         sent[number] = hop(joined, toward(number, 0))
@@ -423,28 +478,32 @@
         return [base[number]]
 
     token = stage_join(0, [parts[1][0]])
+    let = gate([part[1] for part in parts[1:3]], token)
+    swapped += [hop(value, swapping) for value in let]
+    token = let[:1]
     for turn in range(1, hops + 1):
         token = stage_add(0, turn, token)
-    token = stage_join(1, token)
     up = halves(up_panel[0, 0], token)
     maps = halves(recovery[0, 0], [up[0]])
-    token = stage_add(1, 1, [maps[0]])
+    early = hold(me, 1, up_panel[0, 0], [maps[0]])
+    early_panel = hop(early, [(p + 1, p) for p in range(0, slabs - 2, 4)])
+    token = stage_join(1, [early])
     token = stage_source(0, token)
     state = list(cleave(base[0], streams, token))
     token = [state[0]]
-    beside_panel = None
+    arrived = [hop(state[t], [(0, 1)]) for t in lanes]
     for s in range(1, slabs):
-        arrived = [hop(state[t], [(s - 1, s)]) for t in lanes]
         number = s // 2 if s < 4 else s // 4 + 1
         for t in lanes:
-            state[t] = down_step(
-                me, s, arrived[t], down, base[number], t * rows, state[t], token
-            )
+            state[t] = step("down", me, s, arrived[t], down, base[number], t * rows, state[t], token)
             token = [state[t]]
+        if s + 1 < slabs:
+            arrived = [hop(state[t], [(s, s + 1)]) for t in lanes]
+        else:
+            beside = [hop(state[t], [(p + 1, p) for p in range(0, slabs, 2)]) for t in lanes]
         if s == 1:
-            for turn in range(2, hops + 1):
+            for turn in range(1, hops + 1):
                 token = stage_add(1, turn, token)
-            token = stage_source(1, token)
         number = s // 4 + 2
         if number < len(sets):
             if s % 4 == 1:
@@ -455,27 +514,25 @@
             if s % 4 == 3:
                 token = stage_source(number, token)
         if s == 1:
-            held = hold(up_panel[0, 0], token)
-            token = [held]
-            beside_panel = hop(held, [(p + 1, p) for p in range(0, slabs - 2, 2)])
-    beside = [hop(state[t], [(p + 1, p) for p in range(0, slabs, 2)]) for t in lanes]
-    odd_up = halves(beside_panel, token)
-    token = [odd_up[0]]
-    above = list(state)
+            late = hold(me, 3, up_panel[0, 0], token)
+            late_panel = hop(late, [(p + 1, p) for p in range(2, slabs - 2, 4)])
+            token = stage_source(1, [late])
+    local = []
     for t in lanes:
-        above[t] = up_step(
-            me, slabs - 2, state[t], odd_up, beside[t], up, state[t], above[t], True, token
-        )
-        token = [above[t]]
+        local.append(step("local", me, None, beside[t], up, state[t], 0, state[t], token))
+        token = [local[t]]
+    above = list(local)
+    arrived = [hop(above[t], [(slabs - 2, slabs - 4)]) for t in lanes]
+    pair = pair_panel(me, early_panel, late_panel, up, token, slabs - 2)
+    token = [pair[0]]
     for p in range(slabs - 4, -1, -2):
-        arrived = [hop(above[t], [(p + 2, p)]) for t in lanes]
         if p == 0:
             after = [hop(above[t], [(q + 2, q + 1) for q in range(0, slabs - 2, 2)]) for t in lanes]
         for t in lanes:
-            above[t] = up_step(
-                me, p, arrived[t], odd_up, beside[t], up, state[t], above[t], False, token
-            )
+            above[t] = step("up", me, p, arrived[t], pair, local[t], 0, above[t], token)
             token = [above[t]]
+        if p > 0:
+            arrived = [hop(above[t], [(p, p - 2)]) for t in lanes]
     ups, head, tail = finish(me, after, up, state, above, width, token)
 
     left = lax.ppermute(tail, "lat", [(i, i + 1) for i in range(lats - 1)])

time: 144 us -> 136 us (0.944)
  waiting for transfers between devices: 64.2 us -> 50.8 us
  Pallas kernels: 15.6 us -> 19.9 us
  starting transfers between devices: 47 us -> 49.4 us
  local copies, waits for them, and re-layouts: 4.99 us -> 3.05 us
    ppermute x34 -> x35, waiting for transfers between devices: 62.5 us -> 49.1 us  [hop(): return lax.ppermute(value, 'slab', route)]
    ppermute x34 -> x35, starting transfers between devices: 32.8 us -> 38 us  [hop(): return lax.ppermute(value, 'slab', route)]
    pallas_call x43 -> x45, Pallas kernels: 15.6 us -> 19.9 us  [call(): pl.pallas_call(run, in_specs=list(specs) + [ANY] * len(after), out_specs=...]
    ppermute x1, starting transfers between devices: 12.2 us -> 9.42 us  [body(): left = lax.ppermute(tail, 'lat', [(i, i + 1) for i in range(lats - 1)])]
    unnamed x33 -> x31, local copies, waits for them, and re-layouts: 4.99 us -> 3.05 us
  transfers between devices with their start and end apart: 36 -> 37, of which waited for: 14 -> 11; matrix products, arithmetic and copies ran while one was open for 0% -> 0% of each run, Pallas kernels for 8% -> 11%
where the time goes in v3:
time: 136 us
  waiting for transfers between devices  50.8 us (37%)
  starting transfers between devices  49.4 us (36%)
  Pallas kernels  19.9 us (15%)
  blocking collectives  10.5 us (8%)
  local copies, waits for them, and re-layouts  3.05 us (2%)
  between operations  1.59 us (1%)
    ppermute x35, waiting for transfers between devices, hop(): return lax.ppermute(value, 'slab', route)  49.1 us
    ppermute x35, starting transfers between devices, hop(): return lax.ppermute(value, 'slab', route)  38 us
    pallas_call x45, Pallas kernels, call(): pl.pallas_call(run, in_specs=list(specs) + [ANY] * len(after), out_specs=...  19.9 us
    all_to_all x1, blocking collectives, body(): lax.all_to_all(outgoing, 'slab', split_axis=0, concat_axis=0, tiled=True)  10.5 us
    ppermute x1, starting transfers between devices, body(): left = lax.ppermute(tail, 'lat', [(i, i + 1) for i in range(lats - 1)])  9.42 us
    unnamed x31, local copies, waits for them, and re-layouts  3.05 us
  transfers between devices with their start and end apart: 37, of which 11 were waited for; matrix products, arithmetic and copies ran while one was open for 0% of the time, Pallas kernels for 11%

profile of v3, /device:TPU:1, one launch (start us, length us, event | category | flops | bytes accessed | tf_op | source)
XLA Modules:
  0.0 135.7 jit_solution(17963068878951073103)
XLA Ops:
  0.7 2.8 %collect.2 = (f32[1,2,64,512]{3,2,1,0:T(8,128)}, f32[1,2,64,512]{3,2,1,0:T(8,128)}) custom-call(s32[1]{0:T(128)} %bitcast.refs_0_, s32[32]{0:T(128)} %bitcast.22, s32[32]{0:T(128)} %refs_2_.5, f32[32,2,64,128]{3,2,1,0:T(8,128)} %refs_3_.4), custom_call_target="tpu_custom_call" | custom-call | flops 2000000000 | bytes 2000000 | tf_op jit(solution)/shard_map/collect/pallas_call | solution.py:46
  3.5 2.2 %collective-permute-start = (f32[1,2,64,512]{3,2,1,0:T(8,128)}, f32[1,2,64,512]{3,2,1,0:T(8,128)S(1)}, u32[]{:S(2)}, u32[]{:S(2)}) collective-permute-start(f32[1,2,64,512]{3,2,1,0:T(8,128)} %get-tuple-element.32), channel_id=1, source_target_pairs={{0,4},{4,0},{8,12},{12,8},{16,20},{20,16},{24,28},{28,24},{1,5},{5... | collective-permute-start | bytes 786440 | tf_op jit(solution)/shard_map/ppermute | solution.py:440
  5.8 0.9 copy-done.1
  6.7 1.6 %ready.1 = (f32[64,2]{1,0:T(8,128)S(1)}, s32[8]{0:T(128)S(1)}) custom-call(s32[64]{0:T(128)S(1)} %copy-done.4, s32[8]{0:T(128)S(1)} %bitcast.16, s32[8]{0:T(128)S(1)} %copy-done.6, f32[64,2]{1,0:T(8,128)S(1)} %copy.13.refs_3_, f32[1,2,64,512]{3,2,1,0:T(8,128)S(1)} %copy-done.1), custom_call_target="tpu_custom_call" | custom-call | tf_op jit(solution)/shard_map/ready/pallas_call | solution.py:46
  8.9 1.0 copy-done.8
  9.9 2.0 %collect.3 = (f32[1,2,64,512]{3,2,1,0:T(8,128)S(1)}, f32[1,2,64,512]{3,2,1,0:T(8,128)S(1)}, f32[2,2,64,512]{3,2,1,0:T(8,128)S(1)}, f32[2,2,64,512]{3,2,1,0:T(8,128)S(1)}) custom-call(s32[1]{0:T(128)} %bitcast.refs_0_, s32[32]{0:T(128)S(1)} %bitcast.23, s32[32]{0:T(128)S(1)} %copy-done.11, f32[32,2,64,128]{3,2,1,0:T(8,128)S(1)} %copy-done.8, ...), custom_call_target="tpu_custom_call" | custom-call | flops 2000000000 | bytes 2000000 | tf_op jit(solution)/shard_map/collect/pallas_call | solution.py:46
  12.1 1.3 collective-permute-start.1
  13.4 1.0 collective-permute-start.3
  15.0 3.9 %collective-permute-done.1.refs_1_ = f32[2,64,512]{2,1,0:T(8,128)S(1)} collective-permute-done((f32[2,64,512]{2,1,0:T(8,128)S(1)}, f32[2,64,512]{2,1,0:T(8,128)S(1)}, u32[]{:S(2)}, u32[]{:S(2)}) %collective-permute-start.1) | collective-permute-done | bytes 262176 | tf_op jit(solution)/shard_map/ppermute | solution.py:440
  18.9 1.3 collective-permute-start.2
  20.7 1.6 %halves.5 = (bf16[768,2048]{1,0:T(8,128)(2,1)S(1)}, bf16[768,2048]{1,0:T(8,128)(2,1)S(1)}) custom-call(f32[2,768,1024]{2,1,0:T(8,128)S(1)} %bitcast.19, bf16[512,1024]{1,0:T(8,128)(2,1)S(1)} %get-tuple-element.41.refs_1_.refs_2_.refs_3_.refs_7_), custom_call_target="tpu_custom_call" | custom-call | flops 2000000000 | bytes 2000000 | tf_op jit(solution)/shard_map/halves/pallas_call | solution.py:46
  22.5 2.3 %collective-permute-start.6 = (f32[2,64,512]{2,1,0:T(8,128)S(1)}, f32[2,64,512]{2,1,0:T(8,128)S(1)}, u32[]{:S(2)}, u32[]{:S(2)}) collective-permute-start(f32[2,64,512]{2,1,0:T(8,128)S(1)} %get-tuple-element.46), channel_id=1, source_target_pairs={{0,8},{4,12},{16,24},{20,28},{1,9},{5,13},{17,25},{21,29},{2,10},{... | collective-permute-start | bytes 786440 | tf_op jit(solution)/shard_map/ppermute | solution.py:440
  24.7 2.7 %collective-permute-done.2.refs_1_ = f32[2,64,512]{2,1,0:T(8,128)S(1)} collective-permute-done((f32[2,64,512]{2,1,0:T(8,128)S(1)}, f32[2,64,512]{2,1,0:T(8,128)S(1)}, u32[]{:S(2)}, u32[]{:S(2)}) %collective-permute-start.2) | collective-permute-done | bytes 262176 | tf_op jit(solution)/shard_map/ppermute | solution.py:440
  27.6 1.9 %collective-permute-start.4 = (f32[2,32,512]{2,1,0:T(8,128)S(1)}, f32[2,32,512]{2,1,0:T(8,128)S(1)}, u32[]{:S(2)}, u32[]{:S(2)}) collective-permute-start(f32[2,32,512]{2,1,0:T(8,128)S(1)} %get-tuple-element.44.refs_5_.refs_6_), channel_id=1, source_target_pairs={{0,4},{1,5},{2,6},{3,7}} | collective-permute-start | bytes 393224 | tf_op jit(solution)/shard_map/ppermute | solution.py:440
  29.5 1.3 collective-permute-start.7
  30.8 1.3 collective-permute-start.25
  32.1 0.7 collective-permute-done.4.refs_1_
  32.9 2.3 %collective-permute-done.7.refs_1_ = f32[2,32,512]{2,1,0:T(8,128)S(1)} collective-permute-done((f32[2,32,512]{2,1,0:T(8,128)S(1)}, f32[2,32,512]{2,1,0:T(8,128)S(1)}, u32[]{:S(2)}, u32[]{:S(2)}) %collective-permute-start.7) | collective-permute-done | bytes 131104 | tf_op jit(solution)/shard_map/ppermute | solution.py:440
  35.3 0.8 collective-permute-start.26
  36.1 0.7 collective-permute-start.8
  36.9 0.7 collective-permute-start.5
  37.6 0.7 collective-permute-start.12
  38.4 0.7 collective-permute-start.10
  39.1 3.3 %collective-permute-done.11.refs_1_ = f32[2,64,512]{2,1,0:T(8,128)S(1)} collective-permute-done((f32[2,64,512]{2,1,0:T(8,128)S(1)}, f32[2,64,512]{2,1,0:T(8,128)S(1)}, u32[]{:S(2)}, u32[]{:S(2)}) %collective-permute-start.11) | collective-permute-done | bytes 262176 | tf_op jit(solution)/shard_map/ppermute | solution.py:440
  42.4 6.2 %collective-permute-start.14 = (f32[2,64,512]{2,1,0:T(8,128)S(1)}, f32[2,64,512]{2,1,0:T(8,128)S(1)}, u32[]{:S(2)}, u32[]{:S(2)}) collective-permute-start(f32[2,64,512]{2,1,0:T(8,128)S(1)} %add.5.refs_6_.refs_0_), channel_id=1, source_target_pairs={{0,16},{4,20},{8,24},{12,28},{1,17},{5,21},{9,25},{13,29},{2,18},{... | collective-permute-start | bytes 786440 | tf_op jit(solution)/shard_map/ppermute | solution.py:440
  50.7 1.2 collective-permute-done.14.refs_1_
  52.8 0.7 collective-permute-start.19
  53.5 0.7 collective-permute-start.18
  54.2 0.7 collective-permute-start.21
  56.3 1.3 collective-permute-start.22
  57.7 1.3 collective-permute-start.27
  59.0 19.7 %collective-permute-done.22.refs_1_ = f32[2,32,512]{2,1,0:T(8,128)S(1)} collective-permute-done((f32[2,32,512]{2,1,0:T(8,128)S(1)}, f32[2,32,512]{2,1,0:T(8,128)S(1)}, u32[]{:S(2)}, u32[]{:S(2)}) %collective-permute-start.22) | collective-permute-done | bytes 131104 | tf_op jit(solution)/shard_map/ppermute | solution.py:440
  80.1 1.5 %collective-permute-done.27.refs_1_ = f32[2,32,512]{2,1,0:T(8,128)S(1)} collective-permute-done((f32[2,32,512]{2,1,0:T(8,128)S(1)}, f32[2,32,512]{2,1,0:T(8,128)S(1)}, u32[]{:S(2)}, u32[]{:S(2)}) %collective-permute-start.27) | collective-permute-done | bytes 131104 | tf_op jit(solution)/shard_map/ppermute | solution.py:440
  82.9 4.2 %pair.1 = (bf16[512,1024]{1,0:T(8,128)(2,1)S(1)}, bf16[512,1024]{1,0:T(8,128)(2,1)S(1)}) custom-call(s32[1]{0:T(128)} %bitcast.refs_0_, f32[2,512,512]{2,1,0:T(8,128)S(1)} %collective-permute-done.25.refs_1_, f32[2,512,512]{2,1,0:T(8,128)S(1)} %collective-permute-done.26.refs_2_, bf16[512,1024]{1,0:T(8,128)(2,1)S(1)} %get-tuple-element.41.refs_1_.refs_2_.refs_3_.refs_7_, ...), custom_call_target="tpu_custom_call" | custom-call | tf_op jit(solution)/shard_map/pair/pallas_call | solution.py:46
  87.8 0.7 collective-permute-start.31
  88.6 1.3 collective-permute-start.33
  89.9 1.3 collective-permute-start.34
  91.2 0.7 collective-permute-start.32
  92.5 12.5 %collective-permute-done.33.refs_1_ = f32[2,32,512]{2,1,0:T(8,128)S(1)} collective-permute-done((f32[2,32,512]{2,1,0:T(8,128)S(1)}, f32[2,32,512]{2,1,0:T(8,128)S(1)}, u32[]{:S(2)}, u32[]{:S(2)}) %collective-permute-start.33) | collective-permute-done | bytes 131104 | tf_op jit(solution)/shard_map/ppermute | solution.py:440
  105.7 1.3 collective-permute-done.34.refs_1_
  107.7 0.7 finish.1
  108.5 9.4 %collective-permute-start.35 = (f32[2,64,128]{2,1,0:T(8,128)S(1)}, f32[2,64,128]{2,1,0:T(8,128)S(1)}, u32[]{:S(2)}, u32[]{:S(2)}) collective-permute-start(f32[2,64,128]{2,1,0:T(8,128)S(1)} %get-tuple-element.58), channel_id=1, source_target_pairs={{0,1},{1,2},{2,3},{4,5},{5,6},{6,7},{8,9},{9,10},{10,11},{12,13},{... | collective-permute-start | bytes 196616 | tf_op jit(solution)/shard_map/ppermute | solution.py:538
  117.9 1.9 %collective-permute-start.36 = (f32[2,64,128]{2,1,0:T(8,128)S(1)}, f32[2,64,128]{2,1,0:T(8,128)S(1)}, u32[]{:S(2)}, u32[]{:S(2)}) collective-permute-start(f32[2,64,128]{2,1,0:T(8,128)S(1)} %get-tuple-element.59), channel_id=1, source_target_pairs={{1,0},{2,1},{3,2},{5,4},{6,5},{7,6},{9,8},{10,9},{11,10},{13,12},{... | collective-permute-start | bytes 196616 | tf_op jit(solution)/shard_map/ppermute | solution.py:539
  119.8 0.9 copy-done.9
  120.8 1.0 middle.1.refs_1_
  121.8 1.7 %collective-permute-done.36.refs_3_ = f32[2,64,128]{2,1,0:T(8,128)S(1)} collective-permute-done((f32[2,64,128]{2,1,0:T(8,128)S(1)}, f32[2,64,128]{2,1,0:T(8,128)S(1)}, u32[]{:S(2)}, u32[]{:S(2)}) %collective-permute-start.36) | collective-permute-done | bytes 65568 | tf_op jit(solution)/shard_map/ppermute | solution.py:539
  123.5 1.2 rim.1
  124.6 10.5 %all_to_all.9 = f32[8,8,128]{2,1,0:T(8,128)S(1)} all-to-all(f32[8,8,128]{2,1,0:T(8,128)S(1)} %bitcast.15), channel_id=1, replica_groups=mesh['slab'=8,'lat'=4] {'slab'}, dimensions={0} | all-to-all | bytes 65536 | tf_op jit(solution)/shard_map/all_to_all | solution.py:542
  (105 shorter events, 12.8 us)
Async XLA Ops:
  0.6 5.0 %copy-start.12 = (f32[64,2]{0,1:T(2,128)S(1)}, f32[64,2]{0,1:T(2,128)}, u32[]{:S(2)}) copy-start(f32[64,2]{0,1:T(2,128)} %param.15) | copy-start | bytes 1540
  0.6 5.1 %copy-start.4 = (s32[64]{0:T(128)S(1)}, s32[64]{0:T(128)}, u32[]{:S(2)}) copy-start(s32[64]{0:T(128)} %refs_0_.1) | copy-start | bytes 772
  0.7 5.1 %copy-start.5 = (s32[8,1]{0,1:T(1,128)S(1)}, s32[8,1]{0,1:T(1,128)}, u32[]{:S(2)}) copy-start(s32[8,1]{0,1:T(1,128)} %param.20) | copy-start | bytes 100
  0.7 5.1 %copy-start.6 = (s32[8]{0:T(128)S(1)}, s32[8]{0:T(128)}, u32[]{:S(2)}) copy-start(s32[8]{0:T(128)} %refs_2_.4) | copy-start | bytes 100
  0.7 7.6 %copy-start.7 = (f32[1,1,2,512,512]{4,3,2,1,0:T(8,128)S(1)}, f32[1,1,2,512,512]{4,3,2,1,0:T(8,128)}, u32[]{:S(2)}) copy-start(f32[1,1,2,512,512]{4,3,2,1,0:T(8,128)} %param.16) | copy-start | bytes 6291460
  3.5 8.5 %collective-permute-start = (f32[1,2,64,512]{3,2,1,0:T(8,128)}, f32[1,2,64,512]{3,2,1,0:T(8,128)S(1)}, u32[]{:S(2)}, u32[]{:S(2)}) collective-permute-start(f32[1,2,64,512]{3,2,1,0:T(8,128)} %get-tuple-element.32), channel_id=1, source_target_pairs={{0,4},{4,0},{8,12},{12,8},{16,20},{20,16},{24,28},{28,24},{1,5},{5... | collective-permute-start | bytes 786440 | tf_op jit(solution)/shard_map/ppermute | solution.py:440
  8.3 1.6 %copy-start.8 = (f32[32,2,64,128]{3,2,1,0:T(8,128)S(1)}, f32[32,2,64,128]{3,2,1,0:T(8,128)}, u32[]{:S(2)}) copy-start(f32[32,2,64,128]{3,2,1,0:T(8,128)} %refs_3_.4) | copy-start | bytes 6291460
  9.9 2.1 %copy-start.2 = (f32[1,2,64,512]{3,2,1,0:T(8,128)S(1)}, f32[1,2,64,512]{3,2,1,0:T(8,128)}, u32[]{:S(2)}) copy-start(f32[1,2,64,512]{3,2,1,0:T(8,128)} %get-tuple-element.31.refs_4_.refs_0_) | copy-start | bytes 786436
  9.9 10.8 %slice-start = ((s8[6291456]{0:T(1024)(128)(4,1)}), s8[4194304]{0:T(1024)(128)(4,1)S(1)}, s32[]{:S(2)}) async-start(s8[6291456]{0:T(1024)(128)(4,1)} %bitcast.17), calls=%async_computation.1 | async-start | bytes 8388608
  12.0 8.2 %copy-start = (f32[1,1,2,512,512]{4,3,2,1,0:T(8,128)S(1)}, f32[1,1,2,512,512]{4,3,2,1,0:T(8,128)}, u32[]{:S(2)}) copy-start(f32[1,1,2,512,512]{4,3,2,1,0:T(8,128)} %param.17) | copy-start | bytes 6291460
  12.1 6.8 %collective-permute-start.1 = (f32[2,64,512]{2,1,0:T(8,128)S(1)}, f32[2,64,512]{2,1,0:T(8,128)S(1)}, u32[]{:S(2)}, u32[]{:S(2)}) collective-permute-start(f32[2,64,512]{2,1,0:T(8,128)S(1)} %get-tuple-element.37), channel_id=1, source_target_pairs={{0,8},{4,12},{8,0},{12,4},{16,24},{20,28},{24,16},{28,20},{1,9},{5... | collective-permute-start | bytes 786440 | tf_op jit(solution)/shard_map/ppermute | solution.py:440
  13.4 7.4 %slice-start.1 = ((s8[6291456]{0:T(1024)(128)(4,1)}), s8[2097152]{0:T(1024)(128)(4,1)S(1)}, s32[]{:S(2)}) async-start(s8[6291456]{0:T(1024)(128)(4,1)} %bitcast.17), calls=%async_computation.2 | async-start | bytes 4194304
  13.4 9.0 %collective-permute-start.3 = (f32[1,2,64,512]{3,2,1,0:T(8,128)S(1)}, f32[1,2,64,512]{3,2,1,0:T(8,128)S(1)}, u32[]{:S(2)}, u32[]{:S(2)}) collective-permute-start(f32[1,2,64,512]{3,2,1,0:T(8,128)S(1)} %get-tuple-element.40.refs_2_), channel_id=1, source_target_pairs={{0,4},{4,0},{8,12},{12,8},{16,20},{20,16},{24,28},{28,24},{1,5},{5... | collective-permute-start | bytes 786440 | tf_op jit(solution)/shard_map/ppermute | solution.py:440
  14.5 20.8 %collective-permute-start.9 = (f32[2,2,64,512]{3,2,1,0:T(8,128)S(1)}, f32[2,2,64,512]{3,2,1,0:T(8,128)S(1)}, u32[]{:S(2)}, u32[]{:S(2)}) collective-permute-start(f32[2,2,64,512]{3,2,1,0:T(8,128)S(1)} %get-tuple-element.49), channel_id=1, source_target_pairs={{0,4},{4,0},{8,12},{12,8},{16,20},{20,16},{24,28},{28,24},{1,5},{5... | collective-permute-start | bytes 1572872 | tf_op jit(solution)/shard_map/ppermute | solution.py:440
  18.9 8.6 %collective-permute-start.2 = (f32[2,64,512]{2,1,0:T(8,128)S(1)}, f32[2,64,512]{2,1,0:T(8,128)S(1)}, u32[]{:S(2)}, u32[]{:S(2)}) collective-permute-start(f32[2,64,512]{2,1,0:T(8,128)S(1)} %add.3.refs_1_.refs_0_), channel_id=1, source_target_pairs={{16,0},{20,4},{17,1},{21,5},{18,2},{22,6},{19,3},{23,7}} | collective-permute-start | bytes 786440 | tf_op jit(solution)/shard_map/ppermute | solution.py:440
  22.5 12.7 %collective-permute-start.6 = (f32[2,64,512]{2,1,0:T(8,128)S(1)}, f32[2,64,512]{2,1,0:T(8,128)S(1)}, u32[]{:S(2)}, u32[]{:S(2)}) collective-permute-start(f32[2,64,512]{2,1,0:T(8,128)S(1)} %get-tuple-element.46), channel_id=1, source_target_pairs={{0,8},{4,12},{16,24},{20,28},{1,9},{5,13},{17,25},{21,29},{2,10},{... | collective-permute-start | bytes 786440 | tf_op jit(solution)/shard_map/ppermute | solution.py:440
  27.6 5.3 %collective-permute-start.4 = (f32[2,32,512]{2,1,0:T(8,128)S(1)}, f32[2,32,512]{2,1,0:T(8,128)S(1)}, u32[]{:S(2)}, u32[]{:S(2)}) collective-permute-start(f32[2,32,512]{2,1,0:T(8,128)S(1)} %get-tuple-element.44.refs_5_.refs_6_), channel_id=1, source_target_pairs={{0,4},{1,5},{2,6},{3,7}} | collective-permute-start | bytes 393224 | tf_op jit(solution)/shard_map/ppermute | solution.py:440
  29.5 5.7 %collective-permute-start.7 = (f32[2,32,512]{2,1,0:T(8,128)S(1)}, f32[2,32,512]{2,1,0:T(8,128)S(1)}, u32[]{:S(2)}, u32[]{:S(2)}) collective-permute-start(f32[2,32,512]{2,1,0:T(8,128)S(1)} %get-tuple-element.47.refs_5_), channel_id=1, source_target_pairs={{0,4},{1,5},{2,6},{3,7}} | collective-permute-start | bytes 393224 | tf_op jit(solution)/shard_map/ppermute | solution.py:440
  30.8 52.1 %collective-permute-start.25 = (f32[2,512,512]{2,1,0:T(8,128)S(1)}, f32[2,512,512]{2,1,0:T(8,128)S(1)}, u32[]{:S(2)}, u32[]{:S(2)}) collective-permute-start(f32[2,512,512]{2,1,0:T(8,128)S(1)} %hold.2.refs_2_), channel_id=1, source_target_pairs={{4,0},{20,16},{5,1},{21,17},{6,2},{22,18},{7,3},{23,19}} | collective-permute-start | bytes 6291464 | tf_op jit(solution)/shard_map/ppermute | solution.py:440
  35.3 47.6 %collective-permute-start.26 = (f32[2,512,512]{2,1,0:T(8,128)S(1)}, f32[2,512,512]{2,1,0:T(8,128)S(1)}, u32[]{:S(2)}, u32[]{:S(2)}) collective-permute-start(f32[2,512,512]{2,1,0:T(8,128)S(1)} %hold.3.refs_3_), channel_id=1, source_target_pairs={{12,8},{13,9},{14,10},{15,11}} | collective-permute-start | bytes 6291464 | tf_op jit(solution)/shard_map/ppermute | solution.py:440
  36.1 1.4 %collective-permute-start.8 = (f32[2,64,512]{2,1,0:T(8,128)S(1)}, f32[2,64,512]{2,1,0:T(8,128)S(1)}, u32[]{:S(2)}, u32[]{:S(2)}) collective-permute-start(f32[2,64,512]{2,1,0:T(8,128)S(1)} %add.4.refs_2_.refs_0_), channel_id=1, source_target_pairs={{24,8},{28,12},{25,9},{29,13},{26,10},{30,14},{27,11},{31,15}} | collective-permute-start | bytes 786440 | tf_op jit(solution)/shard_map/ppermute | solution.py:440
  36.8 5.6 %collective-permute-start.11 = (f32[2,64,512]{2,1,0:T(8,128)S(1)}, f32[2,64,512]{2,1,0:T(8,128)S(1)}, u32[]{:S(2)}, u32[]{:S(2)}) collective-permute-start(f32[2,64,512]{2,1,0:T(8,128)S(1)} %get-tuple-element.51), channel_id=1, source_target_pairs={{0,8},{4,12},{8,0},{12,4},{16,24},{20,28},{24,16},{28,20},{1,9},{5... | collective-permute-start | bytes 786440 | tf_op jit(solution)/shard_map/ppermute | solution.py:440
  36.9 1.5 %collective-permute-start.5 = (f32[2,32,512]{2,1,0:T(8,128)S(1)}, f32[2,32,512]{2,1,0:T(8,128)S(1)}, u32[]{:S(2)}, u32[]{:S(2)}) collective-permute-start(f32[2,32,512]{2,1,0:T(8,128)S(1)} %down.14.refs_6_.refs_5_), channel_id=1, source_target_pairs={{4,8},{5,9},{6,10},{7,11}} | collective-permute-start | bytes 393224 | tf_op jit(solution)/shard_map/ppermute | solution.py:440
  37.6 1.5 %collective-permute-start.12 = (f32[2,32,512]{2,1,0:T(8,128)S(1)}, f32[2,32,512]{2,1,0:T(8,128)S(1)}, u32[]{:S(2)}, u32[]{:S(2)}) collective-permute-start(f32[2,32,512]{2,1,0:T(8,128)S(1)} %down.15.refs_2_.refs_5_), channel_id=1, source_target_pairs={{4,8},{5,9},{6,10},{7,11}} | collective-permute-start | bytes 393224 | tf_op jit(solution)/shard_map/ppermute | solution.py:440
  38.4 10.9 %collective-permute-start.10 = (f32[2,32,512]{2,1,0:T(8,128)S(1)}, f32[2,32,512]{2,1,0:T(8,128)S(1)}, u32[]{:S(2)}, u32[]{:S(2)}) collective-permute-start(f32[2,32,512]{2,1,0:T(8,128)S(1)} %down.16.refs_6_.refs_5_), channel_id=1, source_target_pairs={{8,12},{9,13},{10,14},{11,15}} | collective-permute-start | bytes 393224 | tf_op jit(solution)/shard_map/ppermute | solution.py:440
  42.4 9.5 %collective-permute-start.14 = (f32[2,64,512]{2,1,0:T(8,128)S(1)}, f32[2,64,512]{2,1,0:T(8,128)S(1)}, u32[]{:S(2)}, u32[]{:S(2)}) collective-permute-start(f32[2,64,512]{2,1,0:T(8,128)S(1)} %add.5.refs_6_.refs_0_), channel_id=1, source_target_pairs={{0,16},{4,20},{8,24},{12,28},{1,17},{5,21},{9,25},{13,29},{2,18},{... | collective-permute-start | bytes 786440 | tf_op jit(solution)/shard_map/ppermute | solution.py:440
  48.6 1.4 %collective-permute-start.15 = (f32[2,32,512]{2,1,0:T(8,128)S(1)}, f32[2,32,512]{2,1,0:T(8,128)S(1)}, u32[]{:S(2)}, u32[]{:S(2)}) collective-permute-start(f32[2,32,512]{2,1,0:T(8,128)S(1)} %down.17.refs_2_.refs_5_), channel_id=1, source_target_pairs={{8,12},{9,13},{10,14},{11,15}} | collective-permute-start | bytes 393224 | tf_op jit(solution)/shard_map/ppermute | solution.py:440
  49.3 2.7 %collective-permute-start.13 = (f32[2,32,512]{2,1,0:T(8,128)S(1)}, f32[2,32,512]{2,1,0:T(8,128)S(1)}, u32[]{:S(2)}, u32[]{:S(2)}) collective-permute-start(f32[2,32,512]{2,1,0:T(8,128)S(1)} %down.18.refs_6_.refs_5_), channel_id=1, source_target_pairs={{12,16},{13,17},{14,18},{15,19}} | collective-permute-start | bytes 393224 | tf_op jit(solution)/shard_map/ppermute | solution.py:440
  50.1 2.7 %collective-permute-start.17 = (f32[2,32,512]{2,1,0:T(8,128)S(1)}, f32[2,32,512]{2,1,0:T(8,128)S(1)}, u32[]{:S(2)}, u32[]{:S(2)}) collective-permute-start(f32[2,32,512]{2,1,0:T(8,128)S(1)} %down.19.refs_3_.refs_5_), channel_id=1, source_target_pairs={{12,16},{13,17},{14,18},{15,19}} | collective-permute-start | bytes 393224 | tf_op jit(solution)/shard_map/ppermute | solution.py:440
  52.1 1.4 %collective-permute-start.16 = (f32[2,32,512]{2,1,0:T(8,128)S(1)}, f32[2,32,512]{2,1,0:T(8,128)S(1)}, u32[]{:S(2)}, u32[]{:S(2)}) collective-permute-start(f32[2,32,512]{2,1,0:T(8,128)S(1)} %down.20.refs_6_.refs_5_), channel_id=1, source_target_pairs={{16,20},{17,21},{18,22},{19,23}} | collective-permute-start | bytes 393224 | tf_op jit(solution)/shard_map/ppermute | solution.py:440
  52.8 1.4 %collective-permute-start.19 = (f32[2,32,512]{2,1,0:T(8,128)S(1)}, f32[2,32,512]{2,1,0:T(8,128)S(1)}, u32[]{:S(2)}, u32[]{:S(2)}) collective-permute-start(f32[2,32,512]{2,1,0:T(8,128)S(1)} %down.21.refs_6_.refs_5_), channel_id=1, source_target_pairs={{16,20},{17,21},{18,22},{19,23}} | collective-permute-start | bytes 393224 | tf_op jit(solution)/shard_map/ppermute | solution.py:440
  53.5 1.4 %collective-permute-start.18 = (f32[2,32,512]{2,1,0:T(8,128)S(1)}, f32[2,32,512]{2,1,0:T(8,128)S(1)}, u32[]{:S(2)}, u32[]{:S(2)}) collective-permute-start(f32[2,32,512]{2,1,0:T(8,128)S(1)} %down.22.refs_6_.refs_5_), channel_id=1, source_target_pairs={{20,24},{21,25},{22,26},{23,27}} | collective-permute-start | bytes 393224 | tf_op jit(solution)/shard_map/ppermute | solution.py:440
  54.2 1.4 %collective-permute-start.21 = (f32[2,32,512]{2,1,0:T(8,128)S(1)}, f32[2,32,512]{2,1,0:T(8,128)S(1)}, u32[]{:S(2)}, u32[]{:S(2)}) collective-permute-start(f32[2,32,512]{2,1,0:T(8,128)S(1)} %down.23.refs_6_.refs_5_), channel_id=1, source_target_pairs={{20,24},{21,25},{22,26},{23,27}} | collective-permute-start | bytes 393224 | tf_op jit(solution)/shard_map/ppermute | solution.py:440
  54.9 1.4 %collective-permute-start.20 = (f32[2,32,512]{2,1,0:T(8,128)S(1)}, f32[2,32,512]{2,1,0:T(8,128)S(1)}, u32[]{:S(2)}, u32[]{:S(2)}) collective-permute-start(f32[2,32,512]{2,1,0:T(8,128)S(1)} %down.24.refs_6_.refs_5_), channel_id=1, source_target_pairs={{24,28},{25,29},{26,30},{27,31}} | collective-permute-start | bytes 393224 | tf_op jit(solution)/shard_map/ppermute | solution.py:440
  55.6 2.0 %collective-permute-start.23 = (f32[2,32,512]{2,1,0:T(8,128)S(1)}, f32[2,32,512]{2,1,0:T(8,128)S(1)}, u32[]{:S(2)}, u32[]{:S(2)}) collective-permute-start(f32[2,32,512]{2,1,0:T(8,128)S(1)} %down.25.refs_6_.refs_5_), channel_id=1, source_target_pairs={{24,28},{25,29},{26,30},{27,31}} | collective-permute-start | bytes 393224 | tf_op jit(solution)/shard_map/ppermute | solution.py:440
  56.3 22.4 %collective-permute-start.22 = (f32[2,32,512]{2,1,0:T(8,128)S(1)}, f32[2,32,512]{2,1,0:T(8,128)S(1)}, u32[]{:S(2)}, u32[]{:S(2)}) collective-permute-start(f32[2,32,512]{2,1,0:T(8,128)S(1)} %down.26.refs_6_.refs_4_.refs_5_.refs_3_), channel_id=1, source_target_pairs={{4,0},{12,8},{20,16},{28,24},{5,1},{13,9},{21,17},{29,25},{6,2},{1... | collective-permute-start | bytes 393224 | tf_op jit(solution)/shard_map/ppermute | solution.py:440
  57.7 23.8 %collective-permute-start.27 = (f32[2,32,512]{2,1,0:T(8,128)S(1)}, f32[2,32,512]{2,1,0:T(8,128)S(1)}, u32[]{:S(2)}, u32[]{:S(2)}) collective-permute-start(f32[2,32,512]{2,1,0:T(8,128)S(1)} %down.27.refs_6_.refs_4_.refs_5_), channel_id=1, source_target_pairs={{4,0},{12,8},{20,16},{28,24},{5,1},{13,9},{21,17},{29,25},{6,2},{1... | collective-permute-start | bytes 393224 | tf_op jit(solution)/shard_map/ppermute | solution.py:440
  79.4 7.7 %collective-permute-start.24 = (f32[2,32,512]{2,1,0:T(8,128)S(1)}, f32[2,32,512]{2,1,0:T(8,128)S(1)}, u32[]{:S(2)}, u32[]{:S(2)}) collective-permute-start(f32[2,32,512]{2,1,0:T(8,128)S(1)} %local.2.refs_6_.refs_4_.refs_5_), channel_id=1, source_target_pairs={{24,16},{25,17},{26,18},{27,19}} | collective-permute-start | bytes 393224 | tf_op jit(solution)/shard_map/ppermute | solution.py:440
  82.2 5.6 %collective-permute-start.29 = (f32[2,32,512]{2,1,0:T(8,128)S(1)}, f32[2,32,512]{2,1,0:T(8,128)S(1)}, u32[]{:S(2)}, u32[]{:S(2)}) collective-permute-start(f32[2,32,512]{2,1,0:T(8,128)S(1)} %local.3.refs_5_.refs_4_), channel_id=1, source_target_pairs={{24,16},{25,17},{26,18},{27,19}} | collective-permute-start | bytes 393224 | tf_op jit(solution)/shard_map/ppermute | solution.py:440
  87.1 1.4 %collective-permute-start.28 = (f32[2,32,512]{2,1,0:T(8,128)S(1)}, f32[2,32,512]{2,1,0:T(8,128)S(1)}, u32[]{:S(2)}, u32[]{:S(2)}) collective-permute-start(f32[2,32,512]{2,1,0:T(8,128)S(1)} %up.6.refs_6_.refs_5_), channel_id=1, source_target_pairs={{16,8},{17,9},{18,10},{19,11}} | collective-permute-start | bytes 393224 | tf_op jit(solution)/shard_map/ppermute | solution.py:440
  87.8 2.0 %collective-permute-start.31 = (f32[2,32,512]{2,1,0:T(8,128)S(1)}, f32[2,32,512]{2,1,0:T(8,128)S(1)}, u32[]{:S(2)}, u32[]{:S(2)}) collective-permute-start(f32[2,32,512]{2,1,0:T(8,128)S(1)} %up.7.refs_6_.refs_5_), channel_id=1, source_target_pairs={{16,8},{17,9},{18,10},{19,11}} | collective-permute-start | bytes 393224 | tf_op jit(solution)/shard_map/ppermute | solution.py:440
  88.6 16.5 %collective-permute-start.33 = (f32[2,32,512]{2,1,0:T(8,128)S(1)}, f32[2,32,512]{2,1,0:T(8,128)S(1)}, u32[]{:S(2)}, u32[]{:S(2)}) collective-permute-start(f32[2,32,512]{2,1,0:T(8,128)S(1)} %up.8.refs_6_.refs_5_), channel_id=1, source_target_pairs={{8,0},{9,1},{10,2},{11,3}} | collective-permute-start | bytes 393224 | tf_op jit(solution)/shard_map/ppermute | solution.py:440
  89.9 17.1 %collective-permute-start.34 = (f32[2,32,512]{2,1,0:T(8,128)S(1)}, f32[2,32,512]{2,1,0:T(8,128)S(1)}, u32[]{:S(2)}, u32[]{:S(2)}) collective-permute-start(f32[2,32,512]{2,1,0:T(8,128)S(1)} %up.9.refs_6_.refs_5_), channel_id=1, source_target_pairs={{8,0},{9,1},{10,2},{11,3}} | collective-permute-start | bytes 393224 | tf_op jit(solution)/shard_map/ppermute | solution.py:440
  91.2 16.5 %collective-permute-start.32 = (f32[2,32,512]{2,1,0:T(8,128)S(1)}, f32[2,32,512]{2,1,0:T(8,128)S(1)}, u32[]{:S(2)}, u32[]{:S(2)}) collective-permute-start(f32[2,32,512]{2,1,0:T(8,128)S(1)} %up.9.refs_6_.refs_5_), channel_id=1, source_target_pairs={{8,4},{16,12},{24,20},{9,5},{17,13},{25,21},{10,6},{18,14},{26,22}... | collective-permute-start | bytes 393224 | tf_op jit(solution)/shard_map/ppermute | solution.py:440
  91.9 15.8 %collective-permute-start.30 = (f32[2,32,512]{2,1,0:T(8,128)S(1)}, f32[2,32,512]{2,1,0:T(8,128)S(1)}, u32[]{:S(2)}, u32[]{:S(2)}) collective-permute-start(f32[2,32,512]{2,1,0:T(8,128)S(1)} %up.8.refs_6_.refs_5_), channel_id=1, source_target_pairs={{8,4},{16,12},{24,20},{9,5},{17,13},{25,21},{10,6},{18,14},{26,22}... | collective-permute-start | bytes 393224 | tf_op jit(solution)/shard_map/ppermute | solution.py:440
  107.7 12.1 %copy-start.3 = (f32[1,1,2,64,1024]{4,3,2,1,0:T(8,128)S(1)}, f32[1,1,2,64,1024]{4,3,2,1,0:T(8,128)}, u32[]{:S(2)}) copy-start(f32[1,1,2,64,1024]{4,3,2,1,0:T(8,128)} %param.19) | copy-start | bytes 1572868
  108.5 13.3 %collective-permute-start.35 = (f32[2,64,128]{2,1,0:T(8,128)S(1)}, f32[2,64,128]{2,1,0:T(8,128)S(1)}, u32[]{:S(2)}, u32[]{:S(2)}) collective-permute-start(f32[2,64,128]{2,1,0:T(8,128)S(1)} %get-tuple-element.58), channel_id=1, source_target_pairs={{0,1},{1,2},{2,3},{4,5},{5,6},{6,7},{8,9},{9,10},{10,11},{12,13},{... | collective-permute-start | bytes 196616 | tf_op jit(solution)/shard_map/ppermute | solution.py:538
  117.9 5.6 %collective-permute-start.36 = (f32[2,64,128]{2,1,0:T(8,128)S(1)}, f32[2,64,128]{2,1,0:T(8,128)S(1)}, u32[]{:S(2)}, u32[]{:S(2)}) collective-permute-start(f32[2,64,128]{2,1,0:T(8,128)S(1)} %get-tuple-element.59), channel_id=1, source_target_pairs={{1,0},{2,1},{3,2},{5,4},{6,5},{7,6},{9,8},{10,9},{11,10},{13,12},{... | collective-permute-start | bytes 196616 | tf_op jit(solution)/shard_map/ppermute | solution.py:539
  (4 other events, 5.1 us)

commit v4 on v3

--- a/solution.py
+++ b/solution.py
@@ -78,52 +78,42 @@
     )
 
 
-def pair_kernel(me_ref, one_ref, two_ref, eh, el, high_ref, low_ref, *, top):
-    k, n = one_ref.shape[1:]
-    rows = 128
-    place = lax.rem(me_ref[0], 4)
-
-    def run(panel_ref):
-        def chunk(i, carry):
-            some = pl.ds(pl.multiple_of(i * rows, rows), rows)
-            for part, value in enumerate(product(panel_ref[:, some], eh[...], el[...])):
-                high, low = split(value)
-                high_ref[some, part * n : (part + 1) * n] = high
-                low_ref[some, part * n : (part + 1) * n] = low
-            return carry
-
-        lax.fori_loop(0, k // rows, chunk, 0)
-
-    @pl.when((place == 0) & (me_ref[0] < top))
-    def _():
-        run(one_ref)
-
-    @pl.when((place == 2) & (me_ref[0] < top))
-    def _():
-        run(two_ref)
-
-
-def pair_panel(me, one, two, even, after, top):
-    shape = jax.ShapeDtypeStruct(even[0].shape, jnp.bfloat16)
-    return call(
-        lambda *refs: pair_kernel(*refs, top=top),
-        "pair",
-        [(SMEM, me)] + [(VMEM, value) for value in (one, two, *even)],
-        [shape, shape],
-        [VMEM] * 2,
-        after,
-    )
-
-
-def hold_kernel(me_ref, panel_ref, out_ref, *, place):
-    @pl.when(lax.rem(me_ref[0], 4) == place)
+def either_kernel(me_ref, near_ref, far_ref, high_ref, low_ref):
+    @pl.when(me_ref[0] < 2)
+    def _():
+        halves_kernel(near_ref, high_ref, low_ref)
+
+    @pl.when(me_ref[0] >= 2)
+    def _():
+        halves_kernel(far_ref, high_ref, low_ref)
+
+
+def halves_of_two(me, near, far, after, rows=128):
+    _, k, n = near.shape
+    piece = pl.BlockSpec((2, rows, n), lambda i: (0, i, 0))
+    block = pl.BlockSpec((rows, 2 * n), lambda i: (i, 0))
+    return call(
+        either_kernel,
+        "halves",
+        [(SMEM, me), (piece, near), (piece, far)],
+        [jax.ShapeDtypeStruct((k, 2 * n), jnp.bfloat16)] * 2,
+        [block, block],
+        after,
+        grid=(k // rows,),
+    )
+
+
+def hold_kernel(me_ref, panel_ref, out_ref, *, least):
+    slab = me_ref[0]
+
+    @pl.when((lax.rem(slab, 2) == 1) & ((slab >= least) if least > 1 else (slab == least)))
     def _():
         out_ref[...] = panel_ref[...]
 
 
-def hold(me, place, panel, after):
-    return call(
-        lambda *refs: hold_kernel(*refs, place=place),
+def hold(me, least, panel, after):
+    return call(
+        lambda *refs: hold_kernel(*refs, least=least),
         "hold",
         [(SMEM, me), (VMEM, panel)],
         floats(*panel.shape),
@@ -302,13 +292,15 @@
 
 
 def step_kernel(me_ref, arrived_ref, high_ref, low_ref, own_ref, old_ref, out_ref, *, at, cut):
-    active = lax.rem(me_ref[0], 2) == 0 if at is None else me_ref[0] == at
+    active = me_ref[0] == at
 
     @pl.when(active)
     def _():
-        real, imag = product(arrived_ref[...], high_ref[...], low_ref[...])
-        out_ref[0] = real + own_ref[0, cut]
-        out_ref[1] = imag + own_ref[1, cut]
+        arrived = arrived_ref[...] if arrived_ref.shape == out_ref.shape else arrived_ref[:, cut]
+        real, imag = product(arrived, high_ref[...], low_ref[...])
+        own = own_ref[...] if own_ref.shape == out_ref.shape else own_ref[:, cut]
+        out_ref[0] = real + own[0]
+        out_ref[1] = imag + own[1]
 
     @pl.when(jnp.logical_not(active))
     def _():
@@ -327,36 +319,103 @@
     )
 
 
-def finish_kernel(me_ref, *refs, streams, width):
+def up_kernel(me_ref, arrived_ref, oh, ol, beside_ref, eh, el, own_ref, old_ref, out_ref, *, at):
+    @pl.when(me_ref[0] == at)
+    def _():
+        real, imag = product(arrived_ref[...], oh[...], ol[...])
+        out_ref[0] = real + beside_ref[0]
+        out_ref[1] = imag + beside_ref[1]
+        real, imag = product(out_ref[...], eh[...], el[...])
+        out_ref[0] = real + own_ref[0]
+        out_ref[1] = imag + own_ref[1]
+
+    @pl.when(me_ref[0] != at)
+    def _():
+        out_ref[...] = old_ref[...]
+
+
+def up_step(me, at, arrived, odd, beside, even, own, old, after):
+    return call(
+        lambda *refs: up_kernel(*refs, at=at),
+        "up",
+        [(SMEM, me)] + [(VMEM, value) for value in (arrived, *odd, beside, *even, own, old)],
+        floats(*own.shape),
+        VMEM,
+        after,
+    )
+
+
+def whole(refs):
+    return jnp.concatenate([ref[...] for ref in refs], axis=1)
+
+
+def edges_kernel(me_ref, *refs, streams, width):
     arrived, owns, olds = (refs[i * streams : (i + 1) * streams] for i in range(3))
-    high_ref, low_ref, out_ref, head_ref, tail_ref = refs[3 * streams :]
-    trace = out_ref.shape[-1]
-
-    @pl.when(lax.rem(me_ref[0], 2) == 1)
-    def _():
-        field = jnp.concatenate([ref[...] for ref in arrived], axis=1)
-        real, imag = product(field, high_ref[...], low_ref[...])
-        out_ref[0] = real + jnp.concatenate([ref[0] for ref in owns], axis=0)
-        out_ref[1] = imag + jnp.concatenate([ref[1] for ref in owns], axis=0)
-
-    @pl.when(lax.rem(me_ref[0], 2) == 0)
-    def _():
-        out_ref[...] = jnp.concatenate([ref[...] for ref in olds], axis=1)
-
-    head_ref[...] = out_ref[:, :, :width]
-    tail_ref[...] = out_ref[:, :, trace - width :]
-
-
-def finish(me, arrived, panel, own, old, width, after):
+    high_ref, low_ref, head_ref, tail_ref = refs[3 * streams :]
+    trace = high_ref.shape[1] // 2
+    first, last = slice(0, width), slice(trace - width, trace)
+    passed = lax.rem(me_ref[0], 2) == 1
+
+    def ends(ref):
+        more = (slice(trace, trace + width), slice(2 * trace - width, 2 * trace))
+        return jnp.concatenate([ref[:, cut] for cut in (first, last, *more)], axis=1)
+
+    @pl.when(passed)
+    def _():
+        values = product(whole(arrived), ends(high_ref), ends(low_ref))
+        own = whole(owns)
+        for part, value in enumerate(values):
+            head_ref[part] = value[:, :width] + own[part, :, first]
+            tail_ref[part] = value[:, width:] + own[part, :, last]
+
+    @pl.when(jnp.logical_not(passed))
+    def _():
+        old = whole(olds)
+        head_ref[...] = old[:, :, first]
+        tail_ref[...] = old[:, :, last]
+
+
+def edges(me, arrived, panel, own, old, width, after):
+    streams = len(own)
+    shots = own[0].shape[1] * streams
+    return call(
+        lambda *refs: edges_kernel(*refs, streams=streams, width=width),
+        "edges",
+        [(SMEM, me)] + [(VMEM, value) for value in (*arrived, *own, *old, *panel)],
+        [floats(2, shots, width)] * 2,
+        [VMEM] * 2,
+        after,
+    )
+
+
+def finish_kernel(me_ref, *refs, streams):
+    arrived, owns, olds = (refs[i * streams : (i + 1) * streams] for i in range(3))
+    high_ref, low_ref, out_ref, again_ref = refs[3 * streams :]
+    passed = lax.rem(me_ref[0], 2) == 1
+
+    @pl.when(passed)
+    def _():
+        real, imag = product(whole(arrived), high_ref[...], low_ref[...])
+        own = whole(owns)
+        out_ref[0] = real + own[0]
+        out_ref[1] = imag + own[1]
+
+    @pl.when(jnp.logical_not(passed))
+    def _():
+        out_ref[...] = whole(olds)
+
+    again_ref[...] = out_ref[...]
+
+
+def finish(me, arrived, panel, own, old, after):
     streams = len(own)
     _, rows, trace = own[0].shape
-    shots = rows * streams
-    return call(
-        lambda *refs: finish_kernel(*refs, streams=streams, width=width),
+    return call(
+        lambda *refs: finish_kernel(*refs, streams=streams),
         "finish",
         [(SMEM, me)] + [(VMEM, value) for value in (*arrived, *own, *old, *panel)],
-        [floats(2, shots, trace), floats(2, shots, width), floats(2, shots, width)],
-        [VMEM] * 3,
+        [floats(2, rows * streams, trace)] * 2,
+        [VMEM] * 2,
         after,
     )
 
@@ -376,7 +435,6 @@
         floats(1, forward.shape[-1]),
         VMEM,
         (),
-        4 * 10**9,
     )
 
 
@@ -483,16 +541,26 @@
     token = let[:1]
     for turn in range(1, hops + 1):
         token = stage_add(0, turn, token)
+    token = stage_join(1, token)
     up = halves(up_panel[0, 0], token)
     maps = halves(recovery[0, 0], [up[0]])
-    early = hold(me, 1, up_panel[0, 0], [maps[0]])
-    early_panel = hop(early, [(p + 1, p) for p in range(0, slabs - 2, 4)])
-    token = stage_join(1, [early])
-    token = stage_source(0, token)
-    state = list(cleave(base[0], streams, token))
-    token = [state[0]]
-    arrived = [hop(state[t], [(0, 1)]) for t in lanes]
-    for s in range(1, slabs):
+    held = hold(me, 3, up_panel[0, 0], [maps[0]])
+    far_panel = hop(held, [(p + 1, p) for p in range(2, slabs - 2, 2)])
+    token = stage_source(0, [held])
+    arrived = hop(base[0], [(0, 1)])
+    for turn in range(1, hops + 1):
+        token = stage_add(1, turn, token)
+    token = stage_join(2, token)
+    whole = step("down", me, 1, arrived, down, base[0], 0, base[0], token)
+    arrived = [hop(whole, [(1, 2)])] * streams
+    state = list(cleave(whole, streams, [whole]))
+    token = stage_source(1, state[:1])
+    for turn in range(1, hops + 1):
+        token = stage_add(2, turn, token)
+    held = hold(me, 1, up_panel[0, 0], token + arrived[:1])
+    near_panel = hop(held, [(1, 0)])
+    token = [held]
+    for s in range(2, slabs):
         number = s // 2 if s < 4 else s // 4 + 1
         for t in lanes:
             state[t] = step("down", me, s, arrived[t], down, base[number], t * rows, state[t], token)
@@ -500,44 +568,39 @@
         if s + 1 < slabs:
             arrived = [hop(state[t], [(s, s + 1)]) for t in lanes]
         else:
-            beside = [hop(state[t], [(p + 1, p) for p in range(0, slabs, 2)]) for t in lanes]
-        if s == 1:
-            for turn in range(1, hops + 1):
-                token = stage_add(1, turn, token)
+            arrived = [hop(state[t], [(s, s - 1)]) for t in lanes]
+            beside = [hop(state[t], [(p + 1, p) for p in range(0, slabs - 2, 2)]) for t in lanes]
         number = s // 4 + 2
         if number < len(sets):
             if s % 4 == 1:
                 token = stage_join(number, token)
-            if s % 4 == 2:
+            if s % 4 == 2 and s > 2:
                 for turn in range(1, hops + 1):
                     token = stage_add(number, turn, token)
             if s % 4 == 3:
                 token = stage_source(number, token)
-        if s == 1:
-            late = hold(me, 3, up_panel[0, 0], token)
-            late_panel = hop(late, [(p + 1, p) for p in range(2, slabs - 2, 4)])
-            token = stage_source(1, [late])
-    local = []
+    above = list(state)
     for t in lanes:
-        local.append(step("local", me, None, beside[t], up, state[t], 0, state[t], token))
-        token = [local[t]]
-    above = list(local)
+        above[t] = step("up", me, slabs - 2, arrived[t], up, state[t], 0, above[t], token)
+        token = [above[t]]
     arrived = [hop(above[t], [(slabs - 2, slabs - 4)]) for t in lanes]
-    pair = pair_panel(me, early_panel, late_panel, up, token, slabs - 2)
-    token = [pair[0]]
+    odd_up = halves_of_two(me, near_panel, far_panel, token)
+    token = [odd_up[0]]
     for p in range(slabs - 4, -1, -2):
         if p == 0:
             after = [hop(above[t], [(q + 2, q + 1) for q in range(0, slabs - 2, 2)]) for t in lanes]
         for t in lanes:
-            above[t] = step("up", me, p, arrived[t], pair, local[t], 0, above[t], token)
+            above[t] = up_step(
+                me, p, arrived[t], odd_up, beside[t], up, state[t], above[t], token
+            )
             token = [above[t]]
         if p > 0:
             arrived = [hop(above[t], [(p, p - 2)]) for t in lanes]
-    ups, head, tail = finish(me, after, up, state, above, width, token)
-
+    head, tail = edges(me, after, up, state, above, width, token)
     left = lax.ppermute(tail, "lat", [(i, i + 1) for i in range(lats - 1)])
     right = lax.ppermute(head, "lat", [(i + 1, i) for i in range(lats - 1)])
-    part = middle(ups, maps, forward_field[0, 0], width)
+    ups, field = finish(me, after, up, state, above, [head])
+    part = middle(field, maps, forward_field[0, 0], width)
     outgoing = rim(targets, part, left, right, maps, forward_field[0, 0], slabs)
     arrived = lax.all_to_all(outgoing, "slab", split_axis=0, concat_axis=0, tiled=True)
     model = jnp.sum(arrived.reshape(slabs, MBLK, width), axis=0)

time: 136 us -> 135 us (level)
  Pallas kernels: 19.9 us -> 16.4 us
  waiting for transfers between devices: 50.8 us -> 52.9 us
  starting transfers between devices: 49.4 us -> 50.8 us
    ppermute x1, starting transfers between devices: 9.42 us -> 13.3 us  [body(): left = lax.ppermute(tail, 'lat', [(i, i + 1) for i in range(lats - 1)])]
    pallas_call x45, Pallas kernels: 19.9 us -> 16.4 us  [call(): pl.pallas_call(run, in_specs=list(specs) + [ANY] * len(after), out_specs=...]
    ppermute x35, starting transfers between devices: 38 us -> 35.5 us  [hop(): return lax.ppermute(value, 'slab', route)]
    ppermute x35, waiting for transfers between devices: 49.1 us -> 51 us  [hop(): return lax.ppermute(value, 'slab', route)]
    unnamed x31 -> x29, local copies, waits for them, and re-layouts: 3.05 us -> 2.1 us
  transfers between devices with their start and end apart: 37 -> 37, of which waited for: 11 -> 11; matrix products, arithmetic and copies ran while one was open for 0% -> 0% of each run, Pallas kernels for 11% -> 9%
where the time goes in v4:
time: 135 us; the launch traced here: 134 us
  waiting for transfers between devices  52.9 us (39%)
  starting transfers between devices  50.8 us (38%)
  Pallas kernels  16.4 us (12%)
  blocking collectives  9.64 us (7%)
  local copies, waits for them, and re-layouts  2.1 us (2%)
  between operations  1.56 us (1%)
    ppermute x35, waiting for transfers between devices, hop(): return lax.ppermute(value, 'slab', route)  51 us
    ppermute x35, starting transfers between devices, hop(): return lax.ppermute(value, 'slab', route)  35.5 us
    pallas_call x45, Pallas kernels, call(): pl.pallas_call(run, in_specs=list(specs) + [ANY] * len(after), out_specs=...  16.4 us
    ppermute x1, starting transfers between devices, body(): left = lax.ppermute(tail, 'lat', [(i, i + 1) for i in range(lats - 1)])  13.3 us
    all_to_all x1, blocking collectives, body(): lax.all_to_all(outgoing, 'slab', split_axis=0, concat_axis=0, tiled=True)  9.64 us
  transfers between devices with their start and end apart: 37, of which 11 were waited for; matrix products, arithmetic and copies ran while one was open for 0% of the time, Pallas kernels for 9%

profile of v4, /device:TPU:1, one launch (start us, length us, event | category | flops | bytes accessed | tf_op | source)
XLA Modules:
  0.0 134.0 jit_solution(18351690890488642072)
XLA Ops:
  0.7 2.8 %collect.2 = (f32[1,2,64,512]{3,2,1,0:T(8,128)}, f32[1,2,64,512]{3,2,1,0:T(8,128)}) custom-call(s32[1]{0:T(128)} %bitcast.refs_0_, s32[32]{0:T(128)} %bitcast.21, s32[32]{0:T(128)} %refs_2_.5, f32[32,2,64,128]{3,2,1,0:T(8,128)} %refs_3_.4), custom_call_target="tpu_custom_call" | custom-call | flops 2000000000 | bytes 2000000 | tf_op jit(solution)/shard_map/collect/pallas_call | solution.py:46
  3.5 2.1 %collective-permute-start = (f32[1,2,64,512]{3,2,1,0:T(8,128)}, f32[1,2,64,512]{3,2,1,0:T(8,128)S(1)}, u32[]{:S(2)}, u32[]{:S(2)}) collective-permute-start(f32[1,2,64,512]{3,2,1,0:T(8,128)} %get-tuple-element.33), channel_id=1, source_target_pairs={{0,4},{4,0},{8,12},{12,8},{16,20},{20,16},{24,28},{28,24},{1,5},{5... | collective-permute-start | bytes 786440 | tf_op jit(solution)/shard_map/ppermute | solution.py:498
  5.7 0.9 copy-done.2
  6.7 1.6 %ready.1 = (f32[64,2]{1,0:T(8,128)S(1)}, s32[8]{0:T(128)S(1)}) custom-call(s32[64]{0:T(128)S(1)} %copy-done.4, s32[8]{0:T(128)S(1)} %bitcast.16, s32[8]{0:T(128)S(1)} %copy-done.6, f32[64,2]{1,0:T(8,128)S(1)} %copy.13.refs_3_, f32[1,2,64,512]{3,2,1,0:T(8,128)S(1)} %copy-done.2), custom_call_target="tpu_custom_call" | custom-call | tf_op jit(solution)/shard_map/ready/pallas_call | solution.py:46
  8.9 1.0 copy-done.8
  9.9 2.0 %collect.3 = (f32[1,2,64,512]{3,2,1,0:T(8,128)S(1)}, f32[1,2,64,512]{3,2,1,0:T(8,128)S(1)}, f32[2,2,64,512]{3,2,1,0:T(8,128)S(1)}, f32[2,2,64,512]{3,2,1,0:T(8,128)S(1)}) custom-call(s32[1]{0:T(128)} %bitcast.refs_0_, s32[32]{0:T(128)S(1)} %bitcast.22, s32[32]{0:T(128)S(1)} %copy-done.10, f32[32,2,64,128]{3,2,1,0:T(8,128)S(1)} %copy-done.8, ...), custom_call_target="tpu_custom_call" | custom-call | flops 2000000000 | bytes 2000000 | tf_op jit(solution)/shard_map/collect/pallas_call | solution.py:46
  12.0 1.4 %collective-permute-start.1 = (f32[2,64,512]{2,1,0:T(8,128)S(1)}, f32[2,64,512]{2,1,0:T(8,128)S(1)}, u32[]{:S(2)}, u32[]{:S(2)}) collective-permute-start(f32[2,64,512]{2,1,0:T(8,128)S(1)} %get-tuple-element.38), channel_id=1, source_target_pairs={{0,8},{4,12},{8,0},{12,4},{16,24},{20,28},{24,16},{28,20},{1,9},{5... | collective-permute-start | bytes 786440 | tf_op jit(solution)/shard_map/ppermute | solution.py:498
  13.5 1.1 collective-permute-start.3
  15.0 3.8 %collective-permute-done.1.refs_1_ = f32[2,64,512]{2,1,0:T(8,128)S(1)} collective-permute-done((f32[2,64,512]{2,1,0:T(8,128)S(1)}, f32[2,64,512]{2,1,0:T(8,128)S(1)}, u32[]{:S(2)}, u32[]{:S(2)}) %collective-permute-start.1) | collective-permute-done | bytes 262176 | tf_op jit(solution)/shard_map/ppermute | solution.py:498
  18.8 1.3 collective-permute-start.2
  20.2 2.4 %collective-permute-start.6 = (f32[2,64,512]{2,1,0:T(8,128)S(1)}, f32[2,64,512]{2,1,0:T(8,128)S(1)}, u32[]{:S(2)}, u32[]{:S(2)}) collective-permute-start(f32[2,64,512]{2,1,0:T(8,128)S(1)} %get-tuple-element.48), channel_id=1, source_target_pairs={{0,8},{4,12},{16,24},{20,28},{1,9},{5,13},{17,25},{21,29},{2,10},{... | collective-permute-start | bytes 786440 | tf_op jit(solution)/shard_map/ppermute | solution.py:498
  23.2 1.6 %halves.6 = (bf16[768,2048]{1,0:T(8,128)(2,1)S(1)}, bf16[768,2048]{1,0:T(8,128)(2,1)S(1)}) custom-call(f32[2,768,1024]{2,1,0:T(8,128)S(1)} %bitcast.19, bf16[512,1024]{1,0:T(8,128)(2,1)S(1)} %get-tuple-element.43.refs_1_.refs_2_.refs_5_.refs_7_), custom_call_target="tpu_custom_call" | custom-call | flops 2000000000 | bytes 2000000 | tf_op jit(solution)/shard_map/halves/pallas_call | solution.py:46
  24.9 2.5 %collective-permute-done.2.refs_1_ = f32[2,64,512]{2,1,0:T(8,128)S(1)} collective-permute-done((f32[2,64,512]{2,1,0:T(8,128)S(1)}, f32[2,64,512]{2,1,0:T(8,128)S(1)}, u32[]{:S(2)}, u32[]{:S(2)}) %collective-permute-start.2) | collective-permute-done | bytes 262176 | tf_op jit(solution)/shard_map/ppermute | solution.py:498
  27.5 1.9 %collective-permute-start.4 = (f32[2,64,512]{2,1,0:T(8,128)S(1)}, f32[2,64,512]{2,1,0:T(8,128)S(1)}, u32[]{:S(2)}, u32[]{:S(2)}) collective-permute-start(f32[2,64,512]{2,1,0:T(8,128)S(1)} %source.3.refs_2_.refs_4_.refs_5_), channel_id=1, source_target_pairs={{0,4},{1,5},{2,6},{3,7}} | collective-permute-start | bytes 786440 | tf_op jit(solution)/shard_map/ppermute | solution.py:498
  29.5 0.7 collective-permute-start.8
  30.2 0.8 collective-permute-done.5.refs_1_
  31.5 4.0 %collective-permute-done.4.refs_1_ = f32[2,64,512]{2,1,0:T(8,128)S(1)} collective-permute-done((f32[2,64,512]{2,1,0:T(8,128)S(1)}, f32[2,64,512]{2,1,0:T(8,128)S(1)}, u32[]{:S(2)}, u32[]{:S(2)}) %collective-permute-start.4) | collective-permute-done | bytes 262176 | tf_op jit(solution)/shard_map/ppermute | solution.py:498
  35.5 0.7 collective-permute-start.7
  36.2 0.8 collective-permute-start.24
  37.2 1.3 collective-permute-start.23
  38.5 3.8 %collective-permute-start.12 = (f32[2,64,512]{2,1,0:T(8,128)S(1)}, f32[2,64,512]{2,1,0:T(8,128)S(1)}, u32[]{:S(2)}, u32[]{:S(2)}) collective-permute-start(f32[2,64,512]{2,1,0:T(8,128)S(1)} %add.5.refs_2_.refs_0_), channel_id=1, source_target_pairs={{0,16},{4,20},{8,24},{12,28},{1,17},{5,21},{9,25},{13,29},{2,18},{... | collective-permute-start | bytes 786440 | tf_op jit(solution)/shard_map/ppermute | solution.py:498
  42.3 0.7 collective-permute-start.10
  43.0 0.7 collective-permute-start.13
  43.7 0.7 collective-permute-start.11
  44.4 0.7 collective-permute-start.15
  45.7 0.7 collective-permute-start.14
  47.9 0.7 collective-permute-start.19
  48.6 0.7 collective-permute-start.18
  51.4 1.3 collective-permute-start.26
  53.4 1.3 collective-permute-start.29
  54.8 0.7 collective-permute-start.28
  55.4 32.2 %collective-permute-done.23.refs_1_ = f32[2,512,512]{2,1,0:T(8,128)S(1)} collective-permute-done((f32[2,512,512]{2,1,0:T(8,128)S(1)}, f32[2,512,512]{2,1,0:T(8,128)S(1)}, u32[]{:S(2)}, u32[]{:S(2)}) %collective-permute-start.23) | collective-permute-done | bytes 2097184 | tf_op jit(solution)/shard_map/ppermute | solution.py:498
  87.6 0.7 halves.7
  88.3 2.1 %collective-permute-done.26.refs_4_ = f32[2,32,512]{2,1,0:T(8,128)S(1)} collective-permute-done((f32[2,32,512]{2,1,0:T(8,128)S(1)}, f32[2,32,512]{2,1,0:T(8,128)S(1)}, u32[]{:S(2)}, u32[]{:S(2)}) %collective-permute-start.26) | collective-permute-done | bytes 131104 | tf_op jit(solution)/shard_map/ppermute | solution.py:498
  91.1 2.1 %collective-permute-done.29.refs_4_ = f32[2,32,512]{2,1,0:T(8,128)S(1)} collective-permute-done((f32[2,32,512]{2,1,0:T(8,128)S(1)}, f32[2,32,512]{2,1,0:T(8,128)S(1)}, u32[]{:S(2)}, u32[]{:S(2)}) %collective-permute-start.29) | collective-permute-done | bytes 131104 | tf_op jit(solution)/shard_map/ppermute | solution.py:498
  94.0 1.3 collective-permute-start.33
  95.3 1.3 collective-permute-start.34
  97.9 1.7 %collective-permute-done.33.refs_1_ = f32[2,32,512]{2,1,0:T(8,128)S(1)} collective-permute-done((f32[2,32,512]{2,1,0:T(8,128)S(1)}, f32[2,32,512]{2,1,0:T(8,128)S(1)}, u32[]{:S(2)}, u32[]{:S(2)}) %collective-permute-start.33) | collective-permute-done | bytes 131104 | tf_op jit(solution)/shard_map/ppermute | solution.py:498
  99.7 1.3 up.14.refs_9_.refs_5_
  101.0 1.3 collective-permute-done.34.refs_1_
  102.3 1.3 up.15.refs_6_.refs_9_
  103.7 13.3 %collective-permute-start.35 = (f32[2,64,128]{2,1,0:T(8,128)S(1)}, f32[2,64,128]{2,1,0:T(8,128)S(1)}, u32[]{:S(2)}, u32[]{:S(2)}) collective-permute-start(f32[2,64,128]{2,1,0:T(8,128)S(1)} %get-tuple-element.61), channel_id=1, source_target_pairs={{0,1},{1,2},{2,3},{4,5},{5,6},{6,7},{8,9},{9,10},{10,11},{12,13},{... | collective-permute-start | bytes 196616 | tf_op jit(solution)/shard_map/ppermute | solution.py:600
  117.0 1.9 %collective-permute-start.36 = (f32[2,64,128]{2,1,0:T(8,128)S(1)}, f32[2,64,128]{2,1,0:T(8,128)S(1)}, u32[]{:S(2)}, u32[]{:S(2)}) collective-permute-start(f32[2,64,128]{2,1,0:T(8,128)S(1)} %get-tuple-element.56.refs_9_), channel_id=1, source_target_pairs={{1,0},{2,1},{3,2},{5,4},{6,5},{7,6},{9,8},{10,9},{11,10},{13,12},{... | collective-permute-start | bytes 196616 | tf_op jit(solution)/shard_map/ppermute | solution.py:601
  119.0 0.7 finish.1
  119.7 1.0 middle.1.refs_1_
  120.7 1.9 %collective-permute-done.36.refs_3_ = f32[2,64,128]{2,1,0:T(8,128)S(1)} collective-permute-done((f32[2,64,128]{2,1,0:T(8,128)S(1)}, f32[2,64,128]{2,1,0:T(8,128)S(1)}, u32[]{:S(2)}, u32[]{:S(2)}) %collective-permute-start.36) | collective-permute-done | bytes 65568 | tf_op jit(solution)/shard_map/ppermute | solution.py:601
  122.6 1.2 rim.1
  123.8 9.6 %all_to_all.9 = f32[8,8,128]{2,1,0:T(8,128)S(1)} all-to-all(f32[8,8,128]{2,1,0:T(8,128)S(1)} %bitcast.15), channel_id=1, replica_groups=mesh['slab'=8,'lat'=4] {'slab'}, dimensions={0} | all-to-all | bytes 65536 | tf_op jit(solution)/shard_map/all_to_all | solution.py:605
  (103 shorter events, 11.0 us)
Async XLA Ops:
  0.6 5.0 %copy-start.11 = (f32[64,2]{0,1:T(2,128)S(1)}, f32[64,2]{0,1:T(2,128)}, u32[]{:S(2)}) copy-start(f32[64,2]{0,1:T(2,128)} %param.15) | copy-start | bytes 1540
  0.6 5.1 %copy-start.4 = (s32[64]{0:T(128)S(1)}, s32[64]{0:T(128)}, u32[]{:S(2)}) copy-start(s32[64]{0:T(128)} %refs_0_.1) | copy-start | bytes 772
  0.7 5.1 %copy-start.5 = (s32[8,1]{0,1:T(1,128)S(1)}, s32[8,1]{0,1:T(1,128)}, u32[]{:S(2)}) copy-start(s32[8,1]{0,1:T(1,128)} %param.20) | copy-start | bytes 100
  0.7 5.1 %copy-start.6 = (s32[8]{0:T(128)S(1)}, s32[8]{0:T(128)}, u32[]{:S(2)}) copy-start(s32[8]{0:T(128)} %refs_2_.4) | copy-start | bytes 100
  0.7 7.6 %copy-start.7 = (f32[1,1,2,512,512]{4,3,2,1,0:T(8,128)S(1)}, f32[1,1,2,512,512]{4,3,2,1,0:T(8,128)}, u32[]{:S(2)}) copy-start(f32[1,1,2,512,512]{4,3,2,1,0:T(8,128)} %param.16) | copy-start | bytes 6291460
  3.5 8.5 %collective-permute-start = (f32[1,2,64,512]{3,2,1,0:T(8,128)}, f32[1,2,64,512]{3,2,1,0:T(8,128)S(1)}, u32[]{:S(2)}, u32[]{:S(2)}) collective-permute-start(f32[1,2,64,512]{3,2,1,0:T(8,128)} %get-tuple-element.33), channel_id=1, source_target_pairs={{0,4},{4,0},{8,12},{12,8},{16,20},{20,16},{24,28},{28,24},{1,5},{5... | collective-permute-start | bytes 786440 | tf_op jit(solution)/shard_map/ppermute | solution.py:498
  8.3 1.6 %copy-start.8 = (f32[32,2,64,128]{3,2,1,0:T(8,128)S(1)}, f32[32,2,64,128]{3,2,1,0:T(8,128)}, u32[]{:S(2)}) copy-start(f32[32,2,64,128]{3,2,1,0:T(8,128)} %refs_3_.4) | copy-start | bytes 6291460
  9.9 2.1 %copy-start.3 = (f32[1,2,64,512]{3,2,1,0:T(8,128)S(1)}, f32[1,2,64,512]{3,2,1,0:T(8,128)}, u32[]{:S(2)}) copy-start(f32[1,2,64,512]{3,2,1,0:T(8,128)} %get-tuple-element.32.refs_4_.refs_0_) | copy-start | bytes 786436
  9.9 13.3 %slice-start = ((s8[6291456]{0:T(1024)(128)(4,1)}), s8[4194304]{0:T(1024)(128)(4,1)S(1)}, s32[]{:S(2)}) async-start(s8[6291456]{0:T(1024)(128)(4,1)} %bitcast.17), calls=%async_computation.1 | async-start | bytes 8388608
  11.9 10.7 %copy-start = (f32[1,1,2,512,512]{4,3,2,1,0:T(8,128)S(1)}, f32[1,1,2,512,512]{4,3,2,1,0:T(8,128)}, u32[]{:S(2)}) copy-start(f32[1,1,2,512,512]{4,3,2,1,0:T(8,128)} %param.17) | copy-start | bytes 6291460
  12.0 6.8 %collective-permute-start.1 = (f32[2,64,512]{2,1,0:T(8,128)S(1)}, f32[2,64,512]{2,1,0:T(8,128)S(1)}, u32[]{:S(2)}, u32[]{:S(2)}) collective-permute-start(f32[2,64,512]{2,1,0:T(8,128)S(1)} %get-tuple-element.38), channel_id=1, source_target_pairs={{0,8},{4,12},{8,0},{12,4},{16,24},{20,28},{24,16},{28,20},{1,9},{5... | collective-permute-start | bytes 786440 | tf_op jit(solution)/shard_map/ppermute | solution.py:498
  13.5 9.7 %slice-start.1 = ((s8[6291456]{0:T(1024)(128)(4,1)}), s8[2097152]{0:T(1024)(128)(4,1)S(1)}, s32[]{:S(2)}) async-start(s8[6291456]{0:T(1024)(128)(4,1)} %bitcast.17), calls=%async_computation.2 | async-start | bytes 4194304
  13.5 6.6 %collective-permute-start.3 = (f32[1,2,64,512]{3,2,1,0:T(8,128)S(1)}, f32[1,2,64,512]{3,2,1,0:T(8,128)S(1)}, u32[]{:S(2)}, u32[]{:S(2)}) collective-permute-start(f32[1,2,64,512]{3,2,1,0:T(8,128)S(1)} %get-tuple-element.41.refs_2_), channel_id=1, source_target_pairs={{0,4},{4,0},{8,12},{12,8},{16,20},{20,16},{24,28},{28,24},{1,5},{5... | collective-permute-start | bytes 786440 | tf_op jit(solution)/shard_map/ppermute | solution.py:498
  14.6 16.4 %collective-permute-start.5 = (f32[2,2,64,512]{3,2,1,0:T(8,128)S(1)}, f32[2,2,64,512]{3,2,1,0:T(8,128)S(1)}, u32[]{:S(2)}, u32[]{:S(2)}) collective-permute-start(f32[2,2,64,512]{3,2,1,0:T(8,128)S(1)} %get-tuple-element.47), channel_id=1, source_target_pairs={{0,4},{4,0},{8,12},{12,8},{16,20},{20,16},{24,28},{28,24},{1,5},{5... | collective-permute-start | bytes 1572872 | tf_op jit(solution)/shard_map/ppermute | solution.py:498
  18.8 8.6 %collective-permute-start.2 = (f32[2,64,512]{2,1,0:T(8,128)S(1)}, f32[2,64,512]{2,1,0:T(8,128)S(1)}, u32[]{:S(2)}, u32[]{:S(2)}) collective-permute-start(f32[2,64,512]{2,1,0:T(8,128)S(1)} %add.3.refs_2_.refs_0_), channel_id=1, source_target_pairs={{16,0},{20,4},{17,1},{21,5},{18,2},{22,6},{19,3},{23,7}} | collective-permute-start | bytes 786440 | tf_op jit(solution)/shard_map/ppermute | solution.py:498
  20.2 9.3 %collective-permute-start.6 = (f32[2,64,512]{2,1,0:T(8,128)S(1)}, f32[2,64,512]{2,1,0:T(8,128)S(1)}, u32[]{:S(2)}, u32[]{:S(2)}) collective-permute-start(f32[2,64,512]{2,1,0:T(8,128)S(1)} %get-tuple-element.48), channel_id=1, source_target_pairs={{0,8},{4,12},{16,24},{20,28},{1,9},{5,13},{17,25},{21,29},{2,10},{... | collective-permute-start | bytes 786440 | tf_op jit(solution)/shard_map/ppermute | solution.py:498
  27.5 8.0 %collective-permute-start.4 = (f32[2,64,512]{2,1,0:T(8,128)S(1)}, f32[2,64,512]{2,1,0:T(8,128)S(1)}, u32[]{:S(2)}, u32[]{:S(2)}) collective-permute-start(f32[2,64,512]{2,1,0:T(8,128)S(1)} %source.3.refs_2_.refs_4_.refs_5_), channel_id=1, source_target_pairs={{0,4},{1,5},{2,6},{3,7}} | collective-permute-start | bytes 786440 | tf_op jit(solution)/shard_map/ppermute | solution.py:498
  29.5 7.5 %collective-permute-start.8 = (f32[2,64,512]{2,1,0:T(8,128)S(1)}, f32[2,64,512]{2,1,0:T(8,128)S(1)}, u32[]{:S(2)}, u32[]{:S(2)}) collective-permute-start(f32[2,64,512]{2,1,0:T(8,128)S(1)} %add.4.refs_2_.refs_0_), channel_id=1, source_target_pairs={{24,8},{28,12},{25,9},{29,13},{26,10},{30,14},{27,11},{31,15}} | collective-permute-start | bytes 786440 | tf_op jit(solution)/shard_map/ppermute | solution.py:498
  31.0 6.1 %collective-permute-start.9 = (f32[2,64,512]{2,1,0:T(8,128)S(1)}, f32[2,64,512]{2,1,0:T(8,128)S(1)}, u32[]{:S(2)}, u32[]{:S(2)}) collective-permute-start(f32[2,64,512]{2,1,0:T(8,128)S(1)} %get-tuple-element.51), channel_id=1, source_target_pairs={{0,8},{4,12},{8,0},{12,4},{16,24},{20,28},{24,16},{28,20},{1,9},{5... | collective-permute-start | bytes 786440 | tf_op jit(solution)/shard_map/ppermute | solution.py:498
  35.5 1.7 %collective-permute-start.7 = (f32[2,64,512]{2,1,0:T(8,128)S(1)}, f32[2,64,512]{2,1,0:T(8,128)S(1)}, u32[]{:S(2)}, u32[]{:S(2)}) collective-permute-start(f32[2,64,512]{2,1,0:T(8,128)S(1)} %down.13.refs_0_.refs_1_), channel_id=1, source_target_pairs={{4,8},{5,9},{6,10},{7,11}} | collective-permute-start | bytes 786440 | tf_op jit(solution)/shard_map/ppermute | solution.py:498
  36.2 18.6 %collective-permute-start.24 = (f32[2,512,512]{2,1,0:T(8,128)S(1)}, f32[2,512,512]{2,1,0:T(8,128)S(1)}, u32[]{:S(2)}, u32[]{:S(2)}) collective-permute-start(f32[2,512,512]{2,1,0:T(8,128)S(1)} %hold.2.refs_3_), channel_id=1, source_target_pairs={{12,8},{20,16},{13,9},{21,17},{14,10},{22,18},{15,11},{23,19}} | collective-permute-start | bytes 6291464 | tf_op jit(solution)/shard_map/ppermute | solution.py:498
  37.2 50.4 %collective-permute-start.23 = (f32[2,512,512]{2,1,0:T(8,128)S(1)}, f32[2,512,512]{2,1,0:T(8,128)S(1)}, u32[]{:S(2)}, u32[]{:S(2)}) collective-permute-start(f32[2,512,512]{2,1,0:T(8,128)S(1)} %hold.3.refs_6_), channel_id=1, source_target_pairs={{4,0},{5,1},{6,2},{7,3}} | collective-permute-start | bytes 6291464 | tf_op jit(solution)/shard_map/ppermute | solution.py:498
  38.5 7.1 %collective-permute-start.12 = (f32[2,64,512]{2,1,0:T(8,128)S(1)}, f32[2,64,512]{2,1,0:T(8,128)S(1)}, u32[]{:S(2)}, u32[]{:S(2)}) collective-permute-start(f32[2,64,512]{2,1,0:T(8,128)S(1)} %add.5.refs_2_.refs_0_), channel_id=1, source_target_pairs={{0,16},{4,20},{8,24},{12,28},{1,17},{5,21},{9,25},{13,29},{2,18},{... | collective-permute-start | bytes 786440 | tf_op jit(solution)/shard_map/ppermute | solution.py:498
  42.3 1.4 %collective-permute-start.10 = (f32[2,32,512]{2,1,0:T(8,128)S(1)}, f32[2,32,512]{2,1,0:T(8,128)S(1)}, u32[]{:S(2)}, u32[]{:S(2)}) collective-permute-start(f32[2,32,512]{2,1,0:T(8,128)S(1)} %down.14.refs_6_.refs_5_), channel_id=1, source_target_pairs={{8,12},{9,13},{10,14},{11,15}} | collective-permute-start | bytes 393224 | tf_op jit(solution)/shard_map/ppermute | solution.py:498
  43.0 1.4 %collective-permute-start.13 = (f32[2,32,512]{2,1,0:T(8,128)S(1)}, f32[2,32,512]{2,1,0:T(8,128)S(1)}, u32[]{:S(2)}, u32[]{:S(2)}) collective-permute-start(f32[2,32,512]{2,1,0:T(8,128)S(1)} %down.15.refs_6_.refs_5_), channel_id=1, source_target_pairs={{8,12},{9,13},{10,14},{11,15}} | collective-permute-start | bytes 393224 | tf_op jit(solution)/shard_map/ppermute | solution.py:498
  43.7 1.9 %collective-permute-start.11 = (f32[2,32,512]{2,1,0:T(8,128)S(1)}, f32[2,32,512]{2,1,0:T(8,128)S(1)}, u32[]{:S(2)}, u32[]{:S(2)}) collective-permute-start(f32[2,32,512]{2,1,0:T(8,128)S(1)} %down.16.refs_6_.refs_5_), channel_id=1, source_target_pairs={{12,16},{13,17},{14,18},{15,19}} | collective-permute-start | bytes 393224 | tf_op jit(solution)/shard_map/ppermute | solution.py:498
  44.4 1.9 %collective-permute-start.15 = (f32[2,32,512]{2,1,0:T(8,128)S(1)}, f32[2,32,512]{2,1,0:T(8,128)S(1)}, u32[]{:S(2)}, u32[]{:S(2)}) collective-permute-start(f32[2,32,512]{2,1,0:T(8,128)S(1)} %down.17.refs_3_.refs_5_), channel_id=1, source_target_pairs={{12,16},{13,17},{14,18},{15,19}} | collective-permute-start | bytes 393224 | tf_op jit(solution)/shard_map/ppermute | solution.py:498
  45.7 1.4 %collective-permute-start.14 = (f32[2,32,512]{2,1,0:T(8,128)S(1)}, f32[2,32,512]{2,1,0:T(8,128)S(1)}, u32[]{:S(2)}, u32[]{:S(2)}) collective-permute-start(f32[2,32,512]{2,1,0:T(8,128)S(1)} %down.18.refs_6_.refs_5_), channel_id=1, source_target_pairs={{16,20},{17,21},{18,22},{19,23}} | collective-permute-start | bytes 393224 | tf_op jit(solution)/shard_map/ppermute | solution.py:498
  46.4 1.4 %collective-permute-start.17 = (f32[2,32,512]{2,1,0:T(8,128)S(1)}, f32[2,32,512]{2,1,0:T(8,128)S(1)}, u32[]{:S(2)}, u32[]{:S(2)}) collective-permute-start(f32[2,32,512]{2,1,0:T(8,128)S(1)} %down.19.refs_6_.refs_5_), channel_id=1, source_target_pairs={{16,20},{17,21},{18,22},{19,23}} | collective-permute-start | bytes 393224 | tf_op jit(solution)/shard_map/ppermute | solution.py:498
  47.1 1.4 %collective-permute-start.16 = (f32[2,32,512]{2,1,0:T(8,128)S(1)}, f32[2,32,512]{2,1,0:T(8,128)S(1)}, u32[]{:S(2)}, u32[]{:S(2)}) collective-permute-start(f32[2,32,512]{2,1,0:T(8,128)S(1)} %down.20.refs_6_.refs_5_), channel_id=1, source_target_pairs={{20,24},{21,25},{22,26},{23,27}} | collective-permute-start | bytes 393224 | tf_op jit(solution)/shard_map/ppermute | solution.py:498
  47.9 1.4 %collective-permute-start.19 = (f32[2,32,512]{2,1,0:T(8,128)S(1)}, f32[2,32,512]{2,1,0:T(8,128)S(1)}, u32[]{:S(2)}, u32[]{:S(2)}) collective-permute-start(f32[2,32,512]{2,1,0:T(8,128)S(1)} %down.21.refs_6_.refs_5_), channel_id=1, source_target_pairs={{20,24},{21,25},{22,26},{23,27}} | collective-permute-start | bytes 393224 | tf_op jit(solution)/shard_map/ppermute | solution.py:498
  48.6 1.4 %collective-permute-start.18 = (f32[2,32,512]{2,1,0:T(8,128)S(1)}, f32[2,32,512]{2,1,0:T(8,128)S(1)}, u32[]{:S(2)}, u32[]{:S(2)}) collective-permute-start(f32[2,32,512]{2,1,0:T(8,128)S(1)} %down.22.refs_6_.refs_5_), channel_id=1, source_target_pairs={{24,28},{25,29},{26,30},{27,31}} | collective-permute-start | bytes 393224 | tf_op jit(solution)/shard_map/ppermute | solution.py:498
  49.3 1.4 %collective-permute-start.21 = (f32[2,32,512]{2,1,0:T(8,128)S(1)}, f32[2,32,512]{2,1,0:T(8,128)S(1)}, u32[]{:S(2)}, u32[]{:S(2)}) collective-permute-start(f32[2,32,512]{2,1,0:T(8,128)S(1)} %down.23.refs_6_.refs_5_), channel_id=1, source_target_pairs={{24,28},{25,29},{26,30},{27,31}} | collective-permute-start | bytes 393224 | tf_op jit(solution)/shard_map/ppermute | solution.py:498
  50.0 2.7 %collective-permute-start.20 = (f32[2,32,512]{2,1,0:T(8,128)S(1)}, f32[2,32,512]{2,1,0:T(8,128)S(1)}, u32[]{:S(2)}, u32[]{:S(2)}) collective-permute-start(f32[2,32,512]{2,1,0:T(8,128)S(1)} %down.24.refs_6_.refs_4_.refs_5_.refs_7_.refs_3_), channel_id=1, source_target_pairs={{28,24},{29,25},{30,26},{31,27}} | collective-permute-start | bytes 393224 | tf_op jit(solution)/shard_map/ppermute | solution.py:498
  50.7 2.7 %collective-permute-start.25 = (f32[2,32,512]{2,1,0:T(8,128)S(1)}, f32[2,32,512]{2,1,0:T(8,128)S(1)}, u32[]{:S(2)}, u32[]{:S(2)}) collective-permute-start(f32[2,32,512]{2,1,0:T(8,128)S(1)} %down.25.refs_6_.refs_4_.refs_5_.refs_7_), channel_id=1, source_target_pairs={{28,24},{29,25},{30,26},{31,27}} | collective-permute-start | bytes 393224 | tf_op jit(solution)/shard_map/ppermute | solution.py:498
  51.4 39.0 %collective-permute-start.26 = (f32[2,32,512]{2,1,0:T(8,128)S(1)}, f32[2,32,512]{2,1,0:T(8,128)S(1)}, u32[]{:S(2)}, u32[]{:S(2)}) collective-permute-start(f32[2,32,512]{2,1,0:T(8,128)S(1)} %down.24.refs_6_.refs_4_.refs_5_.refs_7_.refs_3_), channel_id=1, source_target_pairs={{4,0},{12,8},{20,16},{5,1},{13,9},{21,17},{6,2},{14,10},{22,18},{7... | collective-permute-start | bytes 393224 | tf_op jit(solution)/shard_map/ppermute | solution.py:498
  52.7 37.7 %collective-permute-start.22 = (f32[2,32,512]{2,1,0:T(8,128)S(1)}, f32[2,32,512]{2,1,0:T(8,128)S(1)}, u32[]{:S(2)}, u32[]{:S(2)}) collective-permute-start(f32[2,32,512]{2,1,0:T(8,128)S(1)} %up.8.refs_6_.refs_8_), channel_id=1, source_target_pairs={{24,16},{25,17},{26,18},{27,19}} | collective-permute-start | bytes 393224 | tf_op jit(solution)/shard_map/ppermute | solution.py:498
  53.4 39.8 %collective-permute-start.29 = (f32[2,32,512]{2,1,0:T(8,128)S(1)}, f32[2,32,512]{2,1,0:T(8,128)S(1)}, u32[]{:S(2)}, u32[]{:S(2)}) collective-permute-start(f32[2,32,512]{2,1,0:T(8,128)S(1)} %down.25.refs_6_.refs_4_.refs_5_.refs_7_), channel_id=1, source_target_pairs={{4,0},{12,8},{20,16},{5,1},{13,9},{21,17},{6,2},{14,10},{22,18},{7... | collective-permute-start | bytes 393224 | tf_op jit(solution)/shard_map/ppermute | solution.py:498
  54.8 38.5 %collective-permute-start.28 = (f32[2,32,512]{2,1,0:T(8,128)S(1)}, f32[2,32,512]{2,1,0:T(8,128)S(1)}, u32[]{:S(2)}, u32[]{:S(2)}) collective-permute-start(f32[2,32,512]{2,1,0:T(8,128)S(1)} %up.9.refs_3_.refs_8_), channel_id=1, source_target_pairs={{24,16},{25,17},{26,18},{27,19}} | collective-permute-start | bytes 393224 | tf_op jit(solution)/shard_map/ppermute | solution.py:498
  90.4 3.5 %collective-permute-start.27 = (f32[2,32,512]{2,1,0:T(8,128)S(1)}, f32[2,32,512]{2,1,0:T(8,128)S(1)}, u32[]{:S(2)}, u32[]{:S(2)}) collective-permute-start(f32[2,32,512]{2,1,0:T(8,128)S(1)} %up.10.refs_9_.refs_8_), channel_id=1, source_target_pairs={{16,8},{17,9},{18,10},{19,11}} | collective-permute-start | bytes 393224 | tf_op jit(solution)/shard_map/ppermute | solution.py:498
  93.2 2.0 %collective-permute-start.31 = (f32[2,32,512]{2,1,0:T(8,128)S(1)}, f32[2,32,512]{2,1,0:T(8,128)S(1)}, u32[]{:S(2)}, u32[]{:S(2)}) collective-permute-start(f32[2,32,512]{2,1,0:T(8,128)S(1)} %up.11.refs_9_.refs_8_), channel_id=1, source_target_pairs={{16,8},{17,9},{18,10},{19,11}} | collective-permute-start | bytes 393224 | tf_op jit(solution)/shard_map/ppermute | solution.py:498
  94.0 5.7 %collective-permute-start.33 = (f32[2,32,512]{2,1,0:T(8,128)S(1)}, f32[2,32,512]{2,1,0:T(8,128)S(1)}, u32[]{:S(2)}, u32[]{:S(2)}) collective-permute-start(f32[2,32,512]{2,1,0:T(8,128)S(1)} %up.12.refs_9_.refs_8_), channel_id=1, source_target_pairs={{8,0},{9,1},{10,2},{11,3}} | collective-permute-start | bytes 393224 | tf_op jit(solution)/shard_map/ppermute | solution.py:498
  95.3 7.0 %collective-permute-start.34 = (f32[2,32,512]{2,1,0:T(8,128)S(1)}, f32[2,32,512]{2,1,0:T(8,128)S(1)}, u32[]{:S(2)}, u32[]{:S(2)}) collective-permute-start(f32[2,32,512]{2,1,0:T(8,128)S(1)} %up.13.refs_9_.refs_8_), channel_id=1, source_target_pairs={{8,0},{9,1},{10,2},{11,3}} | collective-permute-start | bytes 393224 | tf_op jit(solution)/shard_map/ppermute | solution.py:498
  96.6 7.0 %collective-permute-start.32 = (f32[2,32,512]{2,1,0:T(8,128)S(1)}, f32[2,32,512]{2,1,0:T(8,128)S(1)}, u32[]{:S(2)}, u32[]{:S(2)}) collective-permute-start(f32[2,32,512]{2,1,0:T(8,128)S(1)} %up.13.refs_9_.refs_8_), channel_id=1, source_target_pairs={{8,4},{16,12},{24,20},{9,5},{17,13},{25,21},{10,6},{18,14},{26,22}... | collective-permute-start | bytes 393224 | tf_op jit(solution)/shard_map/ppermute | solution.py:498
  97.3 6.4 %collective-permute-start.30 = (f32[2,32,512]{2,1,0:T(8,128)S(1)}, f32[2,32,512]{2,1,0:T(8,128)S(1)}, u32[]{:S(2)}, u32[]{:S(2)}) collective-permute-start(f32[2,32,512]{2,1,0:T(8,128)S(1)} %up.12.refs_9_.refs_8_), channel_id=1, source_target_pairs={{8,4},{16,12},{24,20},{9,5},{17,13},{25,21},{10,6},{18,14},{26,22}... | collective-permute-start | bytes 393224 | tf_op jit(solution)/shard_map/ppermute | solution.py:498
  103.7 16.0 %copy-start.1 = (f32[1,1,2,64,1024]{4,3,2,1,0:T(8,128)S(1)}, f32[1,1,2,64,1024]{4,3,2,1,0:T(8,128)}, u32[]{:S(2)}) copy-start(f32[1,1,2,64,1024]{4,3,2,1,0:T(8,128)} %param.19) | copy-start | bytes 1572868
  103.7 17.0 %collective-permute-start.35 = (f32[2,64,128]{2,1,0:T(8,128)S(1)}, f32[2,64,128]{2,1,0:T(8,128)S(1)}, u32[]{:S(2)}, u32[]{:S(2)}) collective-permute-start(f32[2,64,128]{2,1,0:T(8,128)S(1)} %get-tuple-element.61), channel_id=1, source_target_pairs={{0,1},{1,2},{2,3},{4,5},{5,6},{6,7},{8,9},{9,10},{10,11},{12,13},{... | collective-permute-start | bytes 196616 | tf_op jit(solution)/shard_map/ppermute | solution.py:600
  117.0 5.6 %collective-permute-start.36 = (f32[2,64,128]{2,1,0:T(8,128)S(1)}, f32[2,64,128]{2,1,0:T(8,128)S(1)}, u32[]{:S(2)}, u32[]{:S(2)}) collective-permute-start(f32[2,64,128]{2,1,0:T(8,128)S(1)} %get-tuple-element.56.refs_9_), channel_id=1, source_target_pairs={{1,0},{2,1},{3,2},{5,4},{6,5},{7,6},{9,8},{10,9},{11,10},{13,12},{... | collective-permute-start | bytes 196616 | tf_op jit(solution)/shard_map/ppermute | solution.py:601
  (3 other events, 4.1 us)

commit v5 on v4

--- a/solution.py
+++ b/solution.py
@@ -438,15 +438,40 @@
     )
 
 
+def frame_kernel(high_ref, low_ref, high_out, low_out):
+    width = high_out.shape[0] // 2
+    depth = high_ref.shape[0]
+    for ref, out in ((high_ref, high_out), (low_ref, low_out)):
+        out[:width] = ref[:width]
+        out[width:] = ref[depth - width :]
+
+
+def frame(maps, width, after):
+    shape = jax.ShapeDtypeStruct((2 * width, maps[0].shape[1]), jnp.bfloat16)
+    return call(
+        frame_kernel,
+        "frame",
+        [(VMEM, maps[0]), (VMEM, maps[1])],
+        [shape] * 2,
+        [VMEM] * 2,
+        after,
+    )
+
+
+def model_kernel(arrived_ref, out_ref):
+    out_ref[...] = jnp.sum(arrived_ref[...], axis=0)
+
+
+def model_rows(arrived):
+    return call(
+        model_kernel, "model", [(VMEM, arrived)], floats(*arrived.shape[1:]), VMEM, ()
+    )
+
+
 def rim_kernel(rows_ref, part_ref, left_ref, right_ref, high_ref, low_ref, forward_ref, out_ref):
     shots, width = left_ref.shape[1], left_ref.shape[2]
-    depth = high_ref.shape[0]
-
-    def ends(ref):
-        return jnp.concatenate([ref[:width], ref[depth - width :]], axis=0)
-
     field = jnp.concatenate([left_ref[...], right_ref[...]], axis=-1)
-    real, imag = product(field, ends(high_ref), ends(low_ref))
+    real, imag = product(field, high_ref[...], low_ref[...])
     total = forward_ref[0] * real + forward_ref[1] * imag
     gradient = part_ref[...] + jnp.sum(total, axis=0, keepdims=True)
     gradient = gradient * shots ** (-0.5)
@@ -544,7 +569,8 @@
     token = stage_join(1, token)
     up = halves(up_panel[0, 0], token)
     maps = halves(recovery[0, 0], [up[0]])
-    held = hold(me, 3, up_panel[0, 0], [maps[0]])
+    rims = frame(maps, width, [])
+    held = hold(me, 3, up_panel[0, 0], [rims[0]])
     far_panel = hop(held, [(p + 1, p) for p in range(2, slabs - 2, 2)])
     token = stage_source(0, [held])
     arrived = hop(base[0], [(0, 1)])
@@ -601,9 +627,9 @@
     right = lax.ppermute(head, "lat", [(i + 1, i) for i in range(lats - 1)])
     ups, field = finish(me, after, up, state, above, [head])
     part = middle(field, maps, forward_field[0, 0], width)
-    outgoing = rim(targets, part, left, right, maps, forward_field[0, 0], slabs)
+    outgoing = rim(targets, part, left, right, rims, forward_field[0, 0], slabs)
     arrived = lax.all_to_all(outgoing, "slab", split_axis=0, concat_axis=0, tiled=True)
-    model = jnp.sum(arrived.reshape(slabs, MBLK, width), axis=0)
+    model = model_rows(arrived.reshape(slabs, MBLK, width))
     return (ups[None, None], model[None, None])
 
 

time: 135 us -> 135 us (level)
    pallas_call x45 -> x47, Pallas kernels: 16.4 us -> 17.2 us  [call(): pl.pallas_call(run, in_specs=list(specs) + [ANY] * len(after), out_specs=...]
where the time goes in v5:
time: 135 us; the launch traced here: 134 us
  waiting for transfers between devices  52.1 us (39%)
  starting transfers between devices  51.4 us (38%)
  Pallas kernels  17.2 us (13%)
  blocking collectives  9.64 us (7%)
  local copies, waits for them, and re-layouts  2.1 us (2%)
  between operations  1.57 us (1%)
    ppermute x35, waiting for transfers between devices, hop(): return lax.ppermute(value, 'slab', route)  50.2 us
    ppermute x35, starting transfers between devices, hop(): return lax.ppermute(value, 'slab', route)  35.8 us
    pallas_call x47, Pallas kernels, call(): pl.pallas_call(run, in_specs=list(specs) + [ANY] * len(after), out_specs=...  17.2 us
    ppermute x1, starting transfers between devices, body(): left = lax.ppermute(tail, 'lat', [(i, i + 1) for i in range(lats - 1)])  13.6 us
    all_to_all x1, blocking collectives, body(): lax.all_to_all(outgoing, 'slab', split_axis=0, concat_axis=0, tiled=True)  9.64 us
  transfers between devices with their start and end apart: 37, of which 11 were waited for; matrix products, arithmetic and copies ran while one was open for 0% of the time, Pallas kernels for 9%

profile of v5, /device:TPU:1, one launch (start us, length us, event | category | flops | bytes accessed | tf_op | source)
XLA Modules:
  0.0 134.0 jit_solution(14849074928099161084)
XLA Ops:
  0.7 2.8 %collect.2 = (f32[1,2,64,512]{3,2,1,0:T(8,128)}, f32[1,2,64,512]{3,2,1,0:T(8,128)}) custom-call(s32[1]{0:T(128)} %bitcast.refs_0_, s32[32]{0:T(128)} %bitcast.21, s32[32]{0:T(128)} %refs_2_.5, f32[32,2,64,128]{3,2,1,0:T(8,128)} %refs_3_.4), custom_call_target="tpu_custom_call" | custom-call | flops 2000000000 | bytes 2000000 | tf_op jit(solution)/shard_map/collect/pallas_call | solution.py:46
  3.5 2.2 %collective-permute-start = (f32[1,2,64,512]{3,2,1,0:T(8,128)}, f32[1,2,64,512]{3,2,1,0:T(8,128)S(1)}, u32[]{:S(2)}, u32[]{:S(2)}) collective-permute-start(f32[1,2,64,512]{3,2,1,0:T(8,128)} %get-tuple-element.35), channel_id=1, source_target_pairs={{0,4},{4,0},{8,12},{12,8},{16,20},{20,16},{24,28},{28,24},{1,5},{5... | collective-permute-start | bytes 786440 | tf_op jit(solution)/shard_map/ppermute | solution.py:523
  5.8 0.9 copy-done.2
  6.7 1.6 %ready.1 = (f32[64,2]{1,0:T(8,128)S(1)}, s32[8]{0:T(128)S(1)}) custom-call(s32[64]{0:T(128)S(1)} %copy-done.4, s32[8]{0:T(128)S(1)} %bitcast.16, s32[8]{0:T(128)S(1)} %copy-done.6, f32[64,2]{1,0:T(8,128)S(1)} %copy.13.refs_3_, f32[1,2,64,512]{3,2,1,0:T(8,128)S(1)} %copy-done.2), custom_call_target="tpu_custom_call" | custom-call | tf_op jit(solution)/shard_map/ready/pallas_call | solution.py:46
  9.0 1.0 copy-done.8
  10.0 2.0 %collect.3 = (f32[1,2,64,512]{3,2,1,0:T(8,128)S(1)}, f32[1,2,64,512]{3,2,1,0:T(8,128)S(1)}, f32[2,2,64,512]{3,2,1,0:T(8,128)S(1)}, f32[2,2,64,512]{3,2,1,0:T(8,128)S(1)}) custom-call(s32[1]{0:T(128)} %bitcast.refs_0_, s32[32]{0:T(128)S(1)} %bitcast.22, s32[32]{0:T(128)S(1)} %copy-done.10, f32[32,2,64,128]{3,2,1,0:T(8,128)S(1)} %copy-done.8, ...), custom_call_target="tpu_custom_call" | custom-call | flops 2000000000 | bytes 2000000 | tf_op jit(solution)/shard_map/collect/pallas_call | solution.py:46
  12.1 1.3 collective-permute-start.1
  13.5 1.1 collective-permute-start.3
  15.0 3.8 %collective-permute-done.1.refs_1_ = f32[2,64,512]{2,1,0:T(8,128)S(1)} collective-permute-done((f32[2,64,512]{2,1,0:T(8,128)S(1)}, f32[2,64,512]{2,1,0:T(8,128)S(1)}, u32[]{:S(2)}, u32[]{:S(2)}) %collective-permute-start.1) | collective-permute-done | bytes 262176 | tf_op jit(solution)/shard_map/ppermute | solution.py:523
  18.9 1.3 collective-permute-start.2
  20.2 2.4 %collective-permute-start.6 = (f32[2,64,512]{2,1,0:T(8,128)S(1)}, f32[2,64,512]{2,1,0:T(8,128)S(1)}, u32[]{:S(2)}, u32[]{:S(2)}) collective-permute-start(f32[2,64,512]{2,1,0:T(8,128)S(1)} %get-tuple-element.52), channel_id=1, source_target_pairs={{0,8},{4,12},{16,24},{20,28},{1,9},{5,13},{17,25},{21,29},{2,10},{... | collective-permute-start | bytes 786440 | tf_op jit(solution)/shard_map/ppermute | solution.py:523
  23.2 1.6 %halves.6 = (bf16[768,2048]{1,0:T(8,128)(2,1)S(1)}, bf16[768,2048]{1,0:T(8,128)(2,1)S(1)}) custom-call(f32[2,768,1024]{2,1,0:T(8,128)S(1)} %bitcast.19, bf16[512,1024]{1,0:T(8,128)(2,1)S(1)} %get-tuple-element.45.refs_1_.refs_2_.refs_5_.refs_7_), custom_call_target="tpu_custom_call" | custom-call | flops 2000000000 | bytes 2000000 | tf_op jit(solution)/shard_map/halves/pallas_call | solution.py:46
  25.0 2.4 %collective-permute-done.2.refs_1_ = f32[2,64,512]{2,1,0:T(8,128)S(1)} collective-permute-done((f32[2,64,512]{2,1,0:T(8,128)S(1)}, f32[2,64,512]{2,1,0:T(8,128)S(1)}, u32[]{:S(2)}, u32[]{:S(2)}) %collective-permute-start.2) | collective-permute-done | bytes 262176 | tf_op jit(solution)/shard_map/ppermute | solution.py:523
  27.6 2.1 %collective-permute-start.4 = (f32[2,64,512]{2,1,0:T(8,128)S(1)}, f32[2,64,512]{2,1,0:T(8,128)S(1)}, u32[]{:S(2)}, u32[]{:S(2)}) collective-permute-start(f32[2,64,512]{2,1,0:T(8,128)S(1)} %source.3.refs_2_.refs_4_.refs_5_), channel_id=1, source_target_pairs={{0,4},{1,5},{2,6},{3,7}} | collective-permute-start | bytes 786440 | tf_op jit(solution)/shard_map/ppermute | solution.py:523
  29.8 0.7 collective-permute-start.8
  31.5 3.8 %collective-permute-done.4.refs_1_ = f32[2,64,512]{2,1,0:T(8,128)S(1)} collective-permute-done((f32[2,64,512]{2,1,0:T(8,128)S(1)}, f32[2,64,512]{2,1,0:T(8,128)S(1)}, u32[]{:S(2)}, u32[]{:S(2)}) %collective-permute-start.4) | collective-permute-done | bytes 262176 | tf_op jit(solution)/shard_map/ppermute | solution.py:523
  35.4 0.7 collective-permute-start.7
  36.1 0.8 collective-permute-start.24
  37.1 1.3 collective-permute-start.23
  38.4 3.9 %collective-permute-start.12 = (f32[2,64,512]{2,1,0:T(8,128)S(1)}, f32[2,64,512]{2,1,0:T(8,128)S(1)}, u32[]{:S(2)}, u32[]{:S(2)}) collective-permute-start(f32[2,64,512]{2,1,0:T(8,128)S(1)} %add.5.refs_2_.refs_0_), channel_id=1, source_target_pairs={{0,16},{4,20},{8,24},{12,28},{1,17},{5,21},{9,25},{13,29},{2,18},{... | collective-permute-start | bytes 786440 | tf_op jit(solution)/shard_map/ppermute | solution.py:523
  42.3 0.7 collective-permute-start.10
  43.0 0.7 collective-permute-start.13
  43.7 0.7 collective-permute-start.11
  46.4 0.7 collective-permute-start.17
  47.1 0.7 collective-permute-start.16
  50.7 0.7 collective-permute-start.25
  51.4 1.3 collective-permute-start.26
  52.7 0.7 collective-permute-start.22
  53.4 1.3 collective-permute-start.29
  55.4 31.5 %collective-permute-done.23.refs_1_ = f32[2,512,512]{2,1,0:T(8,128)S(1)} collective-permute-done((f32[2,512,512]{2,1,0:T(8,128)S(1)}, f32[2,512,512]{2,1,0:T(8,128)S(1)}, u32[]{:S(2)}, u32[]{:S(2)}) %collective-permute-start.23) | collective-permute-done | bytes 2097184 | tf_op jit(solution)/shard_map/ppermute | solution.py:523
  87.0 0.7 halves.7
  87.7 2.1 %collective-permute-done.26.refs_4_ = f32[2,32,512]{2,1,0:T(8,128)S(1)} collective-permute-done((f32[2,32,512]{2,1,0:T(8,128)S(1)}, f32[2,32,512]{2,1,0:T(8,128)S(1)}, u32[]{:S(2)}, u32[]{:S(2)}) %collective-permute-start.26) | collective-permute-done | bytes 131104 | tf_op jit(solution)/shard_map/ppermute | solution.py:523
  90.5 2.1 %collective-permute-done.29.refs_4_ = f32[2,32,512]{2,1,0:T(8,128)S(1)} collective-permute-done((f32[2,32,512]{2,1,0:T(8,128)S(1)}, f32[2,32,512]{2,1,0:T(8,128)S(1)}, u32[]{:S(2)}, u32[]{:S(2)}) %collective-permute-start.29) | collective-permute-done | bytes 131104 | tf_op jit(solution)/shard_map/ppermute | solution.py:523
  93.3 1.3 collective-permute-start.33
  94.7 1.3 collective-permute-start.34
  96.0 0.7 collective-permute-start.32
  96.6 0.7 collective-permute-start.30
  97.3 2.0 %collective-permute-done.33.refs_1_ = f32[2,32,512]{2,1,0:T(8,128)S(1)} collective-permute-done((f32[2,32,512]{2,1,0:T(8,128)S(1)}, f32[2,32,512]{2,1,0:T(8,128)S(1)}, u32[]{:S(2)}, u32[]{:S(2)}) %collective-permute-start.33) | collective-permute-done | bytes 131104 | tf_op jit(solution)/shard_map/ppermute | solution.py:523
  99.4 1.3 up.14.refs_9_.refs_5_
  100.7 1.3 collective-permute-done.34.refs_1_
  102.0 1.3 up.15.refs_6_.refs_9_
  103.4 13.6 %collective-permute-start.35 = (f32[2,64,128]{2,1,0:T(8,128)S(1)}, f32[2,64,128]{2,1,0:T(8,128)S(1)}, u32[]{:S(2)}, u32[]{:S(2)}) collective-permute-start(f32[2,64,128]{2,1,0:T(8,128)S(1)} %get-tuple-element.64), channel_id=1, source_target_pairs={{0,1},{1,2},{2,3},{4,5},{5,6},{6,7},{8,9},{9,10},{10,11},{12,13},{... | collective-permute-start | bytes 196616 | tf_op jit(solution)/shard_map/ppermute | solution.py:626
  117.0 1.9 %collective-permute-start.36 = (f32[2,64,128]{2,1,0:T(8,128)S(1)}, f32[2,64,128]{2,1,0:T(8,128)S(1)}, u32[]{:S(2)}, u32[]{:S(2)}) collective-permute-start(f32[2,64,128]{2,1,0:T(8,128)S(1)} %get-tuple-element.60.refs_9_), channel_id=1, source_target_pairs={{1,0},{2,1},{3,2},{5,4},{6,5},{7,6},{9,8},{10,9},{11,10},{13,12},{... | collective-permute-start | bytes 196616 | tf_op jit(solution)/shard_map/ppermute | solution.py:627
  118.9 0.7 finish.1
  119.7 1.0 middle.1.refs_1_
  120.7 1.9 %collective-permute-done.36.refs_3_ = f32[2,64,128]{2,1,0:T(8,128)S(1)} collective-permute-done((f32[2,64,128]{2,1,0:T(8,128)S(1)}, f32[2,64,128]{2,1,0:T(8,128)S(1)}, u32[]{:S(2)}, u32[]{:S(2)}) %collective-permute-start.36) | collective-permute-done | bytes 65568 | tf_op jit(solution)/shard_map/ppermute | solution.py:627
  122.6 1.2 rim.1
  123.8 9.6 %all_to_all.9.refs_0_ = f32[8,8,128]{2,1,0:T(8,128)S(1)} all-to-all(f32[8,8,128]{2,1,0:T(8,128)S(1)} %bitcast.15), channel_id=1, replica_groups=mesh['slab'=8,'lat'=4] {'slab'}, dimensions={0} | all-to-all | bytes 65536 | tf_op jit(solution)/shard_map/all_to_all | solution.py:631
  (104 shorter events, 11.0 us)
Async XLA Ops:
  0.6 5.0 %copy-start.11 = (f32[64,2]{0,1:T(2,128)S(1)}, f32[64,2]{0,1:T(2,128)}, u32[]{:S(2)}) copy-start(f32[64,2]{0,1:T(2,128)} %param.15) | copy-start | bytes 1540
  0.6 5.1 %copy-start.4 = (s32[64]{0:T(128)S(1)}, s32[64]{0:T(128)}, u32[]{:S(2)}) copy-start(s32[64]{0:T(128)} %refs_0_.1) | copy-start | bytes 772
  0.7 5.1 %copy-start.5 = (s32[8,1]{0,1:T(1,128)S(1)}, s32[8,1]{0,1:T(1,128)}, u32[]{:S(2)}) copy-start(s32[8,1]{0,1:T(1,128)} %param.20) | copy-start | bytes 100
  0.7 5.1 %copy-start.6 = (s32[8]{0:T(128)S(1)}, s32[8]{0:T(128)}, u32[]{:S(2)}) copy-start(s32[8]{0:T(128)} %refs_2_.4) | copy-start | bytes 100
  0.7 7.7 %copy-start.7 = (f32[1,1,2,512,512]{4,3,2,1,0:T(8,128)S(1)}, f32[1,1,2,512,512]{4,3,2,1,0:T(8,128)}, u32[]{:S(2)}) copy-start(f32[1,1,2,512,512]{4,3,2,1,0:T(8,128)} %param.16) | copy-start | bytes 6291460
  3.5 8.5 %collective-permute-start = (f32[1,2,64,512]{3,2,1,0:T(8,128)}, f32[1,2,64,512]{3,2,1,0:T(8,128)S(1)}, u32[]{:S(2)}, u32[]{:S(2)}) collective-permute-start(f32[1,2,64,512]{3,2,1,0:T(8,128)} %get-tuple-element.35), channel_id=1, source_target_pairs={{0,4},{4,0},{8,12},{12,8},{16,20},{20,16},{24,28},{28,24},{1,5},{5... | collective-permute-start | bytes 786440 | tf_op jit(solution)/shard_map/ppermute | solution.py:523
  8.4 1.6 %copy-start.8 = (f32[32,2,64,128]{3,2,1,0:T(8,128)S(1)}, f32[32,2,64,128]{3,2,1,0:T(8,128)}, u32[]{:S(2)}) copy-start(f32[32,2,64,128]{3,2,1,0:T(8,128)} %refs_3_.4) | copy-start | bytes 6291460
  10.0 2.1 %copy-start.3 = (f32[1,2,64,512]{3,2,1,0:T(8,128)S(1)}, f32[1,2,64,512]{3,2,1,0:T(8,128)}, u32[]{:S(2)}) copy-start(f32[1,2,64,512]{3,2,1,0:T(8,128)} %get-tuple-element.34.refs_4_.refs_0_) | copy-start | bytes 786436
  10.0 13.2 %slice-start = ((s8[6291456]{0:T(1024)(128)(4,1)}), s8[4194304]{0:T(1024)(128)(4,1)S(1)}, s32[]{:S(2)}) async-start(s8[6291456]{0:T(1024)(128)(4,1)} %bitcast.17), calls=%async_computation.1 | async-start | bytes 8388608
  12.0 10.6 %copy-start = (f32[1,1,2,512,512]{4,3,2,1,0:T(8,128)S(1)}, f32[1,1,2,512,512]{4,3,2,1,0:T(8,128)}, u32[]{:S(2)}) copy-start(f32[1,1,2,512,512]{4,3,2,1,0:T(8,128)} %param.17) | copy-start | bytes 6291460
  12.1 6.8 %collective-permute-start.1 = (f32[2,64,512]{2,1,0:T(8,128)S(1)}, f32[2,64,512]{2,1,0:T(8,128)S(1)}, u32[]{:S(2)}, u32[]{:S(2)}) collective-permute-start(f32[2,64,512]{2,1,0:T(8,128)S(1)} %get-tuple-element.40), channel_id=1, source_target_pairs={{0,8},{4,12},{8,0},{12,4},{16,24},{20,28},{24,16},{28,20},{1,9},{5... | collective-permute-start | bytes 786440 | tf_op jit(solution)/shard_map/ppermute | solution.py:523
  13.5 9.7 %slice-start.1 = ((s8[6291456]{0:T(1024)(128)(4,1)}), s8[2097152]{0:T(1024)(128)(4,1)S(1)}, s32[]{:S(2)}) async-start(s8[6291456]{0:T(1024)(128)(4,1)} %bitcast.17), calls=%async_computation.2 | async-start | bytes 4194304
  13.5 6.7 %collective-permute-start.3 = (f32[1,2,64,512]{3,2,1,0:T(8,128)S(1)}, f32[1,2,64,512]{3,2,1,0:T(8,128)S(1)}, u32[]{:S(2)}, u32[]{:S(2)}) collective-permute-start(f32[1,2,64,512]{3,2,1,0:T(8,128)S(1)} %get-tuple-element.43.refs_2_), channel_id=1, source_target_pairs={{0,4},{4,0},{8,12},{12,8},{16,20},{20,16},{24,28},{28,24},{1,5},{5... | collective-permute-start | bytes 786440 | tf_op jit(solution)/shard_map/ppermute | solution.py:523
  14.6 16.4 %collective-permute-start.5 = (f32[2,2,64,512]{3,2,1,0:T(8,128)S(1)}, f32[2,2,64,512]{3,2,1,0:T(8,128)S(1)}, u32[]{:S(2)}, u32[]{:S(2)}) collective-permute-start(f32[2,2,64,512]{3,2,1,0:T(8,128)S(1)} %get-tuple-element.51), channel_id=1, source_target_pairs={{0,4},{4,0},{8,12},{12,8},{16,20},{20,16},{24,28},{28,24},{1,5},{5... | collective-permute-start | bytes 1572872 | tf_op jit(solution)/shard_map/ppermute | solution.py:523
  18.9 8.6 %collective-permute-start.2 = (f32[2,64,512]{2,1,0:T(8,128)S(1)}, f32[2,64,512]{2,1,0:T(8,128)S(1)}, u32[]{:S(2)}, u32[]{:S(2)}) collective-permute-start(f32[2,64,512]{2,1,0:T(8,128)S(1)} %add.3.refs_2_.refs_0_), channel_id=1, source_target_pairs={{16,0},{20,4},{17,1},{21,5},{18,2},{22,6},{19,3},{23,7}} | collective-permute-start | bytes 786440 | tf_op jit(solution)/shard_map/ppermute | solution.py:523
  20.2 9.5 %collective-permute-start.6 = (f32[2,64,512]{2,1,0:T(8,128)S(1)}, f32[2,64,512]{2,1,0:T(8,128)S(1)}, u32[]{:S(2)}, u32[]{:S(2)}) collective-permute-start(f32[2,64,512]{2,1,0:T(8,128)S(1)} %get-tuple-element.52), channel_id=1, source_target_pairs={{0,8},{4,12},{16,24},{20,28},{1,9},{5,13},{17,25},{21,29},{2,10},{... | collective-permute-start | bytes 786440 | tf_op jit(solution)/shard_map/ppermute | solution.py:523
  27.6 7.8 %collective-permute-start.4 = (f32[2,64,512]{2,1,0:T(8,128)S(1)}, f32[2,64,512]{2,1,0:T(8,128)S(1)}, u32[]{:S(2)}, u32[]{:S(2)}) collective-permute-start(f32[2,64,512]{2,1,0:T(8,128)S(1)} %source.3.refs_2_.refs_4_.refs_5_), channel_id=1, source_target_pairs={{0,4},{1,5},{2,6},{3,7}} | collective-permute-start | bytes 786440 | tf_op jit(solution)/shard_map/ppermute | solution.py:523
  29.8 7.2 %collective-permute-start.8 = (f32[2,64,512]{2,1,0:T(8,128)S(1)}, f32[2,64,512]{2,1,0:T(8,128)S(1)}, u32[]{:S(2)}, u32[]{:S(2)}) collective-permute-start(f32[2,64,512]{2,1,0:T(8,128)S(1)} %add.4.refs_2_.refs_0_), channel_id=1, source_target_pairs={{24,8},{28,12},{25,9},{29,13},{26,10},{30,14},{27,11},{31,15}} | collective-permute-start | bytes 786440 | tf_op jit(solution)/shard_map/ppermute | solution.py:523
  31.1 6.0 %collective-permute-start.9 = (f32[2,64,512]{2,1,0:T(8,128)S(1)}, f32[2,64,512]{2,1,0:T(8,128)S(1)}, u32[]{:S(2)}, u32[]{:S(2)}) collective-permute-start(f32[2,64,512]{2,1,0:T(8,128)S(1)} %get-tuple-element.55), channel_id=1, source_target_pairs={{0,8},{4,12},{8,0},{12,4},{16,24},{20,28},{24,16},{28,20},{1,9},{5... | collective-permute-start | bytes 786440 | tf_op jit(solution)/shard_map/ppermute | solution.py:523
  35.4 1.7 %collective-permute-start.7 = (f32[2,64,512]{2,1,0:T(8,128)S(1)}, f32[2,64,512]{2,1,0:T(8,128)S(1)}, u32[]{:S(2)}, u32[]{:S(2)}) collective-permute-start(f32[2,64,512]{2,1,0:T(8,128)S(1)} %down.13.refs_0_.refs_1_), channel_id=1, source_target_pairs={{4,8},{5,9},{6,10},{7,11}} | collective-permute-start | bytes 786440 | tf_op jit(solution)/shard_map/ppermute | solution.py:523
  36.1 18.7 %collective-permute-start.24 = (f32[2,512,512]{2,1,0:T(8,128)S(1)}, f32[2,512,512]{2,1,0:T(8,128)S(1)}, u32[]{:S(2)}, u32[]{:S(2)}) collective-permute-start(f32[2,512,512]{2,1,0:T(8,128)S(1)} %hold.2.refs_3_), channel_id=1, source_target_pairs={{12,8},{20,16},{13,9},{21,17},{14,10},{22,18},{15,11},{23,19}} | collective-permute-start | bytes 6291464 | tf_op jit(solution)/shard_map/ppermute | solution.py:523
  37.1 49.9 %collective-permute-start.23 = (f32[2,512,512]{2,1,0:T(8,128)S(1)}, f32[2,512,512]{2,1,0:T(8,128)S(1)}, u32[]{:S(2)}, u32[]{:S(2)}) collective-permute-start(f32[2,512,512]{2,1,0:T(8,128)S(1)} %hold.3.refs_6_), channel_id=1, source_target_pairs={{4,0},{5,1},{6,2},{7,3}} | collective-permute-start | bytes 6291464 | tf_op jit(solution)/shard_map/ppermute | solution.py:523
  38.4 7.1 %collective-permute-start.12 = (f32[2,64,512]{2,1,0:T(8,128)S(1)}, f32[2,64,512]{2,1,0:T(8,128)S(1)}, u32[]{:S(2)}, u32[]{:S(2)}) collective-permute-start(f32[2,64,512]{2,1,0:T(8,128)S(1)} %add.5.refs_2_.refs_0_), channel_id=1, source_target_pairs={{0,16},{4,20},{8,24},{12,28},{1,17},{5,21},{9,25},{13,29},{2,18},{... | collective-permute-start | bytes 786440 | tf_op jit(solution)/shard_map/ppermute | solution.py:523
  42.3 1.4 %collective-permute-start.10 = (f32[2,32,512]{2,1,0:T(8,128)S(1)}, f32[2,32,512]{2,1,0:T(8,128)S(1)}, u32[]{:S(2)}, u32[]{:S(2)}) collective-permute-start(f32[2,32,512]{2,1,0:T(8,128)S(1)} %down.14.refs_6_.refs_5_), channel_id=1, source_target_pairs={{8,12},{9,13},{10,14},{11,15}} | collective-permute-start | bytes 393224 | tf_op jit(solution)/shard_map/ppermute | solution.py:523
  43.0 1.4 %collective-permute-start.13 = (f32[2,32,512]{2,1,0:T(8,128)S(1)}, f32[2,32,512]{2,1,0:T(8,128)S(1)}, u32[]{:S(2)}, u32[]{:S(2)}) collective-permute-start(f32[2,32,512]{2,1,0:T(8,128)S(1)} %down.15.refs_6_.refs_5_), channel_id=1, source_target_pairs={{8,12},{9,13},{10,14},{11,15}} | collective-permute-start | bytes 393224 | tf_op jit(solution)/shard_map/ppermute | solution.py:523
  43.7 1.9 %collective-permute-start.11 = (f32[2,32,512]{2,1,0:T(8,128)S(1)}, f32[2,32,512]{2,1,0:T(8,128)S(1)}, u32[]{:S(2)}, u32[]{:S(2)}) collective-permute-start(f32[2,32,512]{2,1,0:T(8,128)S(1)} %down.16.refs_6_.refs_5_), channel_id=1, source_target_pairs={{12,16},{13,17},{14,18},{15,19}} | collective-permute-start | bytes 393224 | tf_op jit(solution)/shard_map/ppermute | solution.py:523
  44.4 1.9 %collective-permute-start.15 = (f32[2,32,512]{2,1,0:T(8,128)S(1)}, f32[2,32,512]{2,1,0:T(8,128)S(1)}, u32[]{:S(2)}, u32[]{:S(2)}) collective-permute-start(f32[2,32,512]{2,1,0:T(8,128)S(1)} %down.17.refs_3_.refs_5_), channel_id=1, source_target_pairs={{12,16},{13,17},{14,18},{15,19}} | collective-permute-start | bytes 393224 | tf_op jit(solution)/shard_map/ppermute | solution.py:523
  45.7 1.4 %collective-permute-start.14 = (f32[2,32,512]{2,1,0:T(8,128)S(1)}, f32[2,32,512]{2,1,0:T(8,128)S(1)}, u32[]{:S(2)}, u32[]{:S(2)}) collective-permute-start(f32[2,32,512]{2,1,0:T(8,128)S(1)} %down.18.refs_6_.refs_5_), channel_id=1, source_target_pairs={{16,20},{17,21},{18,22},{19,23}} | collective-permute-start | bytes 393224 | tf_op jit(solution)/shard_map/ppermute | solution.py:523
  46.4 1.4 %collective-permute-start.17 = (f32[2,32,512]{2,1,0:T(8,128)S(1)}, f32[2,32,512]{2,1,0:T(8,128)S(1)}, u32[]{:S(2)}, u32[]{:S(2)}) collective-permute-start(f32[2,32,512]{2,1,0:T(8,128)S(1)} %down.19.refs_6_.refs_5_), channel_id=1, source_target_pairs={{16,20},{17,21},{18,22},{19,23}} | collective-permute-start | bytes 393224 | tf_op jit(solution)/shard_map/ppermute | solution.py:523
  47.1 1.4 %collective-permute-start.16 = (f32[2,32,512]{2,1,0:T(8,128)S(1)}, f32[2,32,512]{2,1,0:T(8,128)S(1)}, u32[]{:S(2)}, u32[]{:S(2)}) collective-permute-start(f32[2,32,512]{2,1,0:T(8,128)S(1)} %down.20.refs_6_.refs_5_), channel_id=1, source_target_pairs={{20,24},{21,25},{22,26},{23,27}} | collective-permute-start | bytes 393224 | tf_op jit(solution)/shard_map/ppermute | solution.py:523
  47.8 1.4 %collective-permute-start.19 = (f32[2,32,512]{2,1,0:T(8,128)S(1)}, f32[2,32,512]{2,1,0:T(8,128)S(1)}, u32[]{:S(2)}, u32[]{:S(2)}) collective-permute-start(f32[2,32,512]{2,1,0:T(8,128)S(1)} %down.21.refs_6_.refs_5_), channel_id=1, source_target_pairs={{20,24},{21,25},{22,26},{23,27}} | collective-permute-start | bytes 393224 | tf_op jit(solution)/shard_map/ppermute | solution.py:523
  48.6 1.4 %collective-permute-start.18 = (f32[2,32,512]{2,1,0:T(8,128)S(1)}, f32[2,32,512]{2,1,0:T(8,128)S(1)}, u32[]{:S(2)}, u32[]{:S(2)}) collective-permute-start(f32[2,32,512]{2,1,0:T(8,128)S(1)} %down.22.refs_6_.refs_5_), channel_id=1, source_target_pairs={{24,28},{25,29},{26,30},{27,31}} | collective-permute-start | bytes 393224 | tf_op jit(solution)/shard_map/ppermute | solution.py:523
  49.3 1.4 %collective-permute-start.21 = (f32[2,32,512]{2,1,0:T(8,128)S(1)}, f32[2,32,512]{2,1,0:T(8,128)S(1)}, u32[]{:S(2)}, u32[]{:S(2)}) collective-permute-start(f32[2,32,512]{2,1,0:T(8,128)S(1)} %down.23.refs_6_.refs_5_), channel_id=1, source_target_pairs={{24,28},{25,29},{26,30},{27,31}} | collective-permute-start | bytes 393224 | tf_op jit(solution)/shard_map/ppermute | solution.py:523
  50.0 2.7 %collective-permute-start.20 = (f32[2,32,512]{2,1,0:T(8,128)S(1)}, f32[2,32,512]{2,1,0:T(8,128)S(1)}, u32[]{:S(2)}, u32[]{:S(2)}) collective-permute-start(f32[2,32,512]{2,1,0:T(8,128)S(1)} %down.24.refs_6_.refs_4_.refs_5_.refs_7_.refs_3_), channel_id=1, source_target_pairs={{28,24},{29,25},{30,26},{31,27}} | collective-permute-start | bytes 393224 | tf_op jit(solution)/shard_map/ppermute | solution.py:523
  50.7 2.7 %collective-permute-start.25 = (f32[2,32,512]{2,1,0:T(8,128)S(1)}, f32[2,32,512]{2,1,0:T(8,128)S(1)}, u32[]{:S(2)}, u32[]{:S(2)}) collective-permute-start(f32[2,32,512]{2,1,0:T(8,128)S(1)} %down.25.refs_6_.refs_4_.refs_5_.refs_7_), channel_id=1, source_target_pairs={{28,24},{29,25},{30,26},{31,27}} | collective-permute-start | bytes 393224 | tf_op jit(solution)/shard_map/ppermute | solution.py:523
  51.4 38.4 %collective-permute-start.26 = (f32[2,32,512]{2,1,0:T(8,128)S(1)}, f32[2,32,512]{2,1,0:T(8,128)S(1)}, u32[]{:S(2)}, u32[]{:S(2)}) collective-permute-start(f32[2,32,512]{2,1,0:T(8,128)S(1)} %down.24.refs_6_.refs_4_.refs_5_.refs_7_.refs_3_), channel_id=1, source_target_pairs={{4,0},{12,8},{20,16},{5,1},{13,9},{21,17},{6,2},{14,10},{22,18},{7... | collective-permute-start | bytes 393224 | tf_op jit(solution)/shard_map/ppermute | solution.py:523
  52.7 37.1 %collective-permute-start.22 = (f32[2,32,512]{2,1,0:T(8,128)S(1)}, f32[2,32,512]{2,1,0:T(8,128)S(1)}, u32[]{:S(2)}, u32[]{:S(2)}) collective-permute-start(f32[2,32,512]{2,1,0:T(8,128)S(1)} %up.8.refs_6_.refs_8_), channel_id=1, source_target_pairs={{24,16},{25,17},{26,18},{27,19}} | collective-permute-start | bytes 393224 | tf_op jit(solution)/shard_map/ppermute | solution.py:523
  53.4 39.2 %collective-permute-start.29 = (f32[2,32,512]{2,1,0:T(8,128)S(1)}, f32[2,32,512]{2,1,0:T(8,128)S(1)}, u32[]{:S(2)}, u32[]{:S(2)}) collective-permute-start(f32[2,32,512]{2,1,0:T(8,128)S(1)} %down.25.refs_6_.refs_4_.refs_5_.refs_7_), channel_id=1, source_target_pairs={{4,0},{12,8},{20,16},{5,1},{13,9},{21,17},{6,2},{14,10},{22,18},{7... | collective-permute-start | bytes 393224 | tf_op jit(solution)/shard_map/ppermute | solution.py:523
  54.7 37.8 %collective-permute-start.28 = (f32[2,32,512]{2,1,0:T(8,128)S(1)}, f32[2,32,512]{2,1,0:T(8,128)S(1)}, u32[]{:S(2)}, u32[]{:S(2)}) collective-permute-start(f32[2,32,512]{2,1,0:T(8,128)S(1)} %up.9.refs_3_.refs_8_), channel_id=1, source_target_pairs={{24,16},{25,17},{26,18},{27,19}} | collective-permute-start | bytes 393224 | tf_op jit(solution)/shard_map/ppermute | solution.py:523
  89.8 3.5 %collective-permute-start.27 = (f32[2,32,512]{2,1,0:T(8,128)S(1)}, f32[2,32,512]{2,1,0:T(8,128)S(1)}, u32[]{:S(2)}, u32[]{:S(2)}) collective-permute-start(f32[2,32,512]{2,1,0:T(8,128)S(1)} %up.10.refs_9_.refs_8_), channel_id=1, source_target_pairs={{16,8},{17,9},{18,10},{19,11}} | collective-permute-start | bytes 393224 | tf_op jit(solution)/shard_map/ppermute | solution.py:523
  92.6 2.0 %collective-permute-start.31 = (f32[2,32,512]{2,1,0:T(8,128)S(1)}, f32[2,32,512]{2,1,0:T(8,128)S(1)}, u32[]{:S(2)}, u32[]{:S(2)}) collective-permute-start(f32[2,32,512]{2,1,0:T(8,128)S(1)} %up.11.refs_9_.refs_8_), channel_id=1, source_target_pairs={{16,8},{17,9},{18,10},{19,11}} | collective-permute-start | bytes 393224 | tf_op jit(solution)/shard_map/ppermute | solution.py:523
  93.3 6.0 %collective-permute-start.33 = (f32[2,32,512]{2,1,0:T(8,128)S(1)}, f32[2,32,512]{2,1,0:T(8,128)S(1)}, u32[]{:S(2)}, u32[]{:S(2)}) collective-permute-start(f32[2,32,512]{2,1,0:T(8,128)S(1)} %up.12.refs_9_.refs_8_), channel_id=1, source_target_pairs={{8,0},{9,1},{10,2},{11,3}} | collective-permute-start | bytes 393224 | tf_op jit(solution)/shard_map/ppermute | solution.py:523
  94.7 7.3 %collective-permute-start.34 = (f32[2,32,512]{2,1,0:T(8,128)S(1)}, f32[2,32,512]{2,1,0:T(8,128)S(1)}, u32[]{:S(2)}, u32[]{:S(2)}) collective-permute-start(f32[2,32,512]{2,1,0:T(8,128)S(1)} %up.13.refs_9_.refs_8_), channel_id=1, source_target_pairs={{8,0},{9,1},{10,2},{11,3}} | collective-permute-start | bytes 393224 | tf_op jit(solution)/shard_map/ppermute | solution.py:523
  96.0 7.3 %collective-permute-start.32 = (f32[2,32,512]{2,1,0:T(8,128)S(1)}, f32[2,32,512]{2,1,0:T(8,128)S(1)}, u32[]{:S(2)}, u32[]{:S(2)}) collective-permute-start(f32[2,32,512]{2,1,0:T(8,128)S(1)} %up.13.refs_9_.refs_8_), channel_id=1, source_target_pairs={{8,4},{16,12},{24,20},{9,5},{17,13},{25,21},{10,6},{18,14},{26,22}... | collective-permute-start | bytes 393224 | tf_op jit(solution)/shard_map/ppermute | solution.py:523
  96.6 6.7 %collective-permute-start.30 = (f32[2,32,512]{2,1,0:T(8,128)S(1)}, f32[2,32,512]{2,1,0:T(8,128)S(1)}, u32[]{:S(2)}, u32[]{:S(2)}) collective-permute-start(f32[2,32,512]{2,1,0:T(8,128)S(1)} %up.12.refs_9_.refs_8_), channel_id=1, source_target_pairs={{8,4},{16,12},{24,20},{9,5},{17,13},{25,21},{10,6},{18,14},{26,22}... | collective-permute-start | bytes 393224 | tf_op jit(solution)/shard_map/ppermute | solution.py:523
  103.4 16.3 %copy-start.1 = (f32[1,1,2,64,1024]{4,3,2,1,0:T(8,128)S(1)}, f32[1,1,2,64,1024]{4,3,2,1,0:T(8,128)}, u32[]{:S(2)}) copy-start(f32[1,1,2,64,1024]{4,3,2,1,0:T(8,128)} %param.19) | copy-start | bytes 1572868
  103.4 17.3 %collective-permute-start.35 = (f32[2,64,128]{2,1,0:T(8,128)S(1)}, f32[2,64,128]{2,1,0:T(8,128)S(1)}, u32[]{:S(2)}, u32[]{:S(2)}) collective-permute-start(f32[2,64,128]{2,1,0:T(8,128)S(1)} %get-tuple-element.64), channel_id=1, source_target_pairs={{0,1},{1,2},{2,3},{4,5},{5,6},{6,7},{8,9},{9,10},{10,11},{12,13},{... | collective-permute-start | bytes 196616 | tf_op jit(solution)/shard_map/ppermute | solution.py:626
  117.0 5.6 %collective-permute-start.36 = (f32[2,64,128]{2,1,0:T(8,128)S(1)}, f32[2,64,128]{2,1,0:T(8,128)S(1)}, u32[]{:S(2)}, u32[]{:S(2)}) collective-permute-start(f32[2,64,128]{2,1,0:T(8,128)S(1)} %get-tuple-element.60.refs_9_), channel_id=1, source_target_pairs={{1,0},{2,1},{3,2},{5,4},{6,5},{7,6},{9,8},{10,9},{11,10},{13,12},{... | collective-permute-start | bytes 196616 | tf_op jit(solution)/shard_map/ppermute | solution.py:627
  (3 other events, 4.1 us)

commit v6 on v5

--- a/solution.py
+++ b/solution.py
@@ -349,20 +349,36 @@
     return jnp.concatenate([ref[...] for ref in refs], axis=1)
 
 
+def sides_kernel(high_ref, low_ref, high_out, low_out):
+    trace = high_ref.shape[1] // 2
+    width = high_out.shape[1] // 4
+    for ref, out in ((high_ref, high_out), (low_ref, low_out)):
+        for number, first in enumerate((0, trace - width, trace, 2 * trace - width)):
+            out[:, number * width : (number + 1) * width] = ref[:, first : first + width]
+
+
+def sides(panel, width, after):
+    shape = jax.ShapeDtypeStruct((panel[0].shape[0], 4 * width), jnp.bfloat16)
+    return call(
+        sides_kernel,
+        "sides",
+        [(VMEM, panel[0]), (VMEM, panel[1])],
+        [shape] * 2,
+        [VMEM] * 2,
+        after,
+    )
+
+
 def edges_kernel(me_ref, *refs, streams, width):
     arrived, owns, olds = (refs[i * streams : (i + 1) * streams] for i in range(3))
     high_ref, low_ref, head_ref, tail_ref = refs[3 * streams :]
-    trace = high_ref.shape[1] // 2
+    trace = owns[0].shape[-1]
     first, last = slice(0, width), slice(trace - width, trace)
     passed = lax.rem(me_ref[0], 2) == 1
 
-    def ends(ref):
-        more = (slice(trace, trace + width), slice(2 * trace - width, 2 * trace))
-        return jnp.concatenate([ref[:, cut] for cut in (first, last, *more)], axis=1)
-
     @pl.when(passed)
     def _():
-        values = product(whole(arrived), ends(high_ref), ends(low_ref))
+        values = product(whole(arrived), high_ref[...], low_ref[...])
         own = whole(owns)
         for part, value in enumerate(values):
             head_ref[part] = value[:, :width] + own[part, :, first]
@@ -568,7 +584,8 @@
         token = stage_add(0, turn, token)
     token = stage_join(1, token)
     up = halves(up_panel[0, 0], token)
-    maps = halves(recovery[0, 0], [up[0]])
+    flanks = sides(up, width, [])
+    maps = halves(recovery[0, 0], [flanks[0]])
     rims = frame(maps, width, [])
     held = hold(me, 3, up_panel[0, 0], [rims[0]])
     far_panel = hop(held, [(p + 1, p) for p in range(2, slabs - 2, 2)])
@@ -622,7 +639,7 @@
             token = [above[t]]
         if p > 0:
             arrived = [hop(above[t], [(p, p - 2)]) for t in lanes]
-    head, tail = edges(me, after, up, state, above, width, token)
+    head, tail = edges(me, after, flanks, state, above, width, token)
     left = lax.ppermute(tail, "lat", [(i, i + 1) for i in range(lats - 1)])
     right = lax.ppermute(head, "lat", [(i + 1, i) for i in range(lats - 1)])
     ups, field = finish(me, after, up, state, above, [head])

time: 135 us -> 134 us (level)
    pallas_call x47 -> x48, Pallas kernels: 17.2 us -> 17.3 us  [call(): pl.pallas_call(run, in_specs=list(specs) + [ANY] * len(after), out_specs=...]
where the time goes in v6:
time: 134 us
  starting transfers between devices  51.6 us (39%)
  waiting for transfers between devices  51.6 us (39%)
  Pallas kernels  17.3 us (13%)
  blocking collectives  9.49 us (7%)
  local copies, waits for them, and re-layouts  2.1 us (2%)
  between operations  1.58 us (1%)
    ppermute x35, waiting for transfers between devices, hop(): return lax.ppermute(value, 'slab', route)  49.7 us
    ppermute x35, starting transfers between devices, hop(): return lax.ppermute(value, 'slab', route)  36.2 us
    pallas_call x48, Pallas kernels, call(): pl.pallas_call(run, in_specs=list(specs) + [ANY] * len(after), out_specs=...  17.3 us
    ppermute x1, starting transfers between devices, body(): left = lax.ppermute(tail, 'lat', [(i, i + 1) for i in range(lats - 1)])  13.5 us
    all_to_all x1, blocking collectives, body(): lax.all_to_all(outgoing, 'slab', split_axis=0, concat_axis=0, tiled=True)  9.49 us
  transfers between devices with their start and end apart: 37, of which 11 were waited for; matrix products, arithmetic and copies ran while one was open for 0% of the time, Pallas kernels for 9%

profile of v6, /device:TPU:1, one launch (start us, length us, event | category | flops | bytes accessed | tf_op | source)
XLA Modules:
  0.0 133.7 jit_solution(7710395131731443649)
XLA Ops:
  0.7 2.8 %collect.2 = (f32[1,2,64,512]{3,2,1,0:T(8,128)}, f32[1,2,64,512]{3,2,1,0:T(8,128)}) custom-call(s32[1]{0:T(128)} %bitcast.refs_0_, s32[32]{0:T(128)} %bitcast.21, s32[32]{0:T(128)} %refs_2_.5, f32[32,2,64,128]{3,2,1,0:T(8,128)} %refs_3_.4), custom_call_target="tpu_custom_call" | custom-call | flops 2000000000 | bytes 2000000 | tf_op jit(solution)/shard_map/collect/pallas_call | solution.py:46
  3.5 2.0 %collective-permute-start = (f32[1,2,64,512]{3,2,1,0:T(8,128)}, f32[1,2,64,512]{3,2,1,0:T(8,128)S(1)}, u32[]{:S(2)}, u32[]{:S(2)}) collective-permute-start(f32[1,2,64,512]{3,2,1,0:T(8,128)} %get-tuple-element.37), channel_id=1, source_target_pairs={{0,4},{4,0},{8,12},{12,8},{16,20},{20,16},{24,28},{28,24},{1,5},{5... | collective-permute-start | bytes 786440 | tf_op jit(solution)/shard_map/ppermute | solution.py:539
  5.7 0.9 copy-done.2
  6.7 1.6 %ready.1 = (f32[64,2]{1,0:T(8,128)S(1)}, s32[8]{0:T(128)S(1)}) custom-call(s32[64]{0:T(128)S(1)} %copy-done.4, s32[8]{0:T(128)S(1)} %bitcast.16, s32[8]{0:T(128)S(1)} %copy-done.6, f32[64,2]{1,0:T(8,128)S(1)} %copy.13.refs_3_, f32[1,2,64,512]{3,2,1,0:T(8,128)S(1)} %copy-done.2), custom_call_target="tpu_custom_call" | custom-call | tf_op jit(solution)/shard_map/ready/pallas_call | solution.py:46
  8.9 1.0 copy-done.8
  9.9 2.0 %collect.3 = (f32[1,2,64,512]{3,2,1,0:T(8,128)S(1)}, f32[1,2,64,512]{3,2,1,0:T(8,128)S(1)}, f32[2,2,64,512]{3,2,1,0:T(8,128)S(1)}, f32[2,2,64,512]{3,2,1,0:T(8,128)S(1)}) custom-call(s32[1]{0:T(128)} %bitcast.refs_0_, s32[32]{0:T(128)S(1)} %bitcast.22, s32[32]{0:T(128)S(1)} %copy-done.10, f32[32,2,64,128]{3,2,1,0:T(8,128)S(1)} %copy-done.8, ...), custom_call_target="tpu_custom_call" | custom-call | flops 2000000000 | bytes 2000000 | tf_op jit(solution)/shard_map/collect/pallas_call | solution.py:46
  12.0 1.4 %collective-permute-start.1 = (f32[2,64,512]{2,1,0:T(8,128)S(1)}, f32[2,64,512]{2,1,0:T(8,128)S(1)}, u32[]{:S(2)}, u32[]{:S(2)}) collective-permute-start(f32[2,64,512]{2,1,0:T(8,128)S(1)} %get-tuple-element.42), channel_id=1, source_target_pairs={{0,8},{4,12},{8,0},{12,4},{16,24},{20,28},{24,16},{28,20},{1,9},{5... | collective-permute-start | bytes 786440 | tf_op jit(solution)/shard_map/ppermute | solution.py:539
  13.5 1.0 collective-permute-start.3
  15.0 3.8 %collective-permute-done.1.refs_1_ = f32[2,64,512]{2,1,0:T(8,128)S(1)} collective-permute-done((f32[2,64,512]{2,1,0:T(8,128)S(1)}, f32[2,64,512]{2,1,0:T(8,128)S(1)}, u32[]{:S(2)}, u32[]{:S(2)}) %collective-permute-start.1) | collective-permute-done | bytes 262176 | tf_op jit(solution)/shard_map/ppermute | solution.py:539
  18.8 1.4 %collective-permute-start.2 = (f32[2,64,512]{2,1,0:T(8,128)S(1)}, f32[2,64,512]{2,1,0:T(8,128)S(1)}, u32[]{:S(2)}, u32[]{:S(2)}) collective-permute-start(f32[2,64,512]{2,1,0:T(8,128)S(1)} %add.3.refs_2_.refs_0_), channel_id=1, source_target_pairs={{16,0},{20,4},{17,1},{21,5},{18,2},{22,6},{19,3},{23,7}} | collective-permute-start | bytes 786440 | tf_op jit(solution)/shard_map/ppermute | solution.py:539
  20.3 2.5 %collective-permute-start.6 = (f32[2,64,512]{2,1,0:T(8,128)S(1)}, f32[2,64,512]{2,1,0:T(8,128)S(1)}, u32[]{:S(2)}, u32[]{:S(2)}) collective-permute-start(f32[2,64,512]{2,1,0:T(8,128)S(1)} %get-tuple-element.56), channel_id=1, source_target_pairs={{0,8},{4,12},{16,24},{20,28},{1,9},{5,13},{17,25},{21,29},{2,10},{... | collective-permute-start | bytes 786440 | tf_op jit(solution)/shard_map/ppermute | solution.py:539
  23.5 1.6 %halves.6 = (bf16[768,2048]{1,0:T(8,128)(2,1)S(1)}, bf16[768,2048]{1,0:T(8,128)(2,1)S(1)}) custom-call(f32[2,768,1024]{2,1,0:T(8,128)S(1)} %bitcast.19, bf16[512,512]{1,0:T(8,128)(2,1)S(1)} %get-tuple-element.49.refs_1_.refs_7_), custom_call_target="tpu_custom_call" | custom-call | flops 2000000000 | bytes 2000000 | tf_op jit(solution)/shard_map/halves/pallas_call | solution.py:46
  25.3 2.2 %collective-permute-done.2.refs_1_ = f32[2,64,512]{2,1,0:T(8,128)S(1)} collective-permute-done((f32[2,64,512]{2,1,0:T(8,128)S(1)}, f32[2,64,512]{2,1,0:T(8,128)S(1)}, u32[]{:S(2)}, u32[]{:S(2)}) %collective-permute-start.2) | collective-permute-done | bytes 262176 | tf_op jit(solution)/shard_map/ppermute | solution.py:539
  27.6 1.9 %collective-permute-start.4 = (f32[2,64,512]{2,1,0:T(8,128)S(1)}, f32[2,64,512]{2,1,0:T(8,128)S(1)}, u32[]{:S(2)}, u32[]{:S(2)}) collective-permute-start(f32[2,64,512]{2,1,0:T(8,128)S(1)} %source.3.refs_2_.refs_4_.refs_5_), channel_id=1, source_target_pairs={{0,4},{1,5},{2,6},{3,7}} | collective-permute-start | bytes 786440 | tf_op jit(solution)/shard_map/ppermute | solution.py:539
  29.5 0.7 collective-permute-start.8
  30.2 0.8 collective-permute-done.5.refs_1_
  31.4 3.8 %collective-permute-done.4.refs_1_ = f32[2,64,512]{2,1,0:T(8,128)S(1)} collective-permute-done((f32[2,64,512]{2,1,0:T(8,128)S(1)}, f32[2,64,512]{2,1,0:T(8,128)S(1)}, u32[]{:S(2)}, u32[]{:S(2)}) %collective-permute-start.4) | collective-permute-done | bytes 262176 | tf_op jit(solution)/shard_map/ppermute | solution.py:539
  35.2 0.7 collective-permute-start.7
  35.9 0.8 collective-permute-start.24
  36.9 1.3 collective-permute-start.23
  38.2 4.5 %collective-permute-start.12 = (f32[2,64,512]{2,1,0:T(8,128)S(1)}, f32[2,64,512]{2,1,0:T(8,128)S(1)}, u32[]{:S(2)}, u32[]{:S(2)}) collective-permute-start(f32[2,64,512]{2,1,0:T(8,128)S(1)} %add.5.refs_2_.refs_0_), channel_id=1, source_target_pairs={{0,16},{4,20},{8,24},{12,28},{1,17},{5,21},{9,25},{13,29},{2,18},{... | collective-permute-start | bytes 786440 | tf_op jit(solution)/shard_map/ppermute | solution.py:539
  42.7 0.7 collective-permute-start.10
  44.2 0.7 collective-permute-start.11
  44.9 0.7 collective-permute-start.15
  46.1 0.7 collective-permute-start.14
  49.7 0.7 collective-permute-start.21
  50.4 0.7 collective-permute-start.20
  51.8 1.3 collective-permute-start.26
  53.9 1.3 collective-permute-start.29
  55.2 0.7 collective-permute-start.28
  55.9 31.0 %collective-permute-done.23.refs_1_ = f32[2,512,512]{2,1,0:T(8,128)S(1)} collective-permute-done((f32[2,512,512]{2,1,0:T(8,128)S(1)}, f32[2,512,512]{2,1,0:T(8,128)S(1)}, u32[]{:S(2)}, u32[]{:S(2)}) %collective-permute-start.23) | collective-permute-done | bytes 2097184 | tf_op jit(solution)/shard_map/ppermute | solution.py:539
  86.9 0.7 halves.7
  87.7 2.1 %collective-permute-done.26.refs_4_ = f32[2,32,512]{2,1,0:T(8,128)S(1)} collective-permute-done((f32[2,32,512]{2,1,0:T(8,128)S(1)}, f32[2,32,512]{2,1,0:T(8,128)S(1)}, u32[]{:S(2)}, u32[]{:S(2)}) %collective-permute-start.26) | collective-permute-done | bytes 131104 | tf_op jit(solution)/shard_map/ppermute | solution.py:539
  89.7 0.7 collective-permute-start.27
  90.4 2.1 %collective-permute-done.29.refs_4_ = f32[2,32,512]{2,1,0:T(8,128)S(1)} collective-permute-done((f32[2,32,512]{2,1,0:T(8,128)S(1)}, f32[2,32,512]{2,1,0:T(8,128)S(1)}, u32[]{:S(2)}, u32[]{:S(2)}) %collective-permute-start.29) | collective-permute-done | bytes 131104 | tf_op jit(solution)/shard_map/ppermute | solution.py:539
  93.3 1.3 collective-permute-start.33
  94.6 1.3 collective-permute-start.34
  97.3 2.2 %collective-permute-done.33.refs_1_ = f32[2,32,512]{2,1,0:T(8,128)S(1)} collective-permute-done((f32[2,32,512]{2,1,0:T(8,128)S(1)}, f32[2,32,512]{2,1,0:T(8,128)S(1)}, u32[]{:S(2)}, u32[]{:S(2)}) %collective-permute-start.33) | collective-permute-done | bytes 131104 | tf_op jit(solution)/shard_map/ppermute | solution.py:539
  99.4 1.3 up.14.refs_9_.refs_5_
  100.7 1.3 collective-permute-done.34.refs_1_
  102.1 1.3 up.15.refs_6_.refs_9_
  103.4 13.5 %collective-permute-start.35 = (f32[2,64,128]{2,1,0:T(8,128)S(1)}, f32[2,64,128]{2,1,0:T(8,128)S(1)}, u32[]{:S(2)}, u32[]{:S(2)}) collective-permute-start(f32[2,64,128]{2,1,0:T(8,128)S(1)} %get-tuple-element.68), channel_id=1, source_target_pairs={{0,1},{1,2},{2,3},{4,5},{5,6},{6,7},{8,9},{9,10},{10,11},{12,13},{... | collective-permute-start | bytes 196616 | tf_op jit(solution)/shard_map/ppermute | solution.py:643
  116.9 1.9 %collective-permute-start.36 = (f32[2,64,128]{2,1,0:T(8,128)S(1)}, f32[2,64,128]{2,1,0:T(8,128)S(1)}, u32[]{:S(2)}, u32[]{:S(2)}) collective-permute-start(f32[2,64,128]{2,1,0:T(8,128)S(1)} %get-tuple-element.64.refs_9_), channel_id=1, source_target_pairs={{1,0},{2,1},{3,2},{5,4},{6,5},{7,6},{9,8},{10,9},{11,10},{13,12},{... | collective-permute-start | bytes 196616 | tf_op jit(solution)/shard_map/ppermute | solution.py:644
  118.8 0.7 finish.1
  119.6 1.0 middle.1.refs_1_
  120.6 1.9 %collective-permute-done.36.refs_3_ = f32[2,64,128]{2,1,0:T(8,128)S(1)} collective-permute-done((f32[2,64,128]{2,1,0:T(8,128)S(1)}, f32[2,64,128]{2,1,0:T(8,128)S(1)}, u32[]{:S(2)}, u32[]{:S(2)}) %collective-permute-start.36) | collective-permute-done | bytes 65568 | tf_op jit(solution)/shard_map/ppermute | solution.py:644
  122.5 1.2 rim.1
  123.7 9.5 %all_to_all.9.refs_0_ = f32[8,8,128]{2,1,0:T(8,128)S(1)} all-to-all(f32[8,8,128]{2,1,0:T(8,128)S(1)} %bitcast.15), channel_id=1, replica_groups=mesh['slab'=8,'lat'=4] {'slab'}, dimensions={0} | all-to-all | bytes 65536 | tf_op jit(solution)/shard_map/all_to_all | solution.py:648
  (105 shorter events, 11.2 us)
Async XLA Ops:
  0.6 4.9 %copy-start.11 = (f32[64,2]{0,1:T(2,128)S(1)}, f32[64,2]{0,1:T(2,128)}, u32[]{:S(2)}) copy-start(f32[64,2]{0,1:T(2,128)} %param.15) | copy-start | bytes 1540
  0.6 5.0 %copy-start.4 = (s32[64]{0:T(128)S(1)}, s32[64]{0:T(128)}, u32[]{:S(2)}) copy-start(s32[64]{0:T(128)} %refs_0_.1) | copy-start | bytes 772
  0.7 5.0 %copy-start.5 = (s32[8,1]{0,1:T(1,128)S(1)}, s32[8,1]{0,1:T(1,128)}, u32[]{:S(2)}) copy-start(s32[8,1]{0,1:T(1,128)} %param.20) | copy-start | bytes 100
  0.7 5.0 %copy-start.6 = (s32[8]{0:T(128)S(1)}, s32[8]{0:T(128)}, u32[]{:S(2)}) copy-start(s32[8]{0:T(128)} %refs_2_.4) | copy-start | bytes 100
  0.7 7.6 %copy-start.7 = (f32[1,1,2,512,512]{4,3,2,1,0:T(8,128)S(1)}, f32[1,1,2,512,512]{4,3,2,1,0:T(8,128)}, u32[]{:S(2)}) copy-start(f32[1,1,2,512,512]{4,3,2,1,0:T(8,128)} %param.16) | copy-start | bytes 6291460
  3.5 8.4 %collective-permute-start = (f32[1,2,64,512]{3,2,1,0:T(8,128)}, f32[1,2,64,512]{3,2,1,0:T(8,128)S(1)}, u32[]{:S(2)}, u32[]{:S(2)}) collective-permute-start(f32[1,2,64,512]{3,2,1,0:T(8,128)} %get-tuple-element.37), channel_id=1, source_target_pairs={{0,4},{4,0},{8,12},{12,8},{16,20},{20,16},{24,28},{28,24},{1,5},{5... | collective-permute-start | bytes 786440 | tf_op jit(solution)/shard_map/ppermute | solution.py:539
  8.3 1.6 %copy-start.8 = (f32[32,2,64,128]{3,2,1,0:T(8,128)S(1)}, f32[32,2,64,128]{3,2,1,0:T(8,128)}, u32[]{:S(2)}) copy-start(f32[32,2,64,128]{3,2,1,0:T(8,128)} %refs_3_.4) | copy-start | bytes 6291460
  9.9 2.1 %copy-start.3 = (f32[1,2,64,512]{3,2,1,0:T(8,128)S(1)}, f32[1,2,64,512]{3,2,1,0:T(8,128)}, u32[]{:S(2)}) copy-start(f32[1,2,64,512]{3,2,1,0:T(8,128)} %get-tuple-element.36.refs_4_.refs_0_) | copy-start | bytes 786436
  9.9 13.6 %slice-start = ((s8[6291456]{0:T(1024)(128)(4,1)}), s8[4194304]{0:T(1024)(128)(4,1)S(1)}, s32[]{:S(2)}) async-start(s8[6291456]{0:T(1024)(128)(4,1)} %bitcast.17), calls=%async_computation.1 | async-start | bytes 8388608
  11.9 10.9 %copy-start = (f32[1,1,2,512,512]{4,3,2,1,0:T(8,128)S(1)}, f32[1,1,2,512,512]{4,3,2,1,0:T(8,128)}, u32[]{:S(2)}) copy-start(f32[1,1,2,512,512]{4,3,2,1,0:T(8,128)} %param.17) | copy-start | bytes 6291460
  12.0 6.8 %collective-permute-start.1 = (f32[2,64,512]{2,1,0:T(8,128)S(1)}, f32[2,64,512]{2,1,0:T(8,128)S(1)}, u32[]{:S(2)}, u32[]{:S(2)}) collective-permute-start(f32[2,64,512]{2,1,0:T(8,128)S(1)} %get-tuple-element.42), channel_id=1, source_target_pairs={{0,8},{4,12},{8,0},{12,4},{16,24},{20,28},{24,16},{28,20},{1,9},{5... | collective-permute-start | bytes 786440 | tf_op jit(solution)/shard_map/ppermute | solution.py:539
  13.5 6.8 %collective-permute-start.3 = (f32[1,2,64,512]{3,2,1,0:T(8,128)S(1)}, f32[1,2,64,512]{3,2,1,0:T(8,128)S(1)}, u32[]{:S(2)}, u32[]{:S(2)}) collective-permute-start(f32[1,2,64,512]{3,2,1,0:T(8,128)S(1)} %get-tuple-element.45.refs_2_), channel_id=1, source_target_pairs={{0,4},{4,0},{8,12},{12,8},{16,20},{20,16},{24,28},{28,24},{1,5},{5... | collective-permute-start | bytes 786440 | tf_op jit(solution)/shard_map/ppermute | solution.py:539
  14.5 16.5 %collective-permute-start.5 = (f32[2,2,64,512]{3,2,1,0:T(8,128)S(1)}, f32[2,2,64,512]{3,2,1,0:T(8,128)S(1)}, u32[]{:S(2)}, u32[]{:S(2)}) collective-permute-start(f32[2,2,64,512]{3,2,1,0:T(8,128)S(1)} %get-tuple-element.55), channel_id=1, source_target_pairs={{0,4},{4,0},{8,12},{12,8},{16,20},{20,16},{24,28},{28,24},{1,5},{5... | collective-permute-start | bytes 1572872 | tf_op jit(solution)/shard_map/ppermute | solution.py:539
  18.8 4.7 %slice-start.1 = ((s8[6291456]{0:T(1024)(128)(4,1)}), s8[2097152]{0:T(1024)(128)(4,1)S(1)}, s32[]{:S(2)}) async-start(s8[6291456]{0:T(1024)(128)(4,1)} %bitcast.17), calls=%async_computation.2 | async-start | bytes 4194304
  18.8 8.7 %collective-permute-start.2 = (f32[2,64,512]{2,1,0:T(8,128)S(1)}, f32[2,64,512]{2,1,0:T(8,128)S(1)}, u32[]{:S(2)}, u32[]{:S(2)}) collective-permute-start(f32[2,64,512]{2,1,0:T(8,128)S(1)} %add.3.refs_2_.refs_0_), channel_id=1, source_target_pairs={{16,0},{20,4},{17,1},{21,5},{18,2},{22,6},{19,3},{23,7}} | collective-permute-start | bytes 786440 | tf_op jit(solution)/shard_map/ppermute | solution.py:539
  20.3 9.2 %collective-permute-start.6 = (f32[2,64,512]{2,1,0:T(8,128)S(1)}, f32[2,64,512]{2,1,0:T(8,128)S(1)}, u32[]{:S(2)}, u32[]{:S(2)}) collective-permute-start(f32[2,64,512]{2,1,0:T(8,128)S(1)} %get-tuple-element.56), channel_id=1, source_target_pairs={{0,8},{4,12},{16,24},{20,28},{1,9},{5,13},{17,25},{21,29},{2,10},{... | collective-permute-start | bytes 786440 | tf_op jit(solution)/shard_map/ppermute | solution.py:539
  27.6 7.6 %collective-permute-start.4 = (f32[2,64,512]{2,1,0:T(8,128)S(1)}, f32[2,64,512]{2,1,0:T(8,128)S(1)}, u32[]{:S(2)}, u32[]{:S(2)}) collective-permute-start(f32[2,64,512]{2,1,0:T(8,128)S(1)} %source.3.refs_2_.refs_4_.refs_5_), channel_id=1, source_target_pairs={{0,4},{1,5},{2,6},{3,7}} | collective-permute-start | bytes 786440 | tf_op jit(solution)/shard_map/ppermute | solution.py:539
  29.5 7.2 %collective-permute-start.8 = (f32[2,64,512]{2,1,0:T(8,128)S(1)}, f32[2,64,512]{2,1,0:T(8,128)S(1)}, u32[]{:S(2)}, u32[]{:S(2)}) collective-permute-start(f32[2,64,512]{2,1,0:T(8,128)S(1)} %add.4.refs_2_.refs_0_), channel_id=1, source_target_pairs={{24,8},{28,12},{25,9},{29,13},{26,10},{30,14},{27,11},{31,15}} | collective-permute-start | bytes 786440 | tf_op jit(solution)/shard_map/ppermute | solution.py:539
  31.1 5.8 %collective-permute-start.9 = (f32[2,64,512]{2,1,0:T(8,128)S(1)}, f32[2,64,512]{2,1,0:T(8,128)S(1)}, u32[]{:S(2)}, u32[]{:S(2)}) collective-permute-start(f32[2,64,512]{2,1,0:T(8,128)S(1)} %get-tuple-element.59), channel_id=1, source_target_pairs={{0,8},{4,12},{8,0},{12,4},{16,24},{20,28},{24,16},{28,20},{1,9},{5... | collective-permute-start | bytes 786440 | tf_op jit(solution)/shard_map/ppermute | solution.py:539
  35.2 1.7 %collective-permute-start.7 = (f32[2,64,512]{2,1,0:T(8,128)S(1)}, f32[2,64,512]{2,1,0:T(8,128)S(1)}, u32[]{:S(2)}, u32[]{:S(2)}) collective-permute-start(f32[2,64,512]{2,1,0:T(8,128)S(1)} %down.13.refs_0_.refs_1_), channel_id=1, source_target_pairs={{4,8},{5,9},{6,10},{7,11}} | collective-permute-start | bytes 786440 | tf_op jit(solution)/shard_map/ppermute | solution.py:539
  35.9 19.3 %collective-permute-start.24 = (f32[2,512,512]{2,1,0:T(8,128)S(1)}, f32[2,512,512]{2,1,0:T(8,128)S(1)}, u32[]{:S(2)}, u32[]{:S(2)}) collective-permute-start(f32[2,512,512]{2,1,0:T(8,128)S(1)} %hold.2.refs_3_), channel_id=1, source_target_pairs={{12,8},{20,16},{13,9},{21,17},{14,10},{22,18},{15,11},{23,19}} | collective-permute-start | bytes 6291464 | tf_op jit(solution)/shard_map/ppermute | solution.py:539
  36.9 50.0 %collective-permute-start.23 = (f32[2,512,512]{2,1,0:T(8,128)S(1)}, f32[2,512,512]{2,1,0:T(8,128)S(1)}, u32[]{:S(2)}, u32[]{:S(2)}) collective-permute-start(f32[2,512,512]{2,1,0:T(8,128)S(1)} %hold.3.refs_6_), channel_id=1, source_target_pairs={{4,0},{5,1},{6,2},{7,3}} | collective-permute-start | bytes 6291464 | tf_op jit(solution)/shard_map/ppermute | solution.py:539
  38.2 7.8 %collective-permute-start.12 = (f32[2,64,512]{2,1,0:T(8,128)S(1)}, f32[2,64,512]{2,1,0:T(8,128)S(1)}, u32[]{:S(2)}, u32[]{:S(2)}) collective-permute-start(f32[2,64,512]{2,1,0:T(8,128)S(1)} %add.5.refs_2_.refs_0_), channel_id=1, source_target_pairs={{0,16},{4,20},{8,24},{12,28},{1,17},{5,21},{9,25},{13,29},{2,18},{... | collective-permute-start | bytes 786440 | tf_op jit(solution)/shard_map/ppermute | solution.py:539
  42.7 1.4 %collective-permute-start.10 = (f32[2,32,512]{2,1,0:T(8,128)S(1)}, f32[2,32,512]{2,1,0:T(8,128)S(1)}, u32[]{:S(2)}, u32[]{:S(2)}) collective-permute-start(f32[2,32,512]{2,1,0:T(8,128)S(1)} %down.14.refs_6_.refs_5_), channel_id=1, source_target_pairs={{8,12},{9,13},{10,14},{11,15}} | collective-permute-start | bytes 393224 | tf_op jit(solution)/shard_map/ppermute | solution.py:539
  43.5 1.4 %collective-permute-start.13 = (f32[2,32,512]{2,1,0:T(8,128)S(1)}, f32[2,32,512]{2,1,0:T(8,128)S(1)}, u32[]{:S(2)}, u32[]{:S(2)}) collective-permute-start(f32[2,32,512]{2,1,0:T(8,128)S(1)} %down.15.refs_6_.refs_5_), channel_id=1, source_target_pairs={{8,12},{9,13},{10,14},{11,15}} | collective-permute-start | bytes 393224 | tf_op jit(solution)/shard_map/ppermute | solution.py:539
  44.2 1.9 %collective-permute-start.11 = (f32[2,32,512]{2,1,0:T(8,128)S(1)}, f32[2,32,512]{2,1,0:T(8,128)S(1)}, u32[]{:S(2)}, u32[]{:S(2)}) collective-permute-start(f32[2,32,512]{2,1,0:T(8,128)S(1)} %down.16.refs_6_.refs_5_), channel_id=1, source_target_pairs={{12,16},{13,17},{14,18},{15,19}} | collective-permute-start | bytes 393224 | tf_op jit(solution)/shard_map/ppermute | solution.py:539
  44.9 1.9 %collective-permute-start.15 = (f32[2,32,512]{2,1,0:T(8,128)S(1)}, f32[2,32,512]{2,1,0:T(8,128)S(1)}, u32[]{:S(2)}, u32[]{:S(2)}) collective-permute-start(f32[2,32,512]{2,1,0:T(8,128)S(1)} %down.17.refs_3_.refs_5_), channel_id=1, source_target_pairs={{12,16},{13,17},{14,18},{15,19}} | collective-permute-start | bytes 393224 | tf_op jit(solution)/shard_map/ppermute | solution.py:539
  46.1 1.4 %collective-permute-start.14 = (f32[2,32,512]{2,1,0:T(8,128)S(1)}, f32[2,32,512]{2,1,0:T(8,128)S(1)}, u32[]{:S(2)}, u32[]{:S(2)}) collective-permute-start(f32[2,32,512]{2,1,0:T(8,128)S(1)} %down.18.refs_6_.refs_5_), channel_id=1, source_target_pairs={{16,20},{17,21},{18,22},{19,23}} | collective-permute-start | bytes 393224 | tf_op jit(solution)/shard_map/ppermute | solution.py:539
  46.9 1.4 %collective-permute-start.17 = (f32[2,32,512]{2,1,0:T(8,128)S(1)}, f32[2,32,512]{2,1,0:T(8,128)S(1)}, u32[]{:S(2)}, u32[]{:S(2)}) collective-permute-start(f32[2,32,512]{2,1,0:T(8,128)S(1)} %down.19.refs_6_.refs_5_), channel_id=1, source_target_pairs={{16,20},{17,21},{18,22},{19,23}} | collective-permute-start | bytes 393224 | tf_op jit(solution)/shard_map/ppermute | solution.py:539
  47.6 1.4 %collective-permute-start.16 = (f32[2,32,512]{2,1,0:T(8,128)S(1)}, f32[2,32,512]{2,1,0:T(8,128)S(1)}, u32[]{:S(2)}, u32[]{:S(2)}) collective-permute-start(f32[2,32,512]{2,1,0:T(8,128)S(1)} %down.20.refs_6_.refs_5_), channel_id=1, source_target_pairs={{20,24},{21,25},{22,26},{23,27}} | collective-permute-start | bytes 393224 | tf_op jit(solution)/shard_map/ppermute | solution.py:539
  48.3 1.4 %collective-permute-start.19 = (f32[2,32,512]{2,1,0:T(8,128)S(1)}, f32[2,32,512]{2,1,0:T(8,128)S(1)}, u32[]{:S(2)}, u32[]{:S(2)}) collective-permute-start(f32[2,32,512]{2,1,0:T(8,128)S(1)} %down.21.refs_6_.refs_5_), channel_id=1, source_target_pairs={{20,24},{21,25},{22,26},{23,27}} | collective-permute-start | bytes 393224 | tf_op jit(solution)/shard_map/ppermute | solution.py:539
  49.0 1.4 %collective-permute-start.18 = (f32[2,32,512]{2,1,0:T(8,128)S(1)}, f32[2,32,512]{2,1,0:T(8,128)S(1)}, u32[]{:S(2)}, u32[]{:S(2)}) collective-permute-start(f32[2,32,512]{2,1,0:T(8,128)S(1)} %down.22.refs_6_.refs_5_), channel_id=1, source_target_pairs={{24,28},{25,29},{26,30},{27,31}} | collective-permute-start | bytes 393224 | tf_op jit(solution)/shard_map/ppermute | solution.py:539
  49.7 1.4 %collective-permute-start.21 = (f32[2,32,512]{2,1,0:T(8,128)S(1)}, f32[2,32,512]{2,1,0:T(8,128)S(1)}, u32[]{:S(2)}, u32[]{:S(2)}) collective-permute-start(f32[2,32,512]{2,1,0:T(8,128)S(1)} %down.23.refs_6_.refs_5_), channel_id=1, source_target_pairs={{24,28},{25,29},{26,30},{27,31}} | collective-permute-start | bytes 393224 | tf_op jit(solution)/shard_map/ppermute | solution.py:539
  50.4 2.7 %collective-permute-start.20 = (f32[2,32,512]{2,1,0:T(8,128)S(1)}, f32[2,32,512]{2,1,0:T(8,128)S(1)}, u32[]{:S(2)}, u32[]{:S(2)}) collective-permute-start(f32[2,32,512]{2,1,0:T(8,128)S(1)} %down.24.refs_6_.refs_4_.refs_5_.refs_7_.refs_3_), channel_id=1, source_target_pairs={{28,24},{29,25},{30,26},{31,27}} | collective-permute-start | bytes 393224 | tf_op jit(solution)/shard_map/ppermute | solution.py:539
  51.2 2.7 %collective-permute-start.25 = (f32[2,32,512]{2,1,0:T(8,128)S(1)}, f32[2,32,512]{2,1,0:T(8,128)S(1)}, u32[]{:S(2)}, u32[]{:S(2)}) collective-permute-start(f32[2,32,512]{2,1,0:T(8,128)S(1)} %down.25.refs_6_.refs_4_.refs_5_.refs_7_), channel_id=1, source_target_pairs={{28,24},{29,25},{30,26},{31,27}} | collective-permute-start | bytes 393224 | tf_op jit(solution)/shard_map/ppermute | solution.py:539
  51.8 37.9 %collective-permute-start.26 = (f32[2,32,512]{2,1,0:T(8,128)S(1)}, f32[2,32,512]{2,1,0:T(8,128)S(1)}, u32[]{:S(2)}, u32[]{:S(2)}) collective-permute-start(f32[2,32,512]{2,1,0:T(8,128)S(1)} %down.24.refs_6_.refs_4_.refs_5_.refs_7_.refs_3_), channel_id=1, source_target_pairs={{4,0},{12,8},{20,16},{5,1},{13,9},{21,17},{6,2},{14,10},{22,18},{7... | collective-permute-start | bytes 393224 | tf_op jit(solution)/shard_map/ppermute | solution.py:539
  53.2 36.6 %collective-permute-start.22 = (f32[2,32,512]{2,1,0:T(8,128)S(1)}, f32[2,32,512]{2,1,0:T(8,128)S(1)}, u32[]{:S(2)}, u32[]{:S(2)}) collective-permute-start(f32[2,32,512]{2,1,0:T(8,128)S(1)} %up.8.refs_6_.refs_8_), channel_id=1, source_target_pairs={{24,16},{25,17},{26,18},{27,19}} | collective-permute-start | bytes 393224 | tf_op jit(solution)/shard_map/ppermute | solution.py:539
  53.9 38.7 %collective-permute-start.29 = (f32[2,32,512]{2,1,0:T(8,128)S(1)}, f32[2,32,512]{2,1,0:T(8,128)S(1)}, u32[]{:S(2)}, u32[]{:S(2)}) collective-permute-start(f32[2,32,512]{2,1,0:T(8,128)S(1)} %down.25.refs_6_.refs_4_.refs_5_.refs_7_), channel_id=1, source_target_pairs={{4,0},{12,8},{20,16},{5,1},{13,9},{21,17},{6,2},{14,10},{22,18},{7... | collective-permute-start | bytes 393224 | tf_op jit(solution)/shard_map/ppermute | solution.py:539
  55.2 37.3 %collective-permute-start.28 = (f32[2,32,512]{2,1,0:T(8,128)S(1)}, f32[2,32,512]{2,1,0:T(8,128)S(1)}, u32[]{:S(2)}, u32[]{:S(2)}) collective-permute-start(f32[2,32,512]{2,1,0:T(8,128)S(1)} %up.9.refs_3_.refs_8_), channel_id=1, source_target_pairs={{24,16},{25,17},{26,18},{27,19}} | collective-permute-start | bytes 393224 | tf_op jit(solution)/shard_map/ppermute | solution.py:539
  89.7 3.5 %collective-permute-start.27 = (f32[2,32,512]{2,1,0:T(8,128)S(1)}, f32[2,32,512]{2,1,0:T(8,128)S(1)}, u32[]{:S(2)}, u32[]{:S(2)}) collective-permute-start(f32[2,32,512]{2,1,0:T(8,128)S(1)} %up.10.refs_9_.refs_8_), channel_id=1, source_target_pairs={{16,8},{17,9},{18,10},{19,11}} | collective-permute-start | bytes 393224 | tf_op jit(solution)/shard_map/ppermute | solution.py:539
  92.6 2.0 %collective-permute-start.31 = (f32[2,32,512]{2,1,0:T(8,128)S(1)}, f32[2,32,512]{2,1,0:T(8,128)S(1)}, u32[]{:S(2)}, u32[]{:S(2)}) collective-permute-start(f32[2,32,512]{2,1,0:T(8,128)S(1)} %up.11.refs_9_.refs_8_), channel_id=1, source_target_pairs={{16,8},{17,9},{18,10},{19,11}} | collective-permute-start | bytes 393224 | tf_op jit(solution)/shard_map/ppermute | solution.py:539
  93.3 6.1 %collective-permute-start.33 = (f32[2,32,512]{2,1,0:T(8,128)S(1)}, f32[2,32,512]{2,1,0:T(8,128)S(1)}, u32[]{:S(2)}, u32[]{:S(2)}) collective-permute-start(f32[2,32,512]{2,1,0:T(8,128)S(1)} %up.12.refs_9_.refs_8_), channel_id=1, source_target_pairs={{8,0},{9,1},{10,2},{11,3}} | collective-permute-start | bytes 393224 | tf_op jit(solution)/shard_map/ppermute | solution.py:539
  94.6 7.4 %collective-permute-start.34 = (f32[2,32,512]{2,1,0:T(8,128)S(1)}, f32[2,32,512]{2,1,0:T(8,128)S(1)}, u32[]{:S(2)}, u32[]{:S(2)}) collective-permute-start(f32[2,32,512]{2,1,0:T(8,128)S(1)} %up.13.refs_9_.refs_8_), channel_id=1, source_target_pairs={{8,0},{9,1},{10,2},{11,3}} | collective-permute-start | bytes 393224 | tf_op jit(solution)/shard_map/ppermute | solution.py:539
  95.9 7.5 %collective-permute-start.32 = (f32[2,32,512]{2,1,0:T(8,128)S(1)}, f32[2,32,512]{2,1,0:T(8,128)S(1)}, u32[]{:S(2)}, u32[]{:S(2)}) collective-permute-start(f32[2,32,512]{2,1,0:T(8,128)S(1)} %up.13.refs_9_.refs_8_), channel_id=1, source_target_pairs={{8,4},{16,12},{24,20},{9,5},{17,13},{25,21},{10,6},{18,14},{26,22}... | collective-permute-start | bytes 393224 | tf_op jit(solution)/shard_map/ppermute | solution.py:539
  96.6 6.8 %collective-permute-start.30 = (f32[2,32,512]{2,1,0:T(8,128)S(1)}, f32[2,32,512]{2,1,0:T(8,128)S(1)}, u32[]{:S(2)}, u32[]{:S(2)}) collective-permute-start(f32[2,32,512]{2,1,0:T(8,128)S(1)} %up.12.refs_9_.refs_8_), channel_id=1, source_target_pairs={{8,4},{16,12},{24,20},{9,5},{17,13},{25,21},{10,6},{18,14},{26,22}... | collective-permute-start | bytes 393224 | tf_op jit(solution)/shard_map/ppermute | solution.py:539
  103.4 16.2 %copy-start.1 = (f32[1,1,2,64,1024]{4,3,2,1,0:T(8,128)S(1)}, f32[1,1,2,64,1024]{4,3,2,1,0:T(8,128)}, u32[]{:S(2)}) copy-start(f32[1,1,2,64,1024]{4,3,2,1,0:T(8,128)} %param.19) | copy-start | bytes 1572868
  103.4 17.1 %collective-permute-start.35 = (f32[2,64,128]{2,1,0:T(8,128)S(1)}, f32[2,64,128]{2,1,0:T(8,128)S(1)}, u32[]{:S(2)}, u32[]{:S(2)}) collective-permute-start(f32[2,64,128]{2,1,0:T(8,128)S(1)} %get-tuple-element.68), channel_id=1, source_target_pairs={{0,1},{1,2},{2,3},{4,5},{5,6},{6,7},{8,9},{9,10},{10,11},{12,13},{... | collective-permute-start | bytes 196616 | tf_op jit(solution)/shard_map/ppermute | solution.py:643
  116.9 5.6 %collective-permute-start.36 = (f32[2,64,128]{2,1,0:T(8,128)S(1)}, f32[2,64,128]{2,1,0:T(8,128)S(1)}, u32[]{:S(2)}, u32[]{:S(2)}) collective-permute-start(f32[2,64,128]{2,1,0:T(8,128)S(1)} %get-tuple-element.64.refs_9_), channel_id=1, source_target_pairs={{1,0},{2,1},{3,2},{5,4},{6,5},{7,6},{9,8},{10,9},{11,10},{13,12},{... | collective-permute-start | bytes 196616 | tf_op jit(solution)/shard_map/ppermute | solution.py:644
  (3 other events, 4.1 us)
